TPU v7x, 32 devices: a whole 2x2x4 slice. The times are simulated.
32 devices in a mesh: tm: 2 (over y), blk: 16 (over z, x, core).
Axes of the slice: x: 2, y: 2, z: 4, core: 2. Of those that a mesh axis runs over, the one named last changes fastest.
Arguments:
- propagator: float32 [2, 8192, 2048], P('tm', 'blk'), may hold values from -0.09375 to 0.09375
- inv_diag: float32 [2, 8192, 2048], P('tm', 'blk'), may hold values from -0.09375 to 0.09375
- rhs: float32 [2, 4096, 128], P('tm', 'blk'), may hold values from -6 to 6
- arrow: float32 [2, 64, 4096], P('tm', None, 'blk'), may hold values from -0.0625 to 0.0625
- tip_inv: float32 [64, 64], replicated, may hold values from -0.75 to 0.75
- tip_rhs: float32 [64, 128], replicated, may hold values from -6 to 6
Outputs:
- solved: float32 [2, 4096, 128], P('tm', 'blk')
- tip: float32 [64, 128], replicated
All inputs are finite; a program needn't handle non-finite values.
Results may differ from a plain program's by a relative error of at most 0.00011.
Values sent between devices are 32-bit elements; how exact they have to be, the bound alone decides.
No kernel may reach another device: no remote copies, remote signals or barrier semaphores. Data moves between devices by JAX's collectives and lax.ppermute only.
A program may use at most 64 MiB of HBM per device.

v0:
```python
import jax
import jax.numpy as jnp
from jax import lax
from jax.sharding import PartitionSpec as P

GROUP = 8


HIGHEST_PREC = lax.Precision.HIGHEST


def swapped(block, axis, distance):
    count = lax.axis_size(axis)
    route = []
    for low in range(count):
        high = low | 1 << distance
        if high != low and high < count:
            route += [(low, high), (high, low)]
    return lax.ppermute(block, axis, route)


def from_behind(block, axis, distance):
    devices = range(lax.axis_size(axis))
    route = [(i - distance, i) for i in devices if i - distance in devices]
    return lax.ppermute(block, axis, route)


def on_device(propagator, inv_diag, rhs, arrow, tip_inv, tip_rhs):
    tile_m = propagator[0]
    tile_g = inv_diag[0]
    right_side = rhs[0]
    arrow_rows = arrow[0]
    shard_rows = right_side.shape[0]
    blocks = lax.axis_size("blk")
    position = lax.axis_index("blk")
    high_index = position // GROUP
    low_count = GROUP.bit_length() - 1
    all_count = blocks.bit_length() - 1

    def digit_set(bit_number):
        return position // (1 << bit_number) % 2 == 1

    def assemble(shard):
        joined = shard
        for bit_number in range(low_count):
            other = swapped(joined, "blk", bit_number)
            joined = jnp.where(
                digit_set(bit_number),
                jnp.concatenate([other, joined], axis=0),
                jnp.concatenate([joined, other], axis=0),
            )
        return joined

    def combine(partial_value):
        running = partial_value
        for bit_number in range(low_count, all_count):
            running = running + swapped(running, "blk", bit_number)
        return lax.dynamic_slice_in_dim(running, high_index * shard_rows, shard_rows, 0)

    def apply_tile(tile, columns):
        partial_value = jnp.dot(
            tile, columns, precision=HIGHEST_PREC, preferred_element_type=jnp.float32
        )
        return combine(partial_value)

    own_part = apply_tile(tile_g, assemble(right_side))

    def advance(counter, current):
        earlier = from_behind(current, "tm", 1)
        columns = assemble(earlier)
        return own_part - apply_tile(tile_m, columns)

    solved = lax.fori_loop(0, lax.axis_size("tm") - 1, advance, own_part)
    partial_tip = jnp.dot(
        arrow_rows, solved, precision=HIGHEST_PREC, preferred_element_type=jnp.float32
    )
    summed = lax.psum(partial_tip, ("tm", "blk"))
    reduced = tip_rhs - summed
    tip = jnp.dot(tip_inv, reduced, precision=HIGHEST_PREC, preferred_element_type=jnp.float32)
    return (solved[None], tip)


def solution(mesh):
    placed = (
        P("tm", "blk", None),
        P("tm", "blk", None),
        P("tm", "blk", None),
        P("tm", None, "blk"),
        P(),
        P(),
    )
    return jax.shard_map(
        on_device,
        mesh=mesh,
        in_specs=placed,
        out_specs=(P("tm", "blk", None), P()),
        check_vma=False,
    )
```

profile of v0, /device:TPU:0, one launch (start us, length us, event | category | flops | bytes accessed | tf_op | source)
XLA Modules:
  0.0 137.9 jit_solution(4845125214244512455)
XLA Ops:
  0.6 0.0 copy-start
  0.6 1.0 copy.8
  1.7 0.5 collective-permute-start
  2.2 1.0 collective-permute-done
  3.2 2.9 %collective-permute-start.1 = (f32[512,128]{0,1:T(8,128)S(1)}, f32[512,128]{0,1:T(8,128)S(1)}, u32[]{:S(2)}, u32[]{:S(2)}) collective-permute-start(f32[512,128]{0,1:T(8,128)S(1)} %maximum_select_fusion.6), channel_id=1, source_target_pairs={{0,2},{2,0},{1,3},{3,1},{4,6},{6,4},{5,7},{7,5},{8,10},{10,8},{9,1... | collective-permute-start | bytes 786440 | tf_op jit(solution)/shard_map/ppermute | solution.py:19
  6.1 6.6 %collective-permute-done.1 = f32[512,128]{0,1:T(8,128)S(1)} collective-permute-done((f32[512,128]{0,1:T(8,128)S(1)}, f32[512,128]{0,1:T(8,128)S(1)}, u32[]{:S(2)}, u32[]{:S(2)}) %collective-permute-start.1) | collective-permute-done | bytes 262176 | tf_op jit(solution)/shard_map/ppermute | solution.py:19
  12.8 1.9 %collective-permute-start.2 = (f32[1024,128]{0,1:T(8,128)S(1)}, f32[1024,128]{0,1:T(8,128)S(1)}, u32[]{:S(2)}, u32[]{:S(2)}) collective-permute-start(f32[1024,128]{0,1:T(8,128)S(1)} %maximum_select_fusion.4), channel_id=1, source_target_pairs={{0,4},{4,0},{1,5},{5,1},{2,6},{6,2},{3,7},{7,3},{8,12},{12,8},{9,1... | collective-permute-start | bytes 1572872 | tf_op jit(solution)/shard_map/ppermute | solution.py:19
  14.7 11.6 %collective-permute-done.2 = f32[1024,128]{0,1:T(8,128)S(1)} collective-permute-done((f32[1024,128]{0,1:T(8,128)S(1)}, f32[1024,128]{0,1:T(8,128)S(1)}, u32[]{:S(2)}, u32[]{:S(2)}) %collective-permute-start.2) | collective-permute-done | bytes 524320 | tf_op jit(solution)/shard_map/ppermute | solution.py:19
  26.3 6.5 %fusion.4 = f32[512,128]{0,1:T(8,128)S(1)} fusion(f32[1,512,2048]{2,1,0:T(8,128)} %param.7, f32[1024,128]{0,1:T(8,128)S(1)} %maximum_select_fusion.4, f32[1024,128]{0,1:T(8,128)S(1)} %collective-permute-done.2, pred[]{:T(512)S(6)} %eq.23), kind=kOutput, calls=%fused_computation.4 | convolution fusion | flops 1611399168 | bytes 5505025 | tf_op jit(solution)/shard_map/dot_general | solution.py:61
  32.8 2.6 %collective-permute-start.3 = (f32[512,128]{0,1:T(8,128)S(1)}, f32[512,128]{0,1:T(8,128)S(1)}, u32[]{:S(2)}, u32[]{:S(2)}) collective-permute-start(f32[512,128]{0,1:T(8,128)S(1)} %fusion.4), channel_id=1, source_target_pairs={{0,8},{8,0},{1,9},{9,1},{2,10},{10,2},{3,11},{11,3},{4,12},{12,4},... | collective-permute-start | bytes 786440 | tf_op jit(solution)/shard_map/ppermute | solution.py:19
  35.4 0.0 copy-start.1
  35.4 0.0 copy-start.2
  35.4 10.9 %collective-permute-done.3 = f32[512,128]{0,1:T(8,128)S(1)} collective-permute-done((f32[512,128]{0,1:T(8,128)S(1)}, f32[512,128]{0,1:T(8,128)S(1)}, u32[]{:S(2)}, u32[]{:S(2)}) %collective-permute-start.3) | collective-permute-done | bytes 262176 | tf_op jit(solution)/shard_map/ppermute | solution.py:19
  46.4 3.0 %collective-permute-start.4 = (f32[256,128]{0,1:T(8,128)S(1)}, f32[256,128]{0,1:T(8,128)S(1)}, u32[]{:S(2)}, u32[]{:S(2)}) collective-permute-start(f32[256,128]{0,1:T(8,128)S(1)} %dynamic-slice_add_fusion.1), channel_id=1, source_target_pairs={{0,16},{1,17},{2,18},{3,19},{4,20},{5,21},{6,22},{7,23},{8,24},{9,... | collective-permute-start | bytes 393224 | tf_op jit(solution)/shard_map/while/body/eval_jaxpr/ppermute | solution.py:25
  49.4 2.5 %collective-permute-done.4 = f32[256,128]{0,1:T(8,128)S(1)} collective-permute-done((f32[256,128]{0,1:T(8,128)S(1)}, f32[256,128]{0,1:T(8,128)S(1)}, u32[]{:S(2)}, u32[]{:S(2)}) %collective-permute-start.4) | collective-permute-done | bytes 131104 | tf_op jit(solution)/shard_map/while/body/eval_jaxpr/ppermute | solution.py:25
  51.9 0.0 collective-permute-start.5
  51.9 1.3 collective-permute-done.5
  53.3 1.6 %collective-permute-start.6 = (f32[512,128]{0,1:T(8,128)S(1)}, f32[512,128]{0,1:T(8,128)S(1)}, u32[]{:S(2)}, u32[]{:S(2)}) collective-permute-start(f32[512,128]{0,1:T(8,128)S(1)} %maximum_select_fusion.7), channel_id=1, source_target_pairs={{0,2},{2,0},{1,3},{3,1},{4,6},{6,4},{5,7},{7,5},{8,10},{10,8},{9,1... | collective-permute-start | bytes 786440 | tf_op jit(solution)/shard_map/while/body/eval_jaxpr/ppermute | solution.py:19
  54.8 6.9 %collective-permute-done.6 = f32[512,128]{0,1:T(8,128)S(1)} collective-permute-done((f32[512,128]{0,1:T(8,128)S(1)}, f32[512,128]{0,1:T(8,128)S(1)}, u32[]{:S(2)}, u32[]{:S(2)}) %collective-permute-start.6) | collective-permute-done | bytes 262176 | tf_op jit(solution)/shard_map/while/body/eval_jaxpr/ppermute | solution.py:19
  61.8 1.2 collective-permute-start.7
  62.9 12.1 %collective-permute-done.7 = f32[1024,128]{0,1:T(8,128)S(1)} collective-permute-done((f32[1024,128]{0,1:T(8,128)S(1)}, f32[1024,128]{0,1:T(8,128)S(1)}, u32[]{:S(2)}, u32[]{:S(2)}) %collective-permute-start.7) | collective-permute-done | bytes 524320 | tf_op jit(solution)/shard_map/while/body/eval_jaxpr/ppermute | solution.py:19
  75.0 6.5 %fusion.7 = f32[512,128]{0,1:T(8,128)S(1)} fusion(f32[1,512,2048]{2,1,0:T(8,128)} %param.6, f32[1024,128]{0,1:T(8,128)S(1)} %maximum_select_fusion.5, f32[1024,128]{0,1:T(8,128)S(1)} %collective-permute-done.7, pred[]{:T(512)S(6)} %eq.23), kind=kOutput, calls=%fused_computation.5 | convolution fusion | flops 1611399168 | bytes 5505025 | tf_op jit(solution)/shard_map/while/body/eval_jaxpr/dot_general | solution.py:61
  81.5 2.8 %collective-permute-start.8 = (f32[512,128]{0,1:T(8,128)S(1)}, f32[512,128]{0,1:T(8,128)S(1)}, u32[]{:S(2)}, u32[]{:S(2)}) collective-permute-start(f32[512,128]{0,1:T(8,128)S(1)} %fusion.7), channel_id=1, source_target_pairs={{0,8},{8,0},{1,9},{9,1},{2,10},{10,2},{3,11},{11,3},{4,12},{12,4},... | collective-permute-start | bytes 786440 | tf_op jit(solution)/shard_map/while/body/eval_jaxpr/ppermute | solution.py:19
  84.3 10.8 %collective-permute-done.8 = f32[512,128]{0,1:T(8,128)S(1)} collective-permute-done((f32[512,128]{0,1:T(8,128)S(1)}, f32[512,128]{0,1:T(8,128)S(1)}, u32[]{:S(2)}, u32[]{:S(2)}) %collective-permute-start.8) | collective-permute-done | bytes 262176 | tf_op jit(solution)/shard_map/while/body/eval_jaxpr/ppermute | solution.py:19
  95.1 0.0 copy-done
  95.1 0.3 convolution_bitcast_fusion.1
  95.4 40.9 %psum.7 = f32[64,128]{1,0:T(8,128)S(1)} all-reduce(f32[64,128]{1,0:T(8,128)S(1)} %convolution_bitcast_fusion.1), channel_id=1, replica_groups=mesh['tm'=2,'blk'=16] {'tm','blk'}, use_global_device_ids=true, to_apply=%region_0.1 | all-reduce | flops 8192 | bytes 65536 | tf_op jit(solution)/shard_map/psum | solution.py:77
  136.3 0.8 copy.9
  137.1 0.0 copy-done.1
  137.1 0.0 copy-done.2
  137.1 0.8 convolution_bitcast_fusion
  (6 shorter events, 0.2 us)
Async XLA Ops:
  0.6 94.5 %copy-start = (f32[1,64,256]{2,1,0:T(8,128)S(1)}, f32[1,64,256]{2,1,0:T(8,128)}, u32[]{:S(2)}) copy-start(f32[1,64,256]{2,1,0:T(8,128)} %param.9) | copy-start | bytes 196612
  1.7 1.5 %collective-permute-start = (f32[256,128]{0,1:T(8,128)S(1)}, f32[256,128]{0,1:T(8,128)S(1)}, u32[]{:S(2)}, u32[]{:S(2)}) collective-permute-start(f32[256,128]{0,1:T(8,128)S(1)} %bitcast.26), channel_id=1, source_target_pairs={{0,1},{1,0},{2,3},{3,2},{4,5},{5,4},{6,7},{7,6},{8,9},{9,8},{10,11... | collective-permute-start | bytes 393224 | tf_op jit(solution)/shard_map/ppermute | solution.py:19
  3.2 9.5 %collective-permute-start.1 = (f32[512,128]{0,1:T(8,128)S(1)}, f32[512,128]{0,1:T(8,128)S(1)}, u32[]{:S(2)}, u32[]{:S(2)}) collective-permute-start(f32[512,128]{0,1:T(8,128)S(1)} %maximum_select_fusion.6), channel_id=1, source_target_pairs={{0,2},{2,0},{1,3},{3,1},{4,6},{6,4},{5,7},{7,5},{8,10},{10,8},{9,1... | collective-permute-start | bytes 786440 | tf_op jit(solution)/shard_map/ppermute | solution.py:19
  12.8 13.5 %collective-permute-start.2 = (f32[1024,128]{0,1:T(8,128)S(1)}, f32[1024,128]{0,1:T(8,128)S(1)}, u32[]{:S(2)}, u32[]{:S(2)}) collective-permute-start(f32[1024,128]{0,1:T(8,128)S(1)} %maximum_select_fusion.4), channel_id=1, source_target_pairs={{0,4},{4,0},{1,5},{5,1},{2,6},{6,2},{3,7},{7,3},{8,12},{12,8},{9,1... | collective-permute-start | bytes 1572872 | tf_op jit(solution)/shard_map/ppermute | solution.py:19
  32.8 13.5 %collective-permute-start.3 = (f32[512,128]{0,1:T(8,128)S(1)}, f32[512,128]{0,1:T(8,128)S(1)}, u32[]{:S(2)}, u32[]{:S(2)}) collective-permute-start(f32[512,128]{0,1:T(8,128)S(1)} %fusion.4), channel_id=1, source_target_pairs={{0,8},{8,0},{1,9},{9,1},{2,10},{10,2},{3,11},{11,3},{4,12},{12,4},... | collective-permute-start | bytes 786440 | tf_op jit(solution)/shard_map/ppermute | solution.py:19
  35.4 101.7 %copy-start.1 = (f32[64,64]{1,0:T(8,128)S(1)}, f32[64,64]{1,0:T(8,128)}, u32[]{:S(2)}) copy-start(f32[64,64]{1,0:T(8,128)} %param.10) | copy-start | bytes 49156
  35.4 101.7 %copy-start.2 = (f32[64,128]{1,0:T(8,128)S(1)}, f32[64,128]{1,0:T(8,128)}, u32[]{:S(2)}) copy-start(f32[64,128]{1,0:T(8,128)} %param.11) | copy-start | bytes 98308
  46.4 5.5 %collective-permute-start.4 = (f32[256,128]{0,1:T(8,128)S(1)}, f32[256,128]{0,1:T(8,128)S(1)}, u32[]{:S(2)}, u32[]{:S(2)}) collective-permute-start(f32[256,128]{0,1:T(8,128)S(1)} %dynamic-slice_add_fusion.1), channel_id=1, source_target_pairs={{0,16},{1,17},{2,18},{3,19},{4,20},{5,21},{6,22},{7,23},{8,24},{9,... | collective-permute-start | bytes 393224 | tf_op jit(solution)/shard_map/while/body/eval_jaxpr/ppermute | solution.py:25
  51.9 1.3 collective-permute-start.5
  53.3 8.4 %collective-permute-start.6 = (f32[512,128]{0,1:T(8,128)S(1)}, f32[512,128]{0,1:T(8,128)S(1)}, u32[]{:S(2)}, u32[]{:S(2)}) collective-permute-start(f32[512,128]{0,1:T(8,128)S(1)} %maximum_select_fusion.7), channel_id=1, source_target_pairs={{0,2},{2,0},{1,3},{3,1},{4,6},{6,4},{5,7},{7,5},{8,10},{10,8},{9,1... | collective-permute-start | bytes 786440 | tf_op jit(solution)/shard_map/while/body/eval_jaxpr/ppermute | solution.py:19
  61.8 13.2 %collective-permute-start.7 = (f32[1024,128]{0,1:T(8,128)S(1)}, f32[1024,128]{0,1:T(8,128)S(1)}, u32[]{:S(2)}, u32[]{:S(2)}) collective-permute-start(f32[1024,128]{0,1:T(8,128)S(1)} %maximum_select_fusion.5), channel_id=1, source_target_pairs={{0,4},{4,0},{1,5},{5,1},{2,6},{6,2},{3,7},{7,3},{8,12},{12,8},{9,1... | collective-permute-start | bytes 1572872 | tf_op jit(solution)/shard_map/while/body/eval_jaxpr/ppermute | solution.py:19
  81.5 13.6 %collective-permute-start.8 = (f32[512,128]{0,1:T(8,128)S(1)}, f32[512,128]{0,1:T(8,128)S(1)}, u32[]{:S(2)}, u32[]{:S(2)}) collective-permute-start(f32[512,128]{0,1:T(8,128)S(1)} %fusion.7), channel_id=1, source_target_pairs={{0,8},{8,0},{1,9},{9,1},{2,10},{10,2},{3,11},{11,3},{4,12},{12,4},... | collective-permute-start | bytes 786440 | tf_op jit(solution)/shard_map/while/body/eval_jaxpr/ppermute | solution.py:19
where the time goes:
time: 138 us
  waiting for transfers between devices  63.7 us (46%)
  blocking collectives  40.9 us (30%)
  starting transfers between devices  16.4 us (12%)
  matrix products  14.1 us (10%)
  local copies, waits for them, and re-layouts  1.8 us (1%)
    ppermute x8, waiting for transfers between devices, swapped(): return lax.ppermute(block, axis, route)  61.2 us
    psum x1, blocking collectives, on_device(): summed = lax.psum(partial_tip, ('tm', 'blk'))  40.9 us
    ppermute x8, starting transfers between devices, swapped(): return lax.ppermute(block, axis, route)  13.4 us
    dot_general x2, matrix products, apply_tile(): jnp.dot(tile, columns, precision=HIGHEST_PREC, preferred_element_type=jnp...  13 us
    ppermute x1, starting transfers between devices, from_behind(): return lax.ppermute(block, axis, route)  3.02 us
  transfers between devices with their start and end apart: 9, of which 9 were waited for; matrix products, arithmetic and copies ran while one was open for 0% of the time, Pallas kernels for 0%

commit v1 on v0

v1 whole, which is shorter than its diff:
```python
import jax
import jax.numpy as jnp
from jax import lax
from jax.sharding import PartitionSpec as P

GROUP = 8
AXES = ("tm", "blk")
HIGH = lax.Precision.HIGH


def dot(a, b):
    return jnp.dot(a, b, precision=HIGH, preferred_element_type=jnp.float32)


def on_device(propagator, inv_diag, rhs, arrow, tip_inv, tip_rhs):
    steps = lax.axis_size("tm")
    blocks = lax.axis_size("blk")
    high_count = blocks // GROUP
    position = lax.axis_index("blk")
    low = position % GROUP
    high = position // GROUP
    piece = rhs.shape[1]
    width = rhs.shape[2]

    def move(value, flip, sources=None, ahead=0):
        sources = range(steps) if sources is None else sources
        route = [
            (t * blocks + b, (t + ahead) * blocks + (b ^ flip))
            for t in sources
            for b in range(blocks)
        ]
        return lax.ppermute(value, AXES, route)

    def gather(own, sources=None):
        parts = {0: own}
        for flip in range(2, GROUP, 2):
            parts[flip] = move(own, flip, sources)
        for flip in range(0, GROUP, 2):
            parts[flip + 1] = move(parts[flip], 1, sources)
        return parts

    def apply_tile(tile, parts):
        columns = jnp.zeros((tile.shape[1], width), jnp.float32)
        for flip, part in parts.items():
            columns = lax.dynamic_update_slice_in_dim(columns, part, (low ^ flip) * piece, 0)
        return dot(tile, columns)

    def row_block(partial, flip):
        return lax.dynamic_slice_in_dim(partial, (high ^ flip) * piece, piece, 0)

    partial = apply_tile(inv_diag[0], gather(rhs[0]))
    for t in range(steps - 1):
        earlier = sum(
            move(row_block(partial, e), e * GROUP, (t,), 1) for e in range(high_count)
        )
        partial = partial - apply_tile(propagator[0], gather(earlier, (t + 1,)))

    solved = row_block(partial, 0)
    for e in range(1, high_count):
        solved = solved + move(row_block(partial, e), e * GROUP)

    arrows = [arrow[0]] + [move(arrow[0], e * GROUP) for e in range(1, high_count)]
    terms = sum(dot(arrows[e], row_block(partial, e)) for e in range(high_count))
    flips = [1 << k for k in range(blocks.bit_length() - 1)]
    terms = terms + move(terms, flips[0])
    terms = terms + move(terms, flips[1]) + move(terms, flips[2]) + move(terms, flips[1] | flips[2])
    for flip in flips[3:]:
        terms = terms + move(terms, flip)
    for k in range(steps.bit_length() - 1):
        ring = [
            (t * blocks + b, (t ^ 1 << k) * blocks + b)
            for t in range(steps)
            for b in range(blocks)
        ]
        terms = terms + lax.ppermute(terms, AXES, ring)
    tip = dot(tip_inv, tip_rhs - terms)
    return solved[None], tip


def solution(mesh):
    placed = (
        P("tm", "blk", None),
        P("tm", "blk", None),
        P("tm", "blk", None),
        P("tm", None, "blk"),
        P(),
        P(),
    )
    return jax.shard_map(
        on_device,
        mesh=mesh,
        in_specs=placed,
        out_specs=(P("tm", "blk", None), P()),
        check_vma=False,
    )
```

time: 138 us -> 75.9 us (0.55)
  waiting for transfers between devices: 63.7 us -> 15.6 us
  blocking collectives: 40.9 us -> 0 us
  starting transfers between devices: 16.4 us -> 47.7 us
  matrix products: 14.1 us -> 8.03 us
    ppermute x9 -> x24, waiting for transfers between devices: 63.7 us -> 15.6 us  [the longest x23 14.5 us: move(): return lax.ppermute(value, AXES, route)]
    psum x1 -> x0, blocking collectives: 40.9 us -> none  [on_device(): summed = lax.psum(partial_tip, ('tm', 'blk'))]
    ppermute x9 -> x24, starting transfers between devices: 16.4 us -> 47.7 us  [the longest x23 29.1 us: move(): return lax.ppermute(value, AXES, route)]
    dot_general x4 -> x5, matrix products: 14.1 us -> 8.03 us  [dot(): return jnp.dot(a, b, precision=HIGH, preferred_element_type=jnp.float32)]
  transfers between devices with their start and end apart: 9 -> 24, of which waited for: 9 -> 10; matrix products, arithmetic and copies ran while one was open for 0% -> 7% of each run, Pallas kernels for 0% -> 0%
where the time goes in v1:
time: 75.9 us; the launch traced here: 75.5 us
  starting transfers between devices  47.7 us (63%)
  waiting for transfers between devices  15.6 us (21%)
  matrix products  8.03 us (11%)
  local copies, waits for them, and re-layouts  2.97 us (4%)
  between operations  1.21 us (2%)
    ppermute x23, starting transfers between devices, move(): return lax.ppermute(value, AXES, route)  29.1 us
    ppermute x1, starting transfers between devices, on_device(): terms = terms + lax.ppermute(terms, AXES, ring)  18.6 us
    ppermute x23, waiting for transfers between devices, move(): return lax.ppermute(value, AXES, route)  14.5 us
    dot_general x5, matrix products, dot(): return jnp.dot(a, b, precision=HIGH, preferred_element_type=jnp.float32)  8.03 us
  transfers between devices with their start and end apart: 24, of which 10 were waited for; matrix products, arithmetic and copies ran while one was open for 7% of the time, Pallas kernels for 0%

profile of v1, /device:TPU:0, one launch (start us, length us, event | category | flops | bytes accessed | tf_op | source)
XLA Modules:
  0.0 75.5 jit_solution(4790133616103588803)
XLA Ops:
  0.6 0.0 copy-start
  0.6 3.0 %collective-permute-start = (f32[256,128]{1,0:T(8,128)}, f32[256,128]{1,0:T(8,128)S(1)}, u32[]{:S(2)}, u32[]{:S(2)}) collective-permute-start(f32[256,128]{1,0:T(8,128)} %bitcast.32), channel_id=1, source_target_pairs={{0,2},{1,3},{2,0},{3,1},{4,6},{5,7},{6,4},{7,5},{8,10},{9,11},{10,... | collective-permute-start | bytes 393224 | tf_op jit(solution)/shard_map/ppermute | solution.py:32
  3.6 1.6 %collective-permute-start.1 = (f32[256,128]{1,0:T(8,128)}, f32[256,128]{1,0:T(8,128)S(1)}, u32[]{:S(2)}, u32[]{:S(2)}) collective-permute-start(f32[256,128]{1,0:T(8,128)} %bitcast.33), channel_id=1, source_target_pairs={{0,4},{1,5},{2,6},{3,7},{4,0},{5,1},{6,2},{7,3},{8,12},{9,13},{10,... | collective-permute-start | bytes 393224 | tf_op jit(solution)/shard_map/ppermute | solution.py:32
  5.2 0.0 collective-permute-start.2
  5.2 1.1 %copy.8 = f32[256,128]{0,1:T(8,128)S(1)} copy(f32[256,128]{1,0:T(8,128)} %bitcast.36) | data formatting | bytes 262144 | tf_op jit(solution)/shard_map/squeeze | solution.py:51
  6.3 0.1 broadcast.5.clone
  6.5 0.8 %collective-permute-done = f32[256,128]{1,0:T(8,128)S(1)} collective-permute-done((f32[256,128]{1,0:T(8,128)}, f32[256,128]{1,0:T(8,128)S(1)}, u32[]{:S(2)}, u32[]{:S(2)}) %collective-permute-start) | collective-permute-done | bytes 131104 | tf_op jit(solution)/shard_map/ppermute | solution.py:32
  7.4 0.1 copy.9
  7.5 2.7 %collective-permute-done.1 = f32[256,128]{1,0:T(8,128)S(1)} collective-permute-done((f32[256,128]{1,0:T(8,128)}, f32[256,128]{1,0:T(8,128)S(1)}, u32[]{:S(2)}, u32[]{:S(2)}) %collective-permute-start.1) | collective-permute-done | bytes 131104 | tf_op jit(solution)/shard_map/ppermute | solution.py:32
  10.2 0.1 copy.10
  10.3 0.1 collective-permute-start.4
  10.4 1.0 %collective-permute-done.2 = f32[256,128]{1,0:T(8,128)S(1)} collective-permute-done((f32[256,128]{1,0:T(8,128)}, f32[256,128]{1,0:T(8,128)S(1)}, u32[]{:S(2)}, u32[]{:S(2)}) %collective-permute-start.2) | collective-permute-done | bytes 131104 | tf_op jit(solution)/shard_map/ppermute | solution.py:32
  11.5 0.1 copy.11
  11.6 0.1 collective-permute-start.5
  11.7 0.1 copy.12
  11.8 0.6 collective-permute-start.6
  12.4 0.0 collective-permute-done.4
  12.4 0.1 copy.13
  12.5 0.5 collective-permute-done.5
  13.0 0.1 copy.14
  13.1 0.0 copy-start.2
  13.1 0.2 collective-permute-done.6
  13.3 0.1 copy.15
  13.5 0.0 copy-start.1
  13.5 4.5 %fusion.2 = f32[128,512]{1,0:T(8,128)S(1)} fusion(f32[2048,128]{0,1:T(8,128)S(1)} %constant_dynamic-update-slice_fusion.8, f32[1,512,2048]{2,1,0:T(8,128)} %param.7), kind=kOutput, calls=%fused_computation.2 | convolution fusion | flops 805306368 | bytes 5505024 | tf_op jit(solution)/shard_map/dot_general | solution.py:12
  18.1 3.6 %collective-permute-start.7 = (f32[256,128]{0,1:T(8,128)S(1)}, f32[256,128]{0,1:T(8,128)S(1)}, u32[]{:S(2)}, u32[]{:S(2)}) collective-permute-start(f32[256,128]{0,1:T(8,128)S(1)} %get-tuple-element.7), channel_id=1, source_target_pairs={{0,16},{1,17},{2,18},{3,19},{4,20},{5,21},{6,22},{7,23},{8,24},{9,... | collective-permute-start | bytes 393224 | tf_op jit(solution)/shard_map/ppermute | solution.py:32
  21.6 3.3 %collective-permute-start.8 = (f32[256,128]{0,1:T(8,128)S(1)}, f32[256,128]{0,1:T(8,128)S(1)}, u32[]{:S(2)}, u32[]{:S(2)}) collective-permute-start(f32[256,128]{0,1:T(8,128)S(1)} %get-tuple-element.6), channel_id=1, source_target_pairs={{0,24},{1,25},{2,26},{3,27},{4,28},{5,29},{6,30},{7,31},{8,16},{9,... | collective-permute-start | bytes 393224 | tf_op jit(solution)/shard_map/ppermute | solution.py:32
  25.0 3.3 %collective-permute-done.8 = f32[256,128]{0,1:T(8,128)S(1)} collective-permute-done((f32[256,128]{0,1:T(8,128)S(1)}, f32[256,128]{0,1:T(8,128)S(1)}, u32[]{:S(2)}, u32[]{:S(2)}) %collective-permute-start.8) | collective-permute-done | bytes 131104 | tf_op jit(solution)/shard_map/ppermute | solution.py:32
  28.3 0.1 broadcast.5
  28.4 0.7 collective-permute-start.9
  29.1 0.7 collective-permute-start.10
  29.8 3.4 %collective-permute-start.17 = (f32[64,256]{1,0:T(8,128)S(1)}, f32[64,256]{1,0:T(8,128)S(1)}, u32[]{:S(2)}, u32[]{:S(2)}) collective-permute-start(f32[64,256]{1,0:T(8,128)S(1)} %bitcast.37), channel_id=1, source_target_pairs={{0,8},{1,9},{2,10},{3,11},{4,12},{5,13},{6,14},{7,15},{8,0},{9,1},... | collective-permute-start | bytes 196616 | tf_op jit(solution)/shard_map/ppermute | solution.py:32
  33.2 0.7 collective-permute-start.11
  33.8 0.7 collective-permute-start.12
  34.5 0.0 collective-permute-done.9
  34.5 0.7 collective-permute-start.13
  35.2 0.0 collective-permute-done.10
  35.2 0.7 collective-permute-start.14
  35.9 0.0 collective-permute-done.11
  35.9 0.7 collective-permute-start.15
  36.6 0.0 collective-permute-done.12
  36.7 0.0 copy-start.3
  36.7 0.0 collective-permute-done.13
  36.7 0.0 collective-permute-done.14
  36.8 2.3 %fusion.4 = f32[128,512]{1,0:T(8,128)S(1)} fusion(f32[128,512]{1,0:T(8,128)S(1)} %fusion.2, f32[2048,128]{0,1:T(8,128)S(1)} %constant_dynamic-update-slice_fusion, f32[1,512,2048]{2,1,0:T(8,128)S(1)} %copy-done.1), kind=kOutput, calls=%fused_computation.4 | convolution fusion | flops 805371904 | bytes 5767168 | tf_op jit(solution)/shard_map/dot_general | solution.py:12
  39.1 0.2 fusion.10
  39.3 0.0 collective-permute-done.17
  39.3 0.2 fusion.7
  39.6 0.1 collective-permute-start.18
  39.6 1.2 %collective-permute-done.18 = f32[64,128]{1,0:T(8,128)S(1)} collective-permute-done((f32[64,128]{1,0:T(8,128)S(1)}, f32[64,128]{1,0:T(8,128)S(1)}, u32[]{:S(2)}, u32[]{:S(2)}) %collective-permute-start.18) | collective-permute-done | bytes 32800 | tf_op jit(solution)/shard_map/ppermute | solution.py:32
  40.8 1.5 %collective-permute-start.19 = (f32[64,128]{1,0:T(8,128)S(1)}, f32[64,128]{1,0:T(8,128)S(1)}, u32[]{:S(2)}, u32[]{:S(2)}) collective-permute-start(f32[64,128]{1,0:T(8,128)S(1)} %add.92), channel_id=1, source_target_pairs={{0,2},{1,3},{2,0},{3,1},{4,6},{5,7},{6,4},{7,5},{8,10},{9,11},{10,... | collective-permute-start | bytes 98312 | tf_op jit(solution)/shard_map/ppermute | solution.py:32
  42.3 0.9 %collective-permute-start.20 = (f32[64,128]{1,0:T(8,128)S(1)}, f32[64,128]{1,0:T(8,128)S(1)}, u32[]{:S(2)}, u32[]{:S(2)}) collective-permute-start(f32[64,128]{1,0:T(8,128)S(1)} %add.92), channel_id=1, source_target_pairs={{0,4},{1,5},{2,6},{3,7},{4,0},{5,1},{6,2},{7,3},{8,12},{9,13},{10,... | collective-permute-start | bytes 98312 | tf_op jit(solution)/shard_map/ppermute | solution.py:32
  43.3 1.1 %collective-permute-start.21 = (f32[64,128]{1,0:T(8,128)S(1)}, f32[64,128]{1,0:T(8,128)S(1)}, u32[]{:S(2)}, u32[]{:S(2)}) collective-permute-start(f32[64,128]{1,0:T(8,128)S(1)} %add.92), channel_id=1, source_target_pairs={{0,6},{1,7},{2,4},{3,5},{4,2},{5,3},{6,0},{7,1},{8,14},{9,15},{10,... | collective-permute-start | bytes 98312 | tf_op jit(solution)/shard_map/ppermute | solution.py:32
  44.4 1.9 %collective-permute-start.16 = (f32[256,128]{0,1:T(8,128)S(1)}, f32[256,128]{0,1:T(8,128)S(1)}, u32[]{:S(2)}, u32[]{:S(2)}) collective-permute-start(f32[256,128]{0,1:T(8,128)S(1)} %dynamic-slice_bitcast_fusion.2), channel_id=1, source_target_pairs={{0,8},{1,9},{2,10},{3,11},{4,12},{5,13},{6,14},{7,15},{8,0},{9,1},... | collective-permute-start | bytes 393224 | tf_op jit(solution)/shard_map/ppermute | solution.py:32
  46.2 0.0 collective-permute-done.19
  46.3 0.0 collective-permute-done.20
  46.3 1.8 %collective-permute-done.21 = f32[64,128]{1,0:T(8,128)S(1)} collective-permute-done((f32[64,128]{1,0:T(8,128)S(1)}, f32[64,128]{1,0:T(8,128)S(1)}, u32[]{:S(2)}, u32[]{:S(2)}) %collective-permute-start.21) | collective-permute-done | bytes 32800 | tf_op jit(solution)/shard_map/ppermute | solution.py:32
  48.1 3.4 %collective-permute-start.22 = (f32[64,128]{1,0:T(8,128)S(1)}, f32[64,128]{1,0:T(8,128)S(1)}, u32[]{:S(2)}, u32[]{:S(2)}) collective-permute-start(f32[64,128]{1,0:T(8,128)S(1)} %add_add_fusion), channel_id=1, source_target_pairs={{0,8},{1,9},{2,10},{3,11},{4,12},{5,13},{6,14},{7,15},{8,0},{9,1},... | collective-permute-start | bytes 98312 | tf_op jit(solution)/shard_map/ppermute | solution.py:32
  51.5 2.8 %collective-permute-done.22 = f32[64,128]{1,0:T(8,128)S(1)} collective-permute-done((f32[64,128]{1,0:T(8,128)S(1)}, f32[64,128]{1,0:T(8,128)S(1)}, u32[]{:S(2)}, u32[]{:S(2)}) %collective-permute-start.22) | collective-permute-done | bytes 32800 | tf_op jit(solution)/shard_map/ppermute | solution.py:32
  54.3 18.6 %collective-permute-start.23 = (f32[64,128]{1,0:T(8,128)S(1)}, f32[64,128]{1,0:T(8,128)S(1)}, u32[]{:S(2)}, u32[]{:S(2)}) collective-permute-start(f32[64,128]{1,0:T(8,128)S(1)} %add.96), channel_id=1, source_target_pairs={{0,16},{1,17},{2,18},{3,19},{4,20},{5,21},{6,22},{7,23},{8,24},{9,... | collective-permute-start | bytes 98312 | tf_op jit(solution)/shard_map/ppermute | solution.py:75
  72.9 0.0 collective-permute-done.16
  72.9 0.8 %copy.16 = f32[1,256,128]{2,1,0:T(8,128)} copy(f32[1,256,128]{1,2,0:T(8,128)S(1)} %fusion.8) | data formatting | bytes 262144
  73.6 1.1 %collective-permute-done.23 = f32[64,128]{1,0:T(8,128)S(1)} collective-permute-done((f32[64,128]{1,0:T(8,128)S(1)}, f32[64,128]{1,0:T(8,128)S(1)}, u32[]{:S(2)}, u32[]{:S(2)}) %collective-permute-start.23) | collective-permute-done | bytes 32800 | tf_op jit(solution)/shard_map/ppermute | solution.py:75
  74.8 0.8 %convolution_bitcast_fusion = f32[64,128]{1,0:T(8,128)} fusion(f32[64,64]{1,0:T(8,128)S(1)} %copy-done, f32[64,128]{1,0:T(8,128)S(1)} %copy-done.3, f32[64,128]{1,0:T(8,128)S(1)} %add.96, f32[64,128]{1,0:T(8,128)S(1)} %collective-permute-done.23), kind=kOutput, calls=%fused_computation.5 | convolution fusion | flops 3162112 | bytes 147456 | tf_op jit(solution)/shard_map/dot_general | solution.py:12
  (30 shorter events, 0.4 us)
Async XLA Ops:
  0.6 74.1 %copy-start = (f32[64,64]{1,0:T(8,128)S(1)}, f32[64,64]{1,0:T(8,128)}, u32[]{:S(2)}) copy-start(f32[64,64]{1,0:T(8,128)} %param.10) | copy-start | bytes 49156
  0.6 6.7 %collective-permute-start = (f32[256,128]{1,0:T(8,128)}, f32[256,128]{1,0:T(8,128)S(1)}, u32[]{:S(2)}, u32[]{:S(2)}) collective-permute-start(f32[256,128]{1,0:T(8,128)} %bitcast.32), channel_id=1, source_target_pairs={{0,2},{1,3},{2,0},{3,1},{4,6},{5,7},{6,4},{7,5},{8,10},{9,11},{10,... | collective-permute-start | bytes 393224 | tf_op jit(solution)/shard_map/ppermute | solution.py:32
  3.6 6.6 %collective-permute-start.1 = (f32[256,128]{1,0:T(8,128)}, f32[256,128]{1,0:T(8,128)S(1)}, u32[]{:S(2)}, u32[]{:S(2)}) collective-permute-start(f32[256,128]{1,0:T(8,128)} %bitcast.33), channel_id=1, source_target_pairs={{0,4},{1,5},{2,6},{3,7},{4,0},{5,1},{6,2},{7,3},{8,12},{9,13},{10,... | collective-permute-start | bytes 393224 | tf_op jit(solution)/shard_map/ppermute | solution.py:32
  5.2 6.2 %collective-permute-start.2 = (f32[256,128]{1,0:T(8,128)}, f32[256,128]{1,0:T(8,128)S(1)}, u32[]{:S(2)}, u32[]{:S(2)}) collective-permute-start(f32[256,128]{1,0:T(8,128)} %bitcast.34), channel_id=1, source_target_pairs={{0,6},{1,7},{2,4},{3,5},{4,2},{5,3},{6,0},{7,1},{8,14},{9,15},{10,... | collective-permute-start | bytes 393224 | tf_op jit(solution)/shard_map/ppermute | solution.py:32
  5.2 6.4 %collective-permute-start.3 = (f32[256,128]{1,0:T(8,128)}, f32[256,128]{1,0:T(8,128)S(1)}, u32[]{:S(2)}, u32[]{:S(2)}) collective-permute-start(f32[256,128]{1,0:T(8,128)} %bitcast.35), channel_id=1, source_target_pairs={{0,1},{1,0},{2,3},{3,2},{4,5},{5,4},{6,7},{7,6},{8,9},{9,8},{10,11... | collective-permute-start | bytes 393224 | tf_op jit(solution)/shard_map/ppermute | solution.py:32
  10.3 2.0 %collective-permute-start.4 = (f32[256,128]{1,0:T(8,128)S(1)}, f32[256,128]{1,0:T(8,128)S(1)}, u32[]{:S(2)}, u32[]{:S(2)}) collective-permute-start(f32[256,128]{1,0:T(8,128)S(1)} %collective-permute-done), channel_id=1, source_target_pairs={{0,1},{1,0},{2,3},{3,2},{4,5},{5,4},{6,7},{7,6},{8,9},{9,8},{10,11... | collective-permute-start | bytes 393224 | tf_op jit(solution)/shard_map/ppermute | solution.py:32
  11.6 1.4 %collective-permute-start.5 = (f32[256,128]{1,0:T(8,128)S(1)}, f32[256,128]{1,0:T(8,128)S(1)}, u32[]{:S(2)}, u32[]{:S(2)}) collective-permute-start(f32[256,128]{1,0:T(8,128)S(1)} %collective-permute-done.1), channel_id=1, source_target_pairs={{0,1},{1,0},{2,3},{3,2},{4,5},{5,4},{6,7},{7,6},{8,9},{9,8},{10,11... | collective-permute-start | bytes 393224 | tf_op jit(solution)/shard_map/ppermute | solution.py:32
  11.8 1.5 %collective-permute-start.6 = (f32[256,128]{1,0:T(8,128)S(1)}, f32[256,128]{1,0:T(8,128)S(1)}, u32[]{:S(2)}, u32[]{:S(2)}) collective-permute-start(f32[256,128]{1,0:T(8,128)S(1)} %collective-permute-done.2), channel_id=1, source_target_pairs={{0,1},{1,0},{2,3},{3,2},{4,5},{5,4},{6,7},{7,6},{8,9},{9,8},{10,11... | collective-permute-start | bytes 393224 | tf_op jit(solution)/shard_map/ppermute | solution.py:32
  13.1 16.6 %copy-start.2 = (f32[1,64,256]{2,1,0:T(8,128)S(1)}, f32[1,64,256]{2,1,0:T(8,128)}, u32[]{:S(2)}) copy-start(f32[1,64,256]{2,1,0:T(8,128)} %param.9) | copy-start | bytes 196612
  13.5 23.3 %copy-start.1 = (f32[1,512,2048]{2,1,0:T(8,128)S(1)}, f32[1,512,2048]{2,1,0:T(8,128)}, u32[]{:S(2)}) copy-start(f32[1,512,2048]{2,1,0:T(8,128)} %param.6) | copy-start | bytes 12582916
  18.1 6.9 %collective-permute-start.7 = (f32[256,128]{0,1:T(8,128)S(1)}, f32[256,128]{0,1:T(8,128)S(1)}, u32[]{:S(2)}, u32[]{:S(2)}) collective-permute-start(f32[256,128]{0,1:T(8,128)S(1)} %get-tuple-element.7), channel_id=1, source_target_pairs={{0,16},{1,17},{2,18},{3,19},{4,20},{5,21},{6,22},{7,23},{8,24},{9,... | collective-permute-start | bytes 393224 | tf_op jit(solution)/shard_map/ppermute | solution.py:32
  21.6 6.6 %collective-permute-start.8 = (f32[256,128]{0,1:T(8,128)S(1)}, f32[256,128]{0,1:T(8,128)S(1)}, u32[]{:S(2)}, u32[]{:S(2)}) collective-permute-start(f32[256,128]{0,1:T(8,128)S(1)} %get-tuple-element.6), channel_id=1, source_target_pairs={{0,24},{1,25},{2,26},{3,27},{4,28},{5,29},{6,30},{7,31},{8,16},{9,... | collective-permute-start | bytes 393224 | tf_op jit(solution)/shard_map/ppermute | solution.py:32
  28.4 6.1 %collective-permute-start.9 = (f32[256,128]{0,1:T(8,128)S(1)}, f32[256,128]{0,1:T(8,128)S(1)}, u32[]{:S(2)}, u32[]{:S(2)}) collective-permute-start(f32[256,128]{0,1:T(8,128)S(1)} %get-tuple-element.5), channel_id=1, source_target_pairs={{16,18},{17,19},{18,16},{19,17},{20,22},{21,23},{22,20},{23,21},{2... | collective-permute-start | bytes 393224 | tf_op jit(solution)/shard_map/ppermute | solution.py:32
  29.1 6.1 %collective-permute-start.10 = (f32[256,128]{0,1:T(8,128)S(1)}, f32[256,128]{0,1:T(8,128)S(1)}, u32[]{:S(2)}, u32[]{:S(2)}) collective-permute-start(f32[256,128]{0,1:T(8,128)S(1)} %get-tuple-element.5), channel_id=1, source_target_pairs={{16,20},{17,21},{18,22},{19,23},{20,16},{21,17},{22,18},{23,19},{2... | collective-permute-start | bytes 393224 | tf_op jit(solution)/shard_map/ppermute | solution.py:32
  29.8 9.6 %collective-permute-start.17 = (f32[64,256]{1,0:T(8,128)S(1)}, f32[64,256]{1,0:T(8,128)S(1)}, u32[]{:S(2)}, u32[]{:S(2)}) collective-permute-start(f32[64,256]{1,0:T(8,128)S(1)} %bitcast.37), channel_id=1, source_target_pairs={{0,8},{1,9},{2,10},{3,11},{4,12},{5,13},{6,14},{7,15},{8,0},{9,1},... | collective-permute-start | bytes 196616 | tf_op jit(solution)/shard_map/ppermute | solution.py:32
  33.2 2.8 %collective-permute-start.11 = (f32[256,128]{0,1:T(8,128)S(1)}, f32[256,128]{0,1:T(8,128)S(1)}, u32[]{:S(2)}, u32[]{:S(2)}) collective-permute-start(f32[256,128]{0,1:T(8,128)S(1)} %get-tuple-element.5), channel_id=1, source_target_pairs={{16,22},{17,23},{18,20},{19,21},{20,18},{21,19},{22,16},{23,17},{2... | collective-permute-start | bytes 393224 | tf_op jit(solution)/shard_map/ppermute | solution.py:32
  33.8 2.8 %collective-permute-start.12 = (f32[256,128]{0,1:T(8,128)S(1)}, f32[256,128]{0,1:T(8,128)S(1)}, u32[]{:S(2)}, u32[]{:S(2)}) collective-permute-start(f32[256,128]{0,1:T(8,128)S(1)} %get-tuple-element.5), channel_id=1, source_target_pairs={{16,17},{17,16},{18,19},{19,18},{20,21},{21,20},{22,23},{23,22},{2... | collective-permute-start | bytes 393224 | tf_op jit(solution)/shard_map/ppermute | solution.py:32
  34.5 2.2 %collective-permute-start.13 = (f32[256,128]{0,1:T(8,128)S(1)}, f32[256,128]{0,1:T(8,128)S(1)}, u32[]{:S(2)}, u32[]{:S(2)}) collective-permute-start(f32[256,128]{0,1:T(8,128)S(1)} %collective-permute-done.9), channel_id=1, source_target_pairs={{16,17},{17,16},{18,19},{19,18},{20,21},{21,20},{22,23},{23,22},{2... | collective-permute-start | bytes 393224 | tf_op jit(solution)/shard_map/ppermute | solution.py:32
  35.2 1.5 %collective-permute-start.14 = (f32[256,128]{0,1:T(8,128)S(1)}, f32[256,128]{0,1:T(8,128)S(1)}, u32[]{:S(2)}, u32[]{:S(2)}) collective-permute-start(f32[256,128]{0,1:T(8,128)S(1)} %collective-permute-done.10), channel_id=1, source_target_pairs={{16,17},{17,16},{18,19},{19,18},{20,21},{21,20},{22,23},{23,22},{2... | collective-permute-start | bytes 393224 | tf_op jit(solution)/shard_map/ppermute | solution.py:32
  35.9 0.8 %collective-permute-start.15 = (f32[256,128]{0,1:T(8,128)S(1)}, f32[256,128]{0,1:T(8,128)S(1)}, u32[]{:S(2)}, u32[]{:S(2)}) collective-permute-start(f32[256,128]{0,1:T(8,128)S(1)} %collective-permute-done.11), channel_id=1, source_target_pairs={{16,17},{17,16},{18,19},{19,18},{20,21},{21,20},{22,23},{23,22},{2... | collective-permute-start | bytes 393224 | tf_op jit(solution)/shard_map/ppermute | solution.py:32
  36.7 38.1 %copy-start.3 = (f32[64,128]{1,0:T(8,128)S(1)}, f32[64,128]{1,0:T(8,128)}, u32[]{:S(2)}) copy-start(f32[64,128]{1,0:T(8,128)} %param.11) | copy-start | bytes 98308
  39.6 1.3 %collective-permute-start.18 = (f32[64,128]{1,0:T(8,128)S(1)}, f32[64,128]{1,0:T(8,128)S(1)}, u32[]{:S(2)}, u32[]{:S(2)}) collective-permute-start(f32[64,128]{1,0:T(8,128)S(1)} %fusion.7), channel_id=1, source_target_pairs={{0,1},{1,0},{2,3},{3,2},{4,5},{5,4},{6,7},{7,6},{8,9},{9,8},{10,11... | collective-permute-start | bytes 98312 | tf_op jit(solution)/shard_map/ppermute | solution.py:32
  40.8 5.4 %collective-permute-start.19 = (f32[64,128]{1,0:T(8,128)S(1)}, f32[64,128]{1,0:T(8,128)S(1)}, u32[]{:S(2)}, u32[]{:S(2)}) collective-permute-start(f32[64,128]{1,0:T(8,128)S(1)} %add.92), channel_id=1, source_target_pairs={{0,2},{1,3},{2,0},{3,1},{4,6},{5,7},{6,4},{7,5},{8,10},{9,11},{10,... | collective-permute-start | bytes 98312 | tf_op jit(solution)/shard_map/ppermute | solution.py:32
  42.3 3.9 %collective-permute-start.20 = (f32[64,128]{1,0:T(8,128)S(1)}, f32[64,128]{1,0:T(8,128)S(1)}, u32[]{:S(2)}, u32[]{:S(2)}) collective-permute-start(f32[64,128]{1,0:T(8,128)S(1)} %add.92), channel_id=1, source_target_pairs={{0,4},{1,5},{2,6},{3,7},{4,0},{5,1},{6,2},{7,3},{8,12},{9,13},{10,... | collective-permute-start | bytes 98312 | tf_op jit(solution)/shard_map/ppermute | solution.py:32
  43.3 4.8 %collective-permute-start.21 = (f32[64,128]{1,0:T(8,128)S(1)}, f32[64,128]{1,0:T(8,128)S(1)}, u32[]{:S(2)}, u32[]{:S(2)}) collective-permute-start(f32[64,128]{1,0:T(8,128)S(1)} %add.92), channel_id=1, source_target_pairs={{0,6},{1,7},{2,4},{3,5},{4,2},{5,3},{6,0},{7,1},{8,14},{9,15},{10,... | collective-permute-start | bytes 98312 | tf_op jit(solution)/shard_map/ppermute | solution.py:32
  44.4 28.5 %collective-permute-start.16 = (f32[256,128]{0,1:T(8,128)S(1)}, f32[256,128]{0,1:T(8,128)S(1)}, u32[]{:S(2)}, u32[]{:S(2)}) collective-permute-start(f32[256,128]{0,1:T(8,128)S(1)} %dynamic-slice_bitcast_fusion.2), channel_id=1, source_target_pairs={{0,8},{1,9},{2,10},{3,11},{4,12},{5,13},{6,14},{7,15},{8,0},{9,1},... | collective-permute-start | bytes 393224 | tf_op jit(solution)/shard_map/ppermute | solution.py:32
  48.1 6.2 %collective-permute-start.22 = (f32[64,128]{1,0:T(8,128)S(1)}, f32[64,128]{1,0:T(8,128)S(1)}, u32[]{:S(2)}, u32[]{:S(2)}) collective-permute-start(f32[64,128]{1,0:T(8,128)S(1)} %add_add_fusion), channel_id=1, source_target_pairs={{0,8},{1,9},{2,10},{3,11},{4,12},{5,13},{6,14},{7,15},{8,0},{9,1},... | collective-permute-start | bytes 98312 | tf_op jit(solution)/shard_map/ppermute | solution.py:32
  54.3 20.5 %collective-permute-start.23 = (f32[64,128]{1,0:T(8,128)S(1)}, f32[64,128]{1,0:T(8,128)S(1)}, u32[]{:S(2)}, u32[]{:S(2)}) collective-permute-start(f32[64,128]{1,0:T(8,128)S(1)} %add.96), channel_id=1, source_target_pairs={{0,16},{1,17},{2,18},{3,19},{4,20},{5,21},{6,22},{7,23},{8,24},{9,... | collective-permute-start | bytes 98312 | tf_op jit(solution)/shard_map/ppermute | solution.py:75

commit v2 on v1

v2 whole, which is shorter than its diff:
```python
import functools

import jax
import jax.numpy as jnp
from jax import lax
from jax.experimental import pallas as pl
from jax.experimental.pallas import tpu as pltpu
from jax.sharding import PartitionSpec as P

GROUP = 8
AXES = ("tm", "blk")
HIGH = lax.Precision.HIGH
VMEM_LIMIT = 16 << 20


def dot(a, b):
    return jnp.dot(a, b, precision=HIGH, preferred_element_type=jnp.float32)


def tie(*values):
    return lax.optimization_barrier(values)


def split(value):
    upper = value.astype(jnp.bfloat16)
    lower = (value - upper.astype(jnp.float32)).astype(jnp.bfloat16)
    return upper, lower


def split_tile_kernel(piece, where, tile, upper, lower, mark, staged, arrived):
    rows, cols = tile.shape
    grid = [(e, j) for j in range(cols // piece) for e in range(rows // piece)]

    def copy(e, j):
        source_row = pl.multiple_of((where[1] ^ e) * piece, piece)
        source_col = pl.multiple_of((where[0] ^ j) * piece, piece)
        return pltpu.make_async_copy(
            tile.at[pl.ds(source_row, piece), pl.ds(source_col, piece)],
            staged.at[pl.ds(e * piece, piece), pl.ds(j * piece, piece)],
            arrived.at[e, j],
        )

    for e, j in grid:
        copy(e, j).start()
    for e, j in grid:
        copy(e, j).wait()
        at = (pl.ds(e * piece, piece), pl.ds(j * piece, piece))
        upper[at], lower[at] = split(staged[at])
    mark[...] = jnp.zeros(mark.shape, jnp.float32)


def split_tile(tile, where, piece):
    rows, cols = tile.shape
    half = jax.ShapeDtypeStruct(tile.shape, jnp.bfloat16)
    in_vmem = pl.BlockSpec(memory_space=pltpu.VMEM)
    return pl.pallas_call(
        functools.partial(split_tile_kernel, piece),
        out_shape=[half, half, jax.ShapeDtypeStruct((8, 128), jnp.float32)],
        in_specs=[pl.BlockSpec(memory_space=pltpu.SMEM), pl.BlockSpec(memory_space=pltpu.HBM)],
        out_specs=[in_vmem] * 3,
        scratch_shapes=[
            pltpu.VMEM(tile.shape, jnp.float32),
            pltpu.SemaphoreType.DMA((rows // piece, cols // piece)),
        ],
        cost_estimate=pl.CostEstimate(flops=8 * rows * cols, bytes_accessed=8 * rows * cols, transcendentals=0),
        compiler_params=pltpu.CompilerParams(vmem_limit_bytes=VMEM_LIMIT),
    )(where, pltpu.with_memory_space_constraint(tile, pltpu.HBM))


def product_kernel(count, sign, upper, lower, _, *refs):
    parts, rest = refs[:count], refs[count:]
    columns = rest[-1]
    outs = rest[:-1]
    high_count = len(outs) if sign > 0 else len(outs) // 2
    bases = outs[: len(outs) - high_count]
    outs = outs[len(outs) - high_count :]
    piece, width = parts[0].shape
    for j, part in enumerate(parts):
        at = pl.ds(j * piece, piece)
        columns[at, :width], columns[at, width:] = split(part[...])
    both = jnp.dot(upper[...], columns[...], preferred_element_type=jnp.float32)
    total = both[:, :width] + both[:, width:]
    total = total + jnp.dot(lower[...], columns[:, :width], preferred_element_type=jnp.float32)
    for e, out in enumerate(outs):
        block = total[e * piece : (e + 1) * piece]
        out[...] = block if sign > 0 else bases[e][...] - block


def tile_product(halves, parts, bases=None):
    rows, cols = halves[0].shape
    piece, width = parts[0].shape
    high_count = rows // piece
    block = jax.ShapeDtypeStruct((piece, width), jnp.float32)
    in_vmem = pl.BlockSpec(memory_space=pltpu.VMEM)
    operands = [*halves, *parts, *(bases or [])]
    return pl.pallas_call(
        functools.partial(product_kernel, len(parts), 1 if bases is None else -1),
        out_shape=[block] * high_count,
        in_specs=[in_vmem] * len(operands),
        out_specs=[in_vmem] * high_count,
        scratch_shapes=[pltpu.VMEM((cols, 2 * width), jnp.bfloat16)],
        cost_estimate=pl.CostEstimate(
            flops=6 * rows * cols * width, bytes_accessed=4 * rows * cols, transcendentals=0
        ),
        compiler_params=pltpu.CompilerParams(vmem_limit_bytes=VMEM_LIMIT),
    )(*operands)


def rows_kernel(count, *refs):
    rows, (upper, lower), outs = refs[:count], refs[count : count + 2], refs[count + 2 :]
    piece = rows[0].shape[1]
    for j, out in enumerate(outs):
        total = jnp.zeros(out.shape, jnp.float32)
        for e in range(count):
            row_upper, row_lower = split(rows[e][...])
            at = (pl.ds(e * piece, piece), pl.ds(j * piece, piece))
            total += jnp.dot(row_upper, upper[at], preferred_element_type=jnp.float32)
            total += jnp.dot(row_lower, upper[at], preferred_element_type=jnp.float32)
            total += jnp.dot(row_upper, lower[at], preferred_element_type=jnp.float32)
        out[...] = total


def rows_product(rows, halves):
    count, piece = rows[0].shape
    cols = halves[0].shape[1]
    in_vmem = pl.BlockSpec(memory_space=pltpu.VMEM)
    return pl.pallas_call(
        functools.partial(rows_kernel, len(rows)),
        out_shape=[jax.ShapeDtypeStruct((count, piece), jnp.float32)] * (cols // piece),
        in_specs=[in_vmem] * (len(rows) + 2),
        out_specs=[in_vmem] * (cols // piece),
        cost_estimate=pl.CostEstimate(
            flops=6 * count * len(rows) * piece * cols,
            bytes_accessed=4 * len(rows) * piece * cols,
            transcendentals=0,
        ),
        compiler_params=pltpu.CompilerParams(vmem_limit_bytes=VMEM_LIMIT),
    )(*rows, *halves)


def on_device(propagator, inv_diag, rhs, arrow, tip_inv, tip_rhs):
    steps = lax.axis_size("tm")
    blocks = lax.axis_size("blk")
    high_count = blocks // GROUP
    step = lax.axis_index("tm")
    position = lax.axis_index("blk")
    low = position % GROUP
    high = position // GROUP
    piece = rhs.shape[1]
    width = rhs.shape[2]

    def move(value, flip, ahead=0):
        route = [
            (t * blocks + b, (t + ahead) % steps * blocks + (b ^ flip))
            for t in range(steps)
            for b in range(blocks)
        ]
        return lax.ppermute(value, AXES, route)

    def scatter(own):
        return [move(own, flip) for flip in range(2, GROUP, 2)]

    def swap(own, sent):
        parts = []
        for part in [own, *sent]:
            parts += [part, move(part, 1)]
        return parts

    by_kernel = piece % 256 == 0 and width % 128 == 0
    where = jnp.stack([low, high]).astype(jnp.int32)

    def prepared(tile):
        return list(split_tile(tile, where, piece)) if by_kernel else [tile, tile[:8, :piece]]

    def in_order(tile):
        rows = [
            lax.dynamic_slice_in_dim(tile, (high ^ e) * piece, piece, 0) for e in range(high_count)
        ]
        tile = jnp.concatenate(rows, axis=0)
        cols = [lax.dynamic_slice_in_dim(tile, (low ^ j) * piece, piece, 1) for j in range(GROUP)]
        return jnp.concatenate(cols, axis=1)

    def apply_tile(tile, parts, bases=None):
        if by_kernel:
            return tile_product(tile, parts, bases)
        total = dot(in_order(tile[0]), jnp.concatenate(parts, axis=0))
        found = [total[e * piece : (e + 1) * piece] for e in range(high_count)]
        return found if bases is None else [b - f for b, f in zip(bases, found)]

    def row_product(rows, tile):
        if by_kernel:
            return rows_product(rows, tile[:2])
        total = dot(jnp.concatenate(rows, axis=1), in_order(tile[0]))
        return [total[:, j * piece : (j + 1) * piece] for j in range(GROUP)]

    def own_columns(found):
        odd = jnp.concatenate(found[1::2], axis=0)
        odd = move(odd, 1)
        count = found[0].shape[0]
        even = [found[j] + odd[j // 2 * count : (j // 2 + 1) * count] for j in range(0, GROUP, 2)]
        return even[0] + sum(move(even[k], 2 * k) for k in range(1, GROUP // 2))

    sent = scatter(rhs[0])
    arrows = [arrow[0]] + [move(arrow[0], e * GROUP) for e in range(1, high_count)]
    apply_g = prepared(inv_diag[0])
    sent[0], apply_g[-1], *arrows[1:] = tie(sent[0], apply_g[-1], *arrows[1:])
    partial = apply_tile(apply_g, swap(rhs[0], sent))
    for t in range(steps - 1):
        arriving = [move(partial[e], e * GROUP, 1) for e in range(high_count)]
        if t == 0:
            apply_m = prepared(propagator[0])
            arriving[0], apply_m[-1] = tie(arriving[0], apply_m[-1])
        earlier = jnp.where(step == t + 1, sum(arriving), 0.0)
        partial = apply_tile(apply_m, swap(earlier, scatter(earlier)), partial)

    others = [move(partial[e], e * GROUP) for e in range(1, high_count)]
    terms = sum(dot(arrows[e], partial[e]) for e in range(high_count))
    terms = terms + move(terms, 1)
    terms = terms + sum(move(terms, flip) for flip in range(2, GROUP, 2))
    if steps == 2 and high_count == 2:
        terms = terms + move(terms, GROUP) + move(terms, 0, 1) + move(terms, GROUP, 1)
    else:
        for e in range(high_count.bit_length() - 1):
            terms = terms + move(terms, GROUP << e)
        terms = sum(move(terms, 0, ahead) for ahead in range(steps))
    solved = partial[0] + sum(others)
    tip = dot(tip_inv, tip_rhs - terms)
    return solved[None], tip


def solution(mesh):
    placed = (
        P("tm", "blk", None),
        P("tm", "blk", None),
        P("tm", "blk", None),
        P("tm", None, "blk"),
        P(),
        P(),
    )
    return jax.shard_map(
        on_device,
        mesh=mesh,
        in_specs=placed,
        out_specs=(P("tm", "blk", None), P()),
        check_vma=False,
    )
```

time: 75.9 us -> 61.9 us (0.82)
  starting transfers between devices: 47.7 us -> 29.3 us
  Pallas kernels: 0 us -> 8.62 us
  matrix products: 8.03 us -> 1.11 us
  waiting for transfers between devices: 15.6 us -> 21.2 us
  local copies, waits for them, and re-layouts: 2.97 us -> 0.02 us
    ppermute x1 -> x0, starting transfers between devices: 18.6 us -> none  [on_device(): terms = terms + lax.ppermute(terms, AXES, ring)]
    pallas_call x0 -> x4, Pallas kernels: none -> 8.62 us  [the longest x2 5.8 us: split_tile(): pl.pallas_call(functools.partial(split_tile_kernel, piece), out_shape=[ha...]
    dot_general x5 -> x3, matrix products: 8.03 us -> 1.11 us  [dot(): return jnp.dot(a, b, precision=HIGH, preferred_element_type=jnp.float32)]
    ppermute x23 -> x25, waiting for transfers between devices: 14.5 us -> 21.2 us  [move(): return lax.ppermute(value, AXES, route)]
    ppermute x1 -> x0, waiting for transfers between devices: 1.11 us -> none  [on_device(): terms = terms + lax.ppermute(terms, AXES, ring)]
    squeeze x1 -> x0, local copies, waits for them, and re-layouts: 1.06 us -> none  [on_device(): partial = apply_tile(inv_diag[0], gather(rhs[0]))]
    unnamed x9 -> x8, local copies, waits for them, and re-layouts: 0.78 us -> 0.02 us
    ppermute x23 -> x25, starting transfers between devices: 29.1 us -> 29.3 us  [move(): return lax.ppermute(value, AXES, route)]
  transfers between devices with their start and end apart: 24 -> 25, of which waited for: 10 -> 16; matrix products, arithmetic and copies ran while one was open for 7% -> 1% of each run, Pallas kernels for 0% -> 9%
where the time goes in v2:
time: 61.9 us; the launch traced here: 61.7 us
  starting transfers between devices  29.3 us (47%)
  waiting for transfers between devices  21.2 us (34%)
  Pallas kernels  8.62 us (14%)
  matrix products  1.11 us (2%)
  other arithmetic  0.78 us (1%)
  between operations  0.74 us (1%)
    ppermute x25, starting transfers between devices, move(): return lax.ppermute(value, AXES, route)  29.3 us
    ppermute x25, waiting for transfers between devices, move(): return lax.ppermute(value, AXES, route)  21.2 us
    pallas_call x2, Pallas kernels, split_tile(): pl.pallas_call(functools.partial(split_tile_kernel, piece), out_shape=[ha...  5.8 us
    pallas_call x2, Pallas kernels, tile_product(): pl.pallas_call(functools.partial(product_kernel, len(parts), 1 if bases i...  2.83 us
  transfers between devices with their start and end apart: 25, of which 16 were waited for; matrix products, arithmetic and copies ran while one was open for 1% of the time, Pallas kernels for 9%

profile of v2, /device:TPU:0, one launch (start us, length us, event | category | flops | bytes accessed | tf_op | source)
XLA Modules:
  0.0 61.7 jit_solution(14024845052672289438)
XLA Ops:
  0.6 0.0 copy-start
  0.6 3.0 %collective-permute-start = (f32[256,128]{1,0:T(8,128)}, f32[256,128]{1,0:T(8,128)S(1)}, u32[]{:S(2)}, u32[]{:S(2)}) collective-permute-start(f32[256,128]{1,0:T(8,128)} %bitcast.20), channel_id=1, source_target_pairs={{0,2},{1,3},{2,0},{3,1},{4,6},{5,7},{6,4},{7,5},{8,10},{9,11},{10,... | collective-permute-start | bytes 393224 | tf_op jit(solution)/shard_map/ppermute | solution.py:158
  3.6 1.6 %collective-permute-start.4 = (f32[256,128]{1,0:T(8,128)}, f32[256,128]{1,0:T(8,128)S(1)}, u32[]{:S(2)}, u32[]{:S(2)}) collective-permute-start(f32[256,128]{1,0:T(8,128)} %bitcast.21), channel_id=1, source_target_pairs={{0,4},{1,5},{2,6},{3,7},{4,0},{5,1},{6,2},{7,3},{8,12},{9,13},{10,... | collective-permute-start | bytes 393224 | tf_op jit(solution)/shard_map/ppermute | solution.py:158
  5.2 0.0 collective-permute-start.6
  5.2 0.0 collective-permute-start.2
  5.2 3.0 %collective-permute-start.1 = (f32[64,256]{1,0:T(8,128)}, f32[64,256]{1,0:T(8,128)S(1)}, u32[]{:S(2)}, u32[]{:S(2)}) collective-permute-start(f32[64,256]{1,0:T(8,128)} %bitcast.27), channel_id=1, source_target_pairs={{0,8},{1,9},{2,10},{3,11},{4,12},{5,13},{6,14},{7,15},{8,0},{9,1},... | collective-permute-start | bytes 196616 | tf_op jit(solution)/shard_map/ppermute | solution.py:158
  8.2 0.1 pad_add_fusion.where
  8.3 2.9 %shard_map.78 = (bf16[512,2048]{1,0:T(8,128)(2,1)S(1)}, bf16[512,2048]{1,0:T(8,128)(2,1)S(1)}, f32[8,128]{1,0:T(8,128)S(1)}) custom-call(s32[2]{0:T(128)S(1)} %pad_add_fusion.where, f32[512,2048]{1,0:T(8,128)} %bitcast.25), custom_call_target="tpu_custom_call" | custom-call | flops 8388608 | bytes 8388608 | tf_op jit(solution)/shard_map/pallas_call | solution.py:56
  11.2 1.0 %collective-permute-done.1 = f32[64,256]{1,0:T(8,128)S(1)} collective-permute-done((f32[64,256]{1,0:T(8,128)}, f32[64,256]{1,0:T(8,128)S(1)}, u32[]{:S(2)}, u32[]{:S(2)}) %collective-permute-start.1) | collective-permute-done | bytes 65568 | tf_op jit(solution)/shard_map/ppermute | solution.py:158
  12.2 0.0 collective-permute-done.refs_2_
  12.2 0.0 collective-permute-start.3
  12.2 0.0 collective-permute-done.4.refs_4_
  12.2 0.5 collective-permute-start.5
  12.7 0.1 collective-permute-done.6.refs_6_
  12.9 0.0 collective-permute-start.7
  12.9 0.0 collective-permute-done.2.refs_1_
  12.9 0.7 %collective-permute-done.3.refs_3_ = f32[256,128]{1,0:T(8,128)S(1)} collective-permute-done((f32[256,128]{1,0:T(8,128)S(1)}, f32[256,128]{1,0:T(8,128)S(1)}, u32[]{:S(2)}, u32[]{:S(2)}) %collective-permute-start.3) | collective-permute-done | bytes 131104 | tf_op jit(solution)/shard_map/ppermute | solution.py:158
  13.6 0.2 collective-permute-done.5.refs_5_
  13.8 0.4 collective-permute-done.7.refs_7_
  14.2 0.0 copy-done.1
  14.2 1.4 %shard_map.79 = (f32[256,128]{1,0:T(8,128)S(1)}, f32[256,128]{1,0:T(8,128)S(1)}) custom-call(bf16[512,2048]{1,0:T(8,128)(2,1)S(1)} %get-tuple-element.19.upper, bf16[512,2048]{1,0:T(8,128)(2,1)S(1)} %get-tuple-element.20.lower, f32[8,128]{1,0:T(8,128)S(1)} %get-tuple-element.22._, f32[256,128]{1,0:T(8,128)S(1)} %bitcast.24, ...), custom_call_target="tpu_custom_call" | custom-call | flops 805306368 | bytes 4194304 | tf_op jit(solution)/shard_map/pallas_call | solution.py:96
  15.6 1.7 %collective-permute-start.8 = (f32[256,128]{1,0:T(8,128)S(1)}, f32[256,128]{1,0:T(8,128)S(1)}, u32[]{:S(2)}, u32[]{:S(2)}) collective-permute-start(f32[256,128]{1,0:T(8,128)S(1)} %get-tuple-element.24.refs_8_), channel_id=1, source_target_pairs={{0,16},{1,17},{2,18},{3,19},{4,20},{5,21},{6,22},{7,23},{8,24},{9,... | collective-permute-start | bytes 393224 | tf_op jit(solution)/shard_map/ppermute | solution.py:158
  17.4 3.0 %collective-permute-start.9 = (f32[256,128]{1,0:T(8,128)S(1)}, f32[256,128]{1,0:T(8,128)S(1)}, u32[]{:S(2)}, u32[]{:S(2)}) collective-permute-start(f32[256,128]{1,0:T(8,128)S(1)} %get-tuple-element.28.refs_9_), channel_id=1, source_target_pairs={{0,24},{1,25},{2,26},{3,27},{4,28},{5,29},{6,30},{7,31},{8,16},{9,... | collective-permute-start | bytes 393224 | tf_op jit(solution)/shard_map/ppermute | solution.py:158
  20.3 2.9 %shard_map.77 = (bf16[512,2048]{1,0:T(8,128)(2,1)S(1)}, bf16[512,2048]{1,0:T(8,128)(2,1)S(1)}, f32[8,128]{1,0:T(8,128)S(1)}) custom-call(s32[2]{0:T(128)S(1)} %pad_add_fusion.where, f32[512,2048]{1,0:T(8,128)} %bitcast.26), custom_call_target="tpu_custom_call" | custom-call | flops 8388608 | bytes 8388608 | tf_op jit(solution)/shard_map/pallas_call | solution.py:56
  23.2 0.0 collective-permute-done.8
  23.2 4.0 %collective-permute-done.9 = f32[256,128]{1,0:T(8,128)S(1)} collective-permute-done((f32[256,128]{1,0:T(8,128)S(1)}, f32[256,128]{1,0:T(8,128)S(1)}, u32[]{:S(2)}, u32[]{:S(2)}) %collective-permute-start.9) | collective-permute-done | bytes 131104 | tf_op jit(solution)/shard_map/ppermute | solution.py:158
  27.3 1.5 %collective-permute-start.11 = (f32[256,128]{1,0:T(8,128)S(1)}, f32[256,128]{1,0:T(8,128)S(1)}, u32[]{:S(2)}, u32[]{:S(2)}) collective-permute-start(f32[256,128]{1,0:T(8,128)S(1)} %add_select_fusion.refs_0_), channel_id=1, source_target_pairs={{0,2},{1,3},{2,0},{3,1},{4,6},{5,7},{6,4},{7,5},{8,10},{9,11},{10,... | collective-permute-start | bytes 393224 | tf_op jit(solution)/shard_map/ppermute | solution.py:158
  28.8 0.0 collective-permute-start.13
  28.8 2.0 %collective-permute-start.15 = (f32[256,128]{1,0:T(8,128)S(1)}, f32[256,128]{1,0:T(8,128)S(1)}, u32[]{:S(2)}, u32[]{:S(2)}) collective-permute-start(f32[256,128]{1,0:T(8,128)S(1)} %add_select_fusion.refs_0_), channel_id=1, source_target_pairs={{0,6},{1,7},{2,4},{3,5},{4,2},{5,3},{6,0},{7,1},{8,14},{9,15},{10,... | collective-permute-start | bytes 393224 | tf_op jit(solution)/shard_map/ppermute | solution.py:158
  30.8 0.0 collective-permute-start.10
  30.8 2.9 %collective-permute-done.11.refs_2_ = f32[256,128]{1,0:T(8,128)S(1)} collective-permute-done((f32[256,128]{1,0:T(8,128)S(1)}, f32[256,128]{1,0:T(8,128)S(1)}, u32[]{:S(2)}, u32[]{:S(2)}) %collective-permute-start.11) | collective-permute-done | bytes 131104 | tf_op jit(solution)/shard_map/ppermute | solution.py:158
  33.7 0.0 collective-permute-start.12
  33.7 0.1 collective-permute-done.13.refs_4_
  33.8 0.4 collective-permute-start.14
  34.2 1.1 %collective-permute-done.15.refs_6_ = f32[256,128]{1,0:T(8,128)S(1)} collective-permute-done((f32[256,128]{1,0:T(8,128)S(1)}, f32[256,128]{1,0:T(8,128)S(1)}, u32[]{:S(2)}, u32[]{:S(2)}) %collective-permute-start.15) | collective-permute-done | bytes 131104 | tf_op jit(solution)/shard_map/ppermute | solution.py:158
  35.3 0.0 collective-permute-start.16
  35.4 0.0 collective-permute-done.10.refs_1_
  35.4 0.0 collective-permute-done.12.refs_3_
  35.4 0.0 collective-permute-done.14.refs_5_
  35.4 1.3 %collective-permute-done.16.refs_7_ = f32[256,128]{1,0:T(8,128)S(1)} collective-permute-done((f32[256,128]{1,0:T(8,128)S(1)}, f32[256,128]{1,0:T(8,128)S(1)}, u32[]{:S(2)}, u32[]{:S(2)}) %collective-permute-start.16) | collective-permute-done | bytes 131104 | tf_op jit(solution)/shard_map/ppermute | solution.py:158
  36.7 1.4 %shard_map.80 = (f32[256,128]{1,0:T(8,128)S(1)}, f32[256,128]{1,0:T(8,128)S(1)}) custom-call(bf16[512,2048]{1,0:T(8,128)(2,1)S(1)} %get-tuple-element.17.upper, bf16[512,2048]{1,0:T(8,128)(2,1)S(1)} %get-tuple-element.18.lower, f32[8,128]{1,0:T(8,128)S(1)} %get-tuple-element.26._, f32[256,128]{1,0:T(8,128)S(1)} %add_select_fusion.refs_0_, ...), custom_call_target="tpu_custom_call" | custom-call | flops 805306368 | bytes 4194304 | tf_op jit(solution)/shard_map/pallas_call | solution.py:96
  38.1 0.2 fusion.6
  38.3 0.0 copy-done.2
  38.3 0.2 fusion
  38.5 0.2 collective-permute-start.18
  38.7 1.1 %collective-permute-done.18 = f32[64,128]{1,0:T(8,128)S(1)} collective-permute-done((f32[64,128]{1,0:T(8,128)S(1)}, f32[64,128]{1,0:T(8,128)S(1)}, u32[]{:S(2)}, u32[]{:S(2)}) %collective-permute-start.18) | collective-permute-done | bytes 32800 | tf_op jit(solution)/shard_map/ppermute | solution.py:158
  39.8 1.3 %collective-permute-start.19 = (f32[64,128]{1,0:T(8,128)S(1)}, f32[64,128]{1,0:T(8,128)S(1)}, u32[]{:S(2)}, u32[]{:S(2)}) collective-permute-start(f32[64,128]{1,0:T(8,128)S(1)} %add.39), channel_id=1, source_target_pairs={{0,2},{1,3},{2,0},{3,1},{4,6},{5,7},{6,4},{7,5},{8,10},{9,11},{10,... | collective-permute-start | bytes 98312 | tf_op jit(solution)/shard_map/ppermute | solution.py:158
  41.1 0.9 %collective-permute-start.20 = (f32[64,128]{1,0:T(8,128)S(1)}, f32[64,128]{1,0:T(8,128)S(1)}, u32[]{:S(2)}, u32[]{:S(2)}) collective-permute-start(f32[64,128]{1,0:T(8,128)S(1)} %add.39), channel_id=1, source_target_pairs={{0,4},{1,5},{2,6},{3,7},{4,0},{5,1},{6,2},{7,3},{8,12},{9,13},{10,... | collective-permute-start | bytes 98312 | tf_op jit(solution)/shard_map/ppermute | solution.py:158
  42.0 1.3 %collective-permute-start.21 = (f32[64,128]{1,0:T(8,128)S(1)}, f32[64,128]{1,0:T(8,128)S(1)}, u32[]{:S(2)}, u32[]{:S(2)}) collective-permute-start(f32[64,128]{1,0:T(8,128)S(1)} %add.39), channel_id=1, source_target_pairs={{0,6},{1,7},{2,4},{3,5},{4,2},{5,3},{6,0},{7,1},{8,14},{9,15},{10,... | collective-permute-start | bytes 98312 | tf_op jit(solution)/shard_map/ppermute | solution.py:158
  43.3 0.4 collective-permute-done.19
  43.7 1.5 %collective-permute-done.20 = f32[64,128]{1,0:T(8,128)S(1)} collective-permute-done((f32[64,128]{1,0:T(8,128)S(1)}, f32[64,128]{1,0:T(8,128)S(1)}, u32[]{:S(2)}, u32[]{:S(2)}) %collective-permute-start.20) | collective-permute-done | bytes 32800 | tf_op jit(solution)/shard_map/ppermute | solution.py:158
  45.2 1.6 %collective-permute-done.21 = f32[64,128]{1,0:T(8,128)S(1)} collective-permute-done((f32[64,128]{1,0:T(8,128)S(1)}, f32[64,128]{1,0:T(8,128)S(1)}, u32[]{:S(2)}, u32[]{:S(2)}) %collective-permute-start.21) | collective-permute-done | bytes 32800 | tf_op jit(solution)/shard_map/ppermute | solution.py:158
  46.8 4.4 %collective-permute-start.22 = (f32[64,128]{1,0:T(8,128)S(1)}, f32[64,128]{1,0:T(8,128)S(1)}, u32[]{:S(2)}, u32[]{:S(2)}) collective-permute-start(f32[64,128]{1,0:T(8,128)S(1)} %add_add_fusion), channel_id=1, source_target_pairs={{0,8},{1,9},{2,10},{3,11},{4,12},{5,13},{6,14},{7,15},{8,0},{9,1},... | collective-permute-start | bytes 98312 | tf_op jit(solution)/shard_map/ppermute | solution.py:158
  51.2 0.5 collective-permute-start.23
  51.7 1.0 %collective-permute-start.24 = (f32[64,128]{1,0:T(8,128)S(1)}, f32[64,128]{1,0:T(8,128)S(1)}, u32[]{:S(2)}, u32[]{:S(2)}) collective-permute-start(f32[64,128]{1,0:T(8,128)S(1)} %add_add_fusion), channel_id=1, source_target_pairs={{0,24},{1,25},{2,26},{3,27},{4,28},{5,29},{6,30},{7,31},{8,16},{9,... | collective-permute-start | bytes 98312 | tf_op jit(solution)/shard_map/ppermute | solution.py:158
  52.7 2.8 %collective-permute-start.17 = (f32[256,128]{1,0:T(8,128)S(1)}, f32[256,128]{1,0:T(8,128)S(1)}, u32[]{:S(2)}, u32[]{:S(2)}) collective-permute-start(f32[256,128]{1,0:T(8,128)S(1)} %get-tuple-element.30), channel_id=1, source_target_pairs={{0,8},{1,9},{2,10},{3,11},{4,12},{5,13},{6,14},{7,15},{8,0},{9,1},... | collective-permute-start | bytes 393224 | tf_op jit(solution)/shard_map/ppermute | solution.py:158
  55.6 0.0 collective-permute-done.22
  55.6 0.0 collective-permute-done.23
  55.6 3.8 %collective-permute-done.24 = f32[64,128]{1,0:T(8,128)S(1)} collective-permute-done((f32[64,128]{1,0:T(8,128)S(1)}, f32[64,128]{1,0:T(8,128)S(1)}, u32[]{:S(2)}, u32[]{:S(2)}) %collective-permute-start.24) | collective-permute-done | bytes 32800 | tf_op jit(solution)/shard_map/ppermute | solution.py:158
  59.4 0.0 copy-done
  59.4 0.0 copy-done.3
  59.4 0.8 %convolution_bitcast_fusion = f32[64,128]{1,0:T(8,128)} fusion(f32[64,64]{1,0:T(8,128)S(1)} %copy-done, f32[64,128]{1,0:T(8,128)S(1)} %copy-done.3, f32[64,128]{1,0:T(8,128)S(1)} %collective-permute-done.24, f32[64,128]{1,0:T(8,128)S(1)} %collective-permute-done.23, f32[64,128]{1,0:T(8,128)S(1)} %add_add_fusion, f32[64,128]{1,0:T(8,128)S(1)} %collective-permute-done.22), kind=kOutput, calls=%fused_computation | convolution fusion | flops 3178496 | bytes 212992 | tf_op jit(solution)/shard_map/dot_general | solution.py:17
  60.2 0.9 %collective-permute-done.17 = f32[256,128]{1,0:T(8,128)S(1)} collective-permute-done((f32[256,128]{1,0:T(8,128)S(1)}, f32[256,128]{1,0:T(8,128)S(1)}, u32[]{:S(2)}, u32[]{:S(2)}) %collective-permute-start.17) | collective-permute-done | bytes 131104 | tf_op jit(solution)/shard_map/ppermute | solution.py:158
  61.1 0.7 %add_bitcast_fusion = f32[1,256,128]{2,1,0:T(8,128)} fusion(f32[256,128]{1,0:T(8,128)S(1)} %get-tuple-element.29, f32[256,128]{1,0:T(8,128)S(1)} %collective-permute-done.17), kind=kLoop, calls=%fused_computation.3 | loop fusion | flops 32768 | bytes 393216 | tf_op jit(solution)/shard_map/broadcast_in_dim | solution.py:228
  (6 shorter events, 0.0 us)
Async XLA Ops:
  0.6 58.8 %copy-start = (f32[64,64]{1,0:T(8,128)S(1)}, f32[64,64]{1,0:T(8,128)}, u32[]{:S(2)}) copy-start(f32[64,64]{1,0:T(8,128)} %param.10) | copy-start | bytes 49156
  0.6 11.6 %collective-permute-start = (f32[256,128]{1,0:T(8,128)}, f32[256,128]{1,0:T(8,128)S(1)}, u32[]{:S(2)}, u32[]{:S(2)}) collective-permute-start(f32[256,128]{1,0:T(8,128)} %bitcast.20), channel_id=1, source_target_pairs={{0,2},{1,3},{2,0},{3,1},{4,6},{5,7},{6,4},{7,5},{8,10},{9,11},{10,... | collective-permute-start | bytes 393224 | tf_op jit(solution)/shard_map/ppermute | solution.py:158
  3.6 8.6 %collective-permute-start.4 = (f32[256,128]{1,0:T(8,128)}, f32[256,128]{1,0:T(8,128)S(1)}, u32[]{:S(2)}, u32[]{:S(2)}) collective-permute-start(f32[256,128]{1,0:T(8,128)} %bitcast.21), channel_id=1, source_target_pairs={{0,4},{1,5},{2,6},{3,7},{4,0},{5,1},{6,2},{7,3},{8,12},{9,13},{10,... | collective-permute-start | bytes 393224 | tf_op jit(solution)/shard_map/ppermute | solution.py:158
  5.2 7.6 %collective-permute-start.6 = (f32[256,128]{1,0:T(8,128)}, f32[256,128]{1,0:T(8,128)S(1)}, u32[]{:S(2)}, u32[]{:S(2)}) collective-permute-start(f32[256,128]{1,0:T(8,128)} %bitcast.22), channel_id=1, source_target_pairs={{0,6},{1,7},{2,4},{3,5},{4,2},{5,3},{6,0},{7,1},{8,14},{9,15},{10,... | collective-permute-start | bytes 393224 | tf_op jit(solution)/shard_map/ppermute | solution.py:158
  5.2 7.6 %collective-permute-start.2 = (f32[256,128]{1,0:T(8,128)}, f32[256,128]{1,0:T(8,128)S(1)}, u32[]{:S(2)}, u32[]{:S(2)}) collective-permute-start(f32[256,128]{1,0:T(8,128)} %bitcast.23), channel_id=1, source_target_pairs={{0,1},{1,0},{2,3},{3,2},{4,5},{5,4},{6,7},{7,6},{8,9},{9,8},{10,11... | collective-permute-start | bytes 393224 | tf_op jit(solution)/shard_map/ppermute | solution.py:158
  5.2 7.0 %collective-permute-start.1 = (f32[64,256]{1,0:T(8,128)}, f32[64,256]{1,0:T(8,128)S(1)}, u32[]{:S(2)}, u32[]{:S(2)}) collective-permute-start(f32[64,256]{1,0:T(8,128)} %bitcast.27), channel_id=1, source_target_pairs={{0,8},{1,9},{2,10},{3,11},{4,12},{5,13},{6,14},{7,15},{8,0},{9,1},... | collective-permute-start | bytes 196616 | tf_op jit(solution)/shard_map/ppermute | solution.py:158
  8.3 5.9 %copy-start.1 = (f32[1,256,128]{2,1,0:T(8,128)S(1)}, f32[1,256,128]{2,1,0:T(8,128)}, u32[]{:S(2)}) copy-start(f32[1,256,128]{2,1,0:T(8,128)} %param.8) | copy-start | bytes 393220
  12.2 1.3 %collective-permute-start.3 = (f32[256,128]{1,0:T(8,128)S(1)}, f32[256,128]{1,0:T(8,128)S(1)}, u32[]{:S(2)}, u32[]{:S(2)}) collective-permute-start(f32[256,128]{1,0:T(8,128)S(1)} %collective-permute-done.refs_2_), channel_id=1, source_target_pairs={{0,1},{1,0},{2,3},{3,2},{4,5},{5,4},{6,7},{7,6},{8,9},{9,8},{10,11... | collective-permute-start | bytes 393224 | tf_op jit(solution)/shard_map/ppermute | solution.py:158
  12.2 1.5 %collective-permute-start.5 = (f32[256,128]{1,0:T(8,128)S(1)}, f32[256,128]{1,0:T(8,128)S(1)}, u32[]{:S(2)}, u32[]{:S(2)}) collective-permute-start(f32[256,128]{1,0:T(8,128)S(1)} %collective-permute-done.4.refs_4_), channel_id=1, source_target_pairs={{0,1},{1,0},{2,3},{3,2},{4,5},{5,4},{6,7},{7,6},{8,9},{9,8},{10,11... | collective-permute-start | bytes 393224 | tf_op jit(solution)/shard_map/ppermute | solution.py:158
  12.9 1.3 %collective-permute-start.7 = (f32[256,128]{1,0:T(8,128)S(1)}, f32[256,128]{1,0:T(8,128)S(1)}, u32[]{:S(2)}, u32[]{:S(2)}) collective-permute-start(f32[256,128]{1,0:T(8,128)S(1)} %collective-permute-done.6.refs_6_), channel_id=1, source_target_pairs={{0,1},{1,0},{2,3},{3,2},{4,5},{5,4},{6,7},{7,6},{8,9},{9,8},{10,11... | collective-permute-start | bytes 393224 | tf_op jit(solution)/shard_map/ppermute | solution.py:158
  15.6 7.6 %collective-permute-start.8 = (f32[256,128]{1,0:T(8,128)S(1)}, f32[256,128]{1,0:T(8,128)S(1)}, u32[]{:S(2)}, u32[]{:S(2)}) collective-permute-start(f32[256,128]{1,0:T(8,128)S(1)} %get-tuple-element.24.refs_8_), channel_id=1, source_target_pairs={{0,16},{1,17},{2,18},{3,19},{4,20},{5,21},{6,22},{7,23},{8,24},{9,... | collective-permute-start | bytes 393224 | tf_op jit(solution)/shard_map/ppermute | solution.py:158
  17.4 9.9 %collective-permute-start.9 = (f32[256,128]{1,0:T(8,128)S(1)}, f32[256,128]{1,0:T(8,128)S(1)}, u32[]{:S(2)}, u32[]{:S(2)}) collective-permute-start(f32[256,128]{1,0:T(8,128)S(1)} %get-tuple-element.28.refs_9_), channel_id=1, source_target_pairs={{0,24},{1,25},{2,26},{3,27},{4,28},{5,29},{6,30},{7,31},{8,16},{9,... | collective-permute-start | bytes 393224 | tf_op jit(solution)/shard_map/ppermute | solution.py:158
  27.3 6.4 %collective-permute-start.11 = (f32[256,128]{1,0:T(8,128)S(1)}, f32[256,128]{1,0:T(8,128)S(1)}, u32[]{:S(2)}, u32[]{:S(2)}) collective-permute-start(f32[256,128]{1,0:T(8,128)S(1)} %add_select_fusion.refs_0_), channel_id=1, source_target_pairs={{0,2},{1,3},{2,0},{3,1},{4,6},{5,7},{6,4},{7,5},{8,10},{9,11},{10,... | collective-permute-start | bytes 393224 | tf_op jit(solution)/shard_map/ppermute | solution.py:158
  28.8 5.0 %collective-permute-start.13 = (f32[256,128]{1,0:T(8,128)S(1)}, f32[256,128]{1,0:T(8,128)S(1)}, u32[]{:S(2)}, u32[]{:S(2)}) collective-permute-start(f32[256,128]{1,0:T(8,128)S(1)} %add_select_fusion.refs_0_), channel_id=1, source_target_pairs={{0,4},{1,5},{2,6},{3,7},{4,0},{5,1},{6,2},{7,3},{8,12},{9,13},{10,... | collective-permute-start | bytes 393224 | tf_op jit(solution)/shard_map/ppermute | solution.py:158
  28.8 6.5 %collective-permute-start.15 = (f32[256,128]{1,0:T(8,128)S(1)}, f32[256,128]{1,0:T(8,128)S(1)}, u32[]{:S(2)}, u32[]{:S(2)}) collective-permute-start(f32[256,128]{1,0:T(8,128)S(1)} %add_select_fusion.refs_0_), channel_id=1, source_target_pairs={{0,6},{1,7},{2,4},{3,5},{4,2},{5,3},{6,0},{7,1},{8,14},{9,15},{10,... | collective-permute-start | bytes 393224 | tf_op jit(solution)/shard_map/ppermute | solution.py:158
  30.8 4.5 %collective-permute-start.10 = (f32[256,128]{1,0:T(8,128)S(1)}, f32[256,128]{1,0:T(8,128)S(1)}, u32[]{:S(2)}, u32[]{:S(2)}) collective-permute-start(f32[256,128]{1,0:T(8,128)S(1)} %add_select_fusion.refs_0_), channel_id=1, source_target_pairs={{0,1},{1,0},{2,3},{3,2},{4,5},{5,4},{6,7},{7,6},{8,9},{9,8},{10,11... | collective-permute-start | bytes 393224 | tf_op jit(solution)/shard_map/ppermute | solution.py:158
  33.7 1.7 %collective-permute-start.12 = (f32[256,128]{1,0:T(8,128)S(1)}, f32[256,128]{1,0:T(8,128)S(1)}, u32[]{:S(2)}, u32[]{:S(2)}) collective-permute-start(f32[256,128]{1,0:T(8,128)S(1)} %collective-permute-done.11.refs_2_), channel_id=1, source_target_pairs={{0,1},{1,0},{2,3},{3,2},{4,5},{5,4},{6,7},{7,6},{8,9},{9,8},{10,11... | collective-permute-start | bytes 393224 | tf_op jit(solution)/shard_map/ppermute | solution.py:158
  33.8 1.6 %collective-permute-start.14 = (f32[256,128]{1,0:T(8,128)S(1)}, f32[256,128]{1,0:T(8,128)S(1)}, u32[]{:S(2)}, u32[]{:S(2)}) collective-permute-start(f32[256,128]{1,0:T(8,128)S(1)} %collective-permute-done.13.refs_4_), channel_id=1, source_target_pairs={{0,1},{1,0},{2,3},{3,2},{4,5},{5,4},{6,7},{7,6},{8,9},{9,8},{10,11... | collective-permute-start | bytes 393224 | tf_op jit(solution)/shard_map/ppermute | solution.py:158
  35.3 1.3 %collective-permute-start.16 = (f32[256,128]{1,0:T(8,128)S(1)}, f32[256,128]{1,0:T(8,128)S(1)}, u32[]{:S(2)}, u32[]{:S(2)}) collective-permute-start(f32[256,128]{1,0:T(8,128)S(1)} %collective-permute-done.15.refs_6_), channel_id=1, source_target_pairs={{0,1},{1,0},{2,3},{3,2},{4,5},{5,4},{6,7},{7,6},{8,9},{9,8},{10,11... | collective-permute-start | bytes 393224 | tf_op jit(solution)/shard_map/ppermute | solution.py:158
  36.7 1.6 %copy-start.2 = (f32[1,64,256]{2,1,0:T(8,128)S(1)}, f32[1,64,256]{2,1,0:T(8,128)}, u32[]{:S(2)}) copy-start(f32[1,64,256]{2,1,0:T(8,128)} %param.9) | copy-start | bytes 196612
  36.7 22.7 %copy-start.3 = (f32[64,128]{1,0:T(8,128)S(1)}, f32[64,128]{1,0:T(8,128)}, u32[]{:S(2)}) copy-start(f32[64,128]{1,0:T(8,128)} %param.11) | copy-start | bytes 98308
  38.5 1.3 %collective-permute-start.18 = (f32[64,128]{1,0:T(8,128)S(1)}, f32[64,128]{1,0:T(8,128)S(1)}, u32[]{:S(2)}, u32[]{:S(2)}) collective-permute-start(f32[64,128]{1,0:T(8,128)S(1)} %fusion), channel_id=1, source_target_pairs={{0,1},{1,0},{2,3},{3,2},{4,5},{5,4},{6,7},{7,6},{8,9},{9,8},{10,11... | collective-permute-start | bytes 98312 | tf_op jit(solution)/shard_map/ppermute | solution.py:158
  39.8 3.9 %collective-permute-start.19 = (f32[64,128]{1,0:T(8,128)S(1)}, f32[64,128]{1,0:T(8,128)S(1)}, u32[]{:S(2)}, u32[]{:S(2)}) collective-permute-start(f32[64,128]{1,0:T(8,128)S(1)} %add.39), channel_id=1, source_target_pairs={{0,2},{1,3},{2,0},{3,1},{4,6},{5,7},{6,4},{7,5},{8,10},{9,11},{10,... | collective-permute-start | bytes 98312 | tf_op jit(solution)/shard_map/ppermute | solution.py:158
  41.1 4.1 %collective-permute-start.20 = (f32[64,128]{1,0:T(8,128)S(1)}, f32[64,128]{1,0:T(8,128)S(1)}, u32[]{:S(2)}, u32[]{:S(2)}) collective-permute-start(f32[64,128]{1,0:T(8,128)S(1)} %add.39), channel_id=1, source_target_pairs={{0,4},{1,5},{2,6},{3,7},{4,0},{5,1},{6,2},{7,3},{8,12},{9,13},{10,... | collective-permute-start | bytes 98312 | tf_op jit(solution)/shard_map/ppermute | solution.py:158
  42.0 4.8 %collective-permute-start.21 = (f32[64,128]{1,0:T(8,128)S(1)}, f32[64,128]{1,0:T(8,128)S(1)}, u32[]{:S(2)}, u32[]{:S(2)}) collective-permute-start(f32[64,128]{1,0:T(8,128)S(1)} %add.39), channel_id=1, source_target_pairs={{0,6},{1,7},{2,4},{3,5},{4,2},{5,3},{6,0},{7,1},{8,14},{9,15},{10,... | collective-permute-start | bytes 98312 | tf_op jit(solution)/shard_map/ppermute | solution.py:158
  46.8 8.8 %collective-permute-start.22 = (f32[64,128]{1,0:T(8,128)S(1)}, f32[64,128]{1,0:T(8,128)S(1)}, u32[]{:S(2)}, u32[]{:S(2)}) collective-permute-start(f32[64,128]{1,0:T(8,128)S(1)} %add_add_fusion), channel_id=1, source_target_pairs={{0,8},{1,9},{2,10},{3,11},{4,12},{5,13},{6,14},{7,15},{8,0},{9,1},... | collective-permute-start | bytes 98312 | tf_op jit(solution)/shard_map/ppermute | solution.py:158
  51.2 4.4 %collective-permute-start.23 = (f32[64,128]{1,0:T(8,128)S(1)}, f32[64,128]{1,0:T(8,128)S(1)}, u32[]{:S(2)}, u32[]{:S(2)}) collective-permute-start(f32[64,128]{1,0:T(8,128)S(1)} %add_add_fusion), channel_id=1, source_target_pairs={{0,16},{1,17},{2,18},{3,19},{4,20},{5,21},{6,22},{7,23},{8,24},{9,... | collective-permute-start | bytes 98312 | tf_op jit(solution)/shard_map/ppermute | solution.py:158
  51.7 7.7 %collective-permute-start.24 = (f32[64,128]{1,0:T(8,128)S(1)}, f32[64,128]{1,0:T(8,128)S(1)}, u32[]{:S(2)}, u32[]{:S(2)}) collective-permute-start(f32[64,128]{1,0:T(8,128)S(1)} %add_add_fusion), channel_id=1, source_target_pairs={{0,24},{1,25},{2,26},{3,27},{4,28},{5,29},{6,30},{7,31},{8,16},{9,... | collective-permute-start | bytes 98312 | tf_op jit(solution)/shard_map/ppermute | solution.py:158
  52.7 8.3 %collective-permute-start.17 = (f32[256,128]{1,0:T(8,128)S(1)}, f32[256,128]{1,0:T(8,128)S(1)}, u32[]{:S(2)}, u32[]{:S(2)}) collective-permute-start(f32[256,128]{1,0:T(8,128)S(1)} %get-tuple-element.30), channel_id=1, source_target_pairs={{0,8},{1,9},{2,10},{3,11},{4,12},{5,13},{6,14},{7,15},{8,0},{9,1},... | collective-permute-start | bytes 393224 | tf_op jit(solution)/shard_map/ppermute | solution.py:158

commit v3 on v2

v3 whole, which is shorter than its diff:
```python
import functools

import jax
import jax.numpy as jnp
from jax import lax
from jax.experimental import pallas as pl
from jax.experimental.pallas import tpu as pltpu
from jax.sharding import PartitionSpec as P

GROUP = 8
AXES = ("tm", "blk")
HIGH = lax.Precision.HIGH
VMEM_LIMIT = 16 << 20
ORDER = (7, 6, 5, 4, 3, 2, 1, 0)
CHUNK = 32
ROWS = 256


def dot(a, b):
    return jnp.dot(a, b, precision=HIGH, preferred_element_type=jnp.float32)


def tie(*values):
    return lax.optimization_barrier(values)


def split(value):
    upper = value.astype(jnp.bfloat16)
    lower = (value - upper.astype(jnp.float32)).astype(jnp.bfloat16)
    return upper, lower


def three_passes(stacked, upper, lower):
    height = stacked.shape[0] // 2
    both = jnp.dot(stacked, upper, preferred_element_type=jnp.float32)
    more = jnp.dot(stacked[:height], lower, preferred_element_type=jnp.float32)
    return both[:height] + both[height:] + more


def split_tile_kernel(piece, where, tile, *refs):
    *given, upper, lower, mark, sums, staged, arrived = refs
    high_count, group = arrived.shape
    rows, values = given[:high_count], given[high_count:]
    blocks = [(e, j) for j in range(group) for e in range(high_count)]

    def copy(e, j):
        source_row = pl.multiple_of((where[1] ^ e) * piece, piece)
        source_col = pl.multiple_of((where[0] ^ j) * piece, piece)
        return pltpu.make_async_copy(
            tile.at[pl.ds(source_row, piece), pl.ds(source_col, piece)],
            staged.at[pl.ds(e * piece, piece), pl.ds(j * piece, piece)],
            arrived.at[e, j],
        )

    for e, j in blocks:
        copy(e, j).start()
    row = lax.broadcasted_iota(jnp.int32, mark.shape, 0)
    mark[...] = jnp.where(row + 1 == where[2], 1.0, 0.0)
    stacked = [jnp.concatenate(split(row[...]), axis=0) for row in rows]
    for e, value in enumerate(values):
        total = three_passes(stacked[e], *split(value[...]))
        to = (slice(None), pl.ds(group * piece, value.shape[1]))
        sums[to] = sums[to] + total if e else total
    for e, j in blocks:
        copy(e, j).wait()
        at = (pl.ds(e * piece, piece), pl.ds(j * piece, piece))
        for r in range(0, piece, CHUNK):
            part = (pl.ds(e * piece + r, CHUNK), pl.ds(j * piece, piece))
            upper[part], lower[part] = split(staged[part])
        if rows:
            total = three_passes(stacked[e], upper[at], lower[at])
            to = (slice(None), pl.ds(j * piece, piece))
            sums[to] = sums[to] + total if e else total


def split_tile(tile, where, piece, steps, rows=(), values=()):
    high_count, group = tile.shape[0] // piece, tile.shape[1] // piece
    half = jax.ShapeDtypeStruct(tile.shape, jnp.bfloat16)
    mark = jax.ShapeDtypeStruct((-(-steps // 8) * 8, 128), jnp.float32)
    sums = mark
    if rows:
        sums = jax.ShapeDtypeStruct((rows[0].shape[0], tile.shape[1] + values[0].shape[1]), jnp.float32)
    in_vmem = pl.BlockSpec(memory_space=pltpu.VMEM)
    return pl.pallas_call(
        functools.partial(split_tile_kernel, piece),
        out_shape=[half, half, mark, sums],
        in_specs=[pl.BlockSpec(memory_space=pltpu.SMEM), pl.BlockSpec(memory_space=pltpu.HBM)]
        + [in_vmem] * (len(rows) + len(values)),
        out_specs=[in_vmem] * 4,
        scratch_shapes=[
            pltpu.VMEM(tile.shape, jnp.float32),
            pltpu.SemaphoreType.DMA((high_count, group)),
        ],
        cost_estimate=pl.CostEstimate(
            flops=8 * tile.size, bytes_accessed=8 * tile.size, transcendentals=0
        ),
        compiler_params=pltpu.CompilerParams(vmem_limit_bytes=VMEM_LIMIT),
    )(where, pltpu.with_memory_space_constraint(tile, pltpu.HBM), *rows, *values)


def product_kernel(count, sign, upper, lower, _, *refs):
    parts, rest = refs[:count], refs[count:]
    columns = rest[-1]
    outs = rest[:-1]
    high_count = len(outs) if sign > 0 else len(outs) // 2
    bases = outs[: len(outs) - high_count]
    outs = outs[len(outs) - high_count :]
    piece, width = parts[0].shape
    for j, part in zip(ORDER, parts):
        at = pl.ds(j * piece, piece)
        columns[at, :width], columns[at, width:] = split(part[...])
    for e, out in enumerate(outs):
        for r in range(0, piece, ROWS):
            at, to = pl.ds(e * piece + r, ROWS), pl.ds(r, ROWS)
            both = jnp.dot(upper[at], columns[...], preferred_element_type=jnp.float32)
            more = jnp.dot(lower[at], columns[:, :width], preferred_element_type=jnp.float32)
            total = both[:, :width] + both[:, width:] + more
            out[to] = total if sign > 0 else bases[e][to] - total


def tile_product(halves, parts, bases=None):
    rows, cols = halves[0].shape
    piece, width = parts[0].shape
    high_count = rows // piece
    block = jax.ShapeDtypeStruct((piece, width), jnp.float32)
    in_vmem = pl.BlockSpec(memory_space=pltpu.VMEM)
    operands = [*halves, *(parts[j] for j in ORDER), *(bases or [])]
    return pl.pallas_call(
        functools.partial(product_kernel, len(parts), 1 if bases is None else -1),
        out_shape=[block] * high_count,
        in_specs=[in_vmem] * len(operands),
        out_specs=[in_vmem] * high_count,
        scratch_shapes=[pltpu.VMEM((cols, 2 * width), jnp.bfloat16)],
        cost_estimate=pl.CostEstimate(
            flops=6 * rows * cols * width, bytes_accessed=4 * rows * cols, transcendentals=0
        ),
        compiler_params=pltpu.CompilerParams(vmem_limit_bytes=VMEM_LIMIT),
    )(*operands)


def terms_kernel(sums, swapped, _, *refs):
    *parts, out = refs
    piece = parts[0].shape[0]
    at = pl.ds(GROUP * piece, out.shape[1])
    total = sums[:, at] + swapped[:, at]
    for j, part in zip(ORDER, parts):
        weights = sums[:, pl.ds(j * piece, piece)] + swapped[:, pl.ds((j ^ 1) * piece, piece)]
        total = total - three_passes(jnp.concatenate(split(weights), axis=0), *split(part[...]))
    out[...] = total


def terms_product(sums, swapped, mark, parts):
    in_vmem = pl.BlockSpec(memory_space=pltpu.VMEM)
    height, cols = sums.shape
    width = parts[0].shape[1]
    return pl.pallas_call(
        terms_kernel,
        out_shape=jax.ShapeDtypeStruct((height, width), jnp.float32),
        in_specs=[in_vmem] * (len(parts) + 3),
        out_specs=in_vmem,
        cost_estimate=pl.CostEstimate(
            flops=6 * height * cols * width, bytes_accessed=8 * height * cols, transcendentals=0
        ),
        compiler_params=pltpu.CompilerParams(vmem_limit_bytes=VMEM_LIMIT),
    )(sums, swapped, mark, *(parts[j] for j in ORDER))


def on_device(propagator, inv_diag, rhs, arrow, tip_inv, tip_rhs):
    steps = lax.axis_size("tm")
    blocks = lax.axis_size("blk")
    high_count = blocks // GROUP
    step = lax.axis_index("tm")
    position = lax.axis_index("blk")
    low = position % GROUP
    high = position // GROUP
    piece = rhs.shape[1]
    width = rhs.shape[2]

    def move(value, flip, ahead=0):
        route = [
            (t * blocks + b, (t + ahead) % steps * blocks + (b ^ flip))
            for t in range(steps)
            for b in range(blocks)
        ]
        return lax.ppermute(value, AXES, route)

    def scatter(own):
        return [move(own, flip) for flip in range(2, GROUP, 2)]

    def swap(own, sent):
        parts = []
        for part in [own, *sent]:
            parts += [part, move(part, 1)]
        return parts

    by_kernel = piece % 256 == 0 and width % 128 == 0
    where = jnp.stack([low, high, step]).astype(jnp.int32)

    def prepared(tile, rows=(), values=()):
        if by_kernel:
            *halves, mark, sums = split_tile(tile, where, piece, steps, rows, values)
            return halves, mark, sums
        mark = jnp.where(jnp.arange(steps)[:, None] + 1 == step, 1.0, jnp.zeros((1, width)))
        if not rows:
            return tile, mark, None
        columns = jnp.concatenate([in_order(tile), jnp.concatenate(values, axis=0)], axis=1)
        return tile, mark, dot(jnp.concatenate(rows, axis=1), columns)

    def in_order(tile):
        rows = [
            lax.dynamic_slice_in_dim(tile, (high ^ e) * piece, piece, 0) for e in range(high_count)
        ]
        tile = jnp.concatenate(rows, axis=0)
        cols = [lax.dynamic_slice_in_dim(tile, (low ^ j) * piece, piece, 1) for j in range(GROUP)]
        return jnp.concatenate(cols, axis=1)

    def apply_tile(tile, mark, parts, bases=None):
        if by_kernel:
            return tile_product([*tile, mark], parts, bases)
        total = dot(in_order(tile), jnp.concatenate(parts, axis=0))
        found = [total[e * piece : (e + 1) * piece] for e in range(high_count)]
        return found if bases is None else [b - f for b, f in zip(bases, found)]

    def subtract_product(sums, swapped, mark, parts):
        if by_kernel:
            return terms_product(sums, swapped, mark, parts)
        total = sums[:, GROUP * piece :] + swapped[:, GROUP * piece :]
        for j, part in enumerate(parts):
            k = j ^ 1
            weights = sums[:, j * piece : (j + 1) * piece] + swapped[:, k * piece : (k + 1) * piece]
            total = total - dot(weights, part)
        return total

    def tip_rounds():
        bits = [1 << k for k in range(1, blocks.bit_length() - 1)]
        rounds = []
        if steps == 2:
            rounds.append([(bits[0], 0), (0, 1), (bits[0], 1)])
            bits = bits[1:]
        elif steps > 2:
            rounds.append([(0, ahead) for ahead in range(1, steps)])
        for k in range(0, len(bits), 2):
            a, *b = bits[k : k + 2]
            rounds.append([(a, 0)] + [(f, 0) for f in b] + [(a | f, 0) for f in b])
        return rounds

    sent = scatter(rhs[0])
    arrows = [arrow[0]] + [move(arrow[0], e * GROUP) for e in range(1, high_count)]
    tile, mark, _ = prepared(inv_diag[0])
    sent[0], mark, *arrows[1:] = tie(sent[0], mark, *arrows[1:])
    mine = mark
    partial = apply_tile(tile, mark, swap(rhs[0], sent))
    if steps == 1:
        terms = sum(dot(arrows[e], partial[e]) for e in range(high_count))
        terms = terms + move(terms, 1)
    for t in range(steps - 1):
        arriving = [move(partial[e], e * GROUP, 1) for e in reversed(range(high_count))]
        if t == steps - 2:
            tile, mark, sums = prepared(propagator[0], arrows, partial)
            arriving[0], mark = tie(arriving[0], mark)
            swapped = move(sums, 1)
        elif t == 0:
            tile, mark, _ = prepared(propagator[0])
        earlier = jnp.where(mine[t : t + 1] > 0.0, sum(arriving), 0.0)
        parts = swap(earlier, scatter(earlier))
        if t == steps - 2:
            terms = mark = subtract_product(sums, swapped, mark, parts)
        partial = apply_tile(tile, mark, parts, partial)

    others = [move(partial[e], e * GROUP) for e in range(1, high_count)]
    for k, moves in enumerate(tip_rounds()):
        around = [move(terms, flip, ahead) for flip, ahead in reversed(moves)]
        if k == 1:
            *others, around[0] = tie(*others, around[0])
        terms = terms + sum(around)
    solved = partial[0] + sum(others)
    tip = dot(tip_inv, tip_rhs - terms)
    return solved[None], tip


def solution(mesh):
    placed = (
        P("tm", "blk", None),
        P("tm", "blk", None),
        P("tm", "blk", None),
        P("tm", None, "blk"),
        P(),
        P(),
    )
    return jax.shard_map(
        on_device,
        mesh=mesh,
        in_specs=placed,
        out_specs=(P("tm", "blk", None), P()),
        check_vma=False,
    )
```

time: 61.9 us -> 54.6 us (0.88)
  waiting for transfers between devices: 21.2 us -> 14.7 us
  starting transfers between devices: 29.3 us -> 26.8 us
  Pallas kernels: 8.62 us -> 10.7 us
    ppermute x25, waiting for transfers between devices: 21.2 us -> 14.7 us  [move(): return lax.ppermute(value, AXES, route)]
    ppermute x25, starting transfers between devices: 29.3 us -> 26.8 us  [move(): return lax.ppermute(value, AXES, route)]
    pallas_call x2, Pallas kernels: 5.8 us -> 7.64 us  [split_tile(): pl.pallas_call(functools.partial(split_tile_kernel, piece), out_shape=[ha...]
  transfers between devices with their start and end apart: 25 -> 25, of which waited for: 16 -> 13; matrix products, arithmetic and copies ran while one was open for 1% -> 1% of each run, Pallas kernels for 9% -> 16%
where the time goes in v3:
time: 54.6 us; the launch traced here: 54.4 us
  starting transfers between devices  26.8 us (49%)
  waiting for transfers between devices  14.7 us (27%)
  Pallas kernels  10.7 us (20%)
  other arithmetic  0.79 us (1%)
  matrix products  0.77 us (1%)
  between operations  0.74 us (1%)
    ppermute x25, starting transfers between devices, move(): return lax.ppermute(value, AXES, route)  26.8 us
    ppermute x25, waiting for transfers between devices, move(): return lax.ppermute(value, AXES, route)  14.7 us
    pallas_call x2, Pallas kernels, split_tile(): pl.pallas_call(functools.partial(split_tile_kernel, piece), out_shape=[ha...  7.64 us
    pallas_call x2, Pallas kernels, tile_product(): pl.pallas_call(functools.partial(product_kernel, len(parts), 1 if bases i...  2.61 us
  transfers between devices with their start and end apart: 25, of which 13 were waited for; matrix products, arithmetic and copies ran while one was open for 1% of the time, Pallas kernels for 16%

profile of v3, /device:TPU:0, one launch (start us, length us, event | category | flops | bytes accessed | tf_op | source)
XLA Modules:
  0.0 54.4 jit_solution(17945281451775827015)
XLA Ops:
  0.6 0.0 copy-start
  0.6 3.0 %collective-permute-start = (f32[256,128]{1,0:T(8,128)}, f32[256,128]{1,0:T(8,128)S(1)}, u32[]{:S(2)}, u32[]{:S(2)}) collective-permute-start(f32[256,128]{1,0:T(8,128)} %bitcast.14), channel_id=1, source_target_pairs={{0,2},{1,3},{2,0},{3,1},{4,6},{5,7},{6,4},{7,5},{8,10},{9,11},{10,... | collective-permute-start | bytes 393224 | tf_op jit(solution)/shard_map/ppermute | solution.py:185
  3.6 1.6 %collective-permute-start.4 = (f32[256,128]{1,0:T(8,128)}, f32[256,128]{1,0:T(8,128)S(1)}, u32[]{:S(2)}, u32[]{:S(2)}) collective-permute-start(f32[256,128]{1,0:T(8,128)} %bitcast.15), channel_id=1, source_target_pairs={{0,4},{1,5},{2,6},{3,7},{4,0},{5,1},{6,2},{7,3},{8,12},{9,13},{10,... | collective-permute-start | bytes 393224 | tf_op jit(solution)/shard_map/ppermute | solution.py:185
  5.2 0.0 collective-permute-start.2
  5.2 0.0 collective-permute-start.7
  5.2 3.0 %collective-permute-start.1 = (f32[64,256]{1,0:T(8,128)}, f32[64,256]{1,0:T(8,128)S(1)}, u32[]{:S(2)}, u32[]{:S(2)}) collective-permute-start(f32[64,256]{1,0:T(8,128)} %bitcast.19), channel_id=1, source_target_pairs={{0,8},{1,9},{2,10},{3,11},{4,12},{5,13},{6,14},{7,15},{8,0},{9,1},... | collective-permute-start | bytes 196616 | tf_op jit(solution)/shard_map/ppermute | solution.py:185
  8.2 0.1 pad_add_fusion.where
  8.3 0.0 copy-start.1
  8.3 3.4 %shard_map.77 = (bf16[512,2048]{1,0:T(8,128)(2,1)S(1)}, bf16[512,2048]{1,0:T(8,128)(2,1)S(1)}, f32[8,128]{1,0:T(8,128)S(1)}, f32[8,128]{1,0:T(8,128)}) custom-call(s32[3]{0:T(128)S(1)} %pad_add_fusion.where, f32[512,2048]{1,0:T(8,128)} %bitcast.22), custom_call_target="tpu_custom_call" | custom-call | flops 8388608 | bytes 8388608 | tf_op jit(solution)/shard_map/pallas_call | solution.py:84
  11.8 0.5 collective-permute-done.1.refs_1_
  12.2 0.0 collective-permute-done.refs_5_
  12.2 0.0 collective-permute-done.4.refs_3_
  12.2 0.0 collective-permute-start.5
  12.2 0.6 %collective-permute-done.2.refs_1_ = f32[256,128]{1,0:T(8,128)S(1)} collective-permute-done((f32[256,128]{1,0:T(8,128)}, f32[256,128]{1,0:T(8,128)S(1)}, u32[]{:S(2)}, u32[]{:S(2)}) %collective-permute-start.2) | collective-permute-done | bytes 131104 | tf_op jit(solution)/shard_map/ppermute | solution.py:185
  12.9 0.0 collective-permute-start.3
  12.9 0.5 collective-permute-start.6
  13.4 0.0 collective-permute-done.7.refs_6_
  13.4 0.2 collective-permute-done.5.refs_2_
  13.6 0.6 %collective-permute-done.3.refs_0_ = f32[256,128]{1,0:T(8,128)S(1)} collective-permute-done((f32[256,128]{1,0:T(8,128)S(1)}, f32[256,128]{1,0:T(8,128)S(1)}, u32[]{:S(2)}, u32[]{:S(2)}) %collective-permute-start.3) | collective-permute-done | bytes 131104 | tf_op jit(solution)/shard_map/ppermute | solution.py:185
  14.2 0.2 collective-permute-done.6.refs_4_
  14.4 0.0 copy-done.1
  14.4 1.3 %shard_map.78 = (f32[256,128]{1,0:T(8,128)S(1)}, f32[256,128]{1,0:T(8,128)S(1)}) custom-call(bf16[512,2048]{1,0:T(8,128)(2,1)S(1)} %get-tuple-element.22.upper, bf16[512,2048]{1,0:T(8,128)(2,1)S(1)} %get-tuple-element.23.lower, f32[8,128]{1,0:T(8,128)S(1)} %get-tuple-element.24._, f32[256,128]{1,0:T(8,128)S(1)} %collective-permute-done.3.refs_0_, ...), custom_call_target="tpu_custom_call" | custom-call | flops 805306368 | bytes 4194304 | tf_op jit(solution)/shard_map/pallas_call | solution.py:128
  15.7 1.7 %collective-permute-start.10 = (f32[256,128]{1,0:T(8,128)S(1)}, f32[256,128]{1,0:T(8,128)S(1)}, u32[]{:S(2)}, u32[]{:S(2)}) collective-permute-start(f32[256,128]{1,0:T(8,128)S(1)} %get-tuple-element.26.refs_2_.refs_8_), channel_id=1, source_target_pairs={{0,16},{1,17},{2,18},{3,19},{4,20},{5,21},{6,22},{7,23},{8,24},{9,... | collective-permute-start | bytes 393224 | tf_op jit(solution)/shard_map/ppermute | solution.py:185
  17.5 2.8 %collective-permute-start.9 = (f32[256,128]{1,0:T(8,128)S(1)}, f32[256,128]{1,0:T(8,128)S(1)}, u32[]{:S(2)}, u32[]{:S(2)}) collective-permute-start(f32[256,128]{1,0:T(8,128)S(1)} %get-tuple-element.27.refs_3_.refs_9_), channel_id=1, source_target_pairs={{0,24},{1,25},{2,26},{3,27},{4,28},{5,29},{6,30},{7,31},{8,16},{9,... | collective-permute-start | bytes 393224 | tf_op jit(solution)/shard_map/ppermute | solution.py:185
  20.2 0.0 copy-done.2
  20.2 4.2 %shard_map.79 = (bf16[512,2048]{1,0:T(8,128)(2,1)S(1)}, bf16[512,2048]{1,0:T(8,128)(2,1)S(1)}, f32[8,128]{1,0:T(8,128)S(1)}, f32[64,2176]{1,0:T(8,128)S(1)}) custom-call(s32[3]{0:T(128)S(1)} %pad_add_fusion.where, f32[512,2048]{1,0:T(8,128)} %bitcast.21, f32[64,256]{1,0:T(8,128)S(1)} %bitcast.20, f32[64,256]{1,0:T(8,128)S(1)} %collective-permute-done.1.refs_1_, ...), custom_call_target="tpu_custom_call" | custom-call | flops 8388608 | bytes 8388608 | tf_op jit(solution)/shard_map/pallas_call | solution.py:84
  24.4 0.1 collective-permute-start.8
  24.5 3.0 %collective-permute-done.9 = f32[256,128]{1,0:T(8,128)S(1)} collective-permute-done((f32[256,128]{1,0:T(8,128)S(1)}, f32[256,128]{1,0:T(8,128)S(1)}, u32[]{:S(2)}, u32[]{:S(2)}) %collective-permute-start.9) | collective-permute-done | bytes 131104 | tf_op jit(solution)/shard_map/ppermute | solution.py:185
  27.5 0.0 collective-permute-done.10
  27.5 1.5 %collective-permute-start.15 = (f32[256,128]{1,0:T(8,128)S(1)}, f32[256,128]{1,0:T(8,128)S(1)}, u32[]{:S(2)}, u32[]{:S(2)}) collective-permute-start(f32[256,128]{1,0:T(8,128)S(1)} %add_select_fusion.refs_7_), channel_id=1, source_target_pairs={{0,2},{1,3},{2,0},{3,1},{4,6},{5,7},{6,4},{7,5},{8,10},{9,11},{10,... | collective-permute-start | bytes 393224 | tf_op jit(solution)/shard_map/ppermute | solution.py:185
  29.1 0.0 collective-permute-start.13
  29.1 2.0 %collective-permute-start.11 = (f32[256,128]{1,0:T(8,128)S(1)}, f32[256,128]{1,0:T(8,128)S(1)}, u32[]{:S(2)}, u32[]{:S(2)}) collective-permute-start(f32[256,128]{1,0:T(8,128)S(1)} %add_select_fusion.refs_7_), channel_id=1, source_target_pairs={{0,6},{1,7},{2,4},{3,5},{4,2},{5,3},{6,0},{7,1},{8,14},{9,15},{10,... | collective-permute-start | bytes 393224 | tf_op jit(solution)/shard_map/ppermute | solution.py:185
  31.1 0.0 collective-permute-start.17
  31.1 2.9 %collective-permute-done.15.refs_5_ = f32[256,128]{1,0:T(8,128)S(1)} collective-permute-done((f32[256,128]{1,0:T(8,128)S(1)}, f32[256,128]{1,0:T(8,128)S(1)}, u32[]{:S(2)}, u32[]{:S(2)}) %collective-permute-start.15) | collective-permute-done | bytes 131104 | tf_op jit(solution)/shard_map/ppermute | solution.py:185
  34.0 0.0 collective-permute-start.16
  34.0 0.8 %collective-permute-done.13.refs_3_ = f32[256,128]{1,0:T(8,128)S(1)} collective-permute-done((f32[256,128]{1,0:T(8,128)S(1)}, f32[256,128]{1,0:T(8,128)S(1)}, u32[]{:S(2)}, u32[]{:S(2)}) %collective-permute-start.13) | collective-permute-done | bytes 131104 | tf_op jit(solution)/shard_map/ppermute | solution.py:185
  34.8 0.0 collective-permute-start.14
  34.8 1.2 %collective-permute-done.11.refs_1_ = f32[256,128]{1,0:T(8,128)S(1)} collective-permute-done((f32[256,128]{1,0:T(8,128)S(1)}, f32[256,128]{1,0:T(8,128)S(1)}, u32[]{:S(2)}, u32[]{:S(2)}) %collective-permute-start.11) | collective-permute-done | bytes 131104 | tf_op jit(solution)/shard_map/ppermute | solution.py:185
  36.0 0.0 collective-permute-start.12
  36.0 0.0 collective-permute-done.17.refs_6_
  36.0 0.0 collective-permute-done.16.refs_4_
  36.0 0.1 collective-permute-done.14.refs_2_
  36.2 1.2 %collective-permute-done.12.refs_0_ = f32[256,128]{1,0:T(8,128)S(1)} collective-permute-done((f32[256,128]{1,0:T(8,128)S(1)}, f32[256,128]{1,0:T(8,128)S(1)}, u32[]{:S(2)}, u32[]{:S(2)}) %collective-permute-start.12) | collective-permute-done | bytes 131104 | tf_op jit(solution)/shard_map/ppermute | solution.py:185
  37.4 0.0 collective-permute-done.8.swapped
  37.4 0.4 shard_map.80._
  37.8 1.7 %collective-permute-start.21 = (f32[64,128]{1,0:T(8,128)S(1)}, f32[64,128]{1,0:T(8,128)S(1)}, u32[]{:S(2)}, u32[]{:S(2)}) collective-permute-start(f32[64,128]{1,0:T(8,128)S(1)} %shard_map.80._), channel_id=1, source_target_pairs={{0,2},{1,3},{2,0},{3,1},{4,6},{5,7},{6,4},{7,5},{8,10},{9,11},{10,... | collective-permute-start | bytes 98312 | tf_op jit(solution)/shard_map/ppermute | solution.py:185
  39.5 0.5 collective-permute-start.20
  40.0 1.3 %collective-permute-start.19 = (f32[64,128]{1,0:T(8,128)S(1)}, f32[64,128]{1,0:T(8,128)S(1)}, u32[]{:S(2)}, u32[]{:S(2)}) collective-permute-start(f32[64,128]{1,0:T(8,128)S(1)} %shard_map.80._), channel_id=1, source_target_pairs={{0,18},{1,19},{2,16},{3,17},{4,22},{5,23},{6,20},{7,21},{8,26},{9,... | collective-permute-start | bytes 98312 | tf_op jit(solution)/shard_map/ppermute | solution.py:185
  41.3 1.3 %shard_map.81 = (f32[256,128]{1,0:T(8,128)S(1)}, f32[256,128]{1,0:T(8,128)S(1)}) custom-call(bf16[512,2048]{1,0:T(8,128)(2,1)S(1)} %get-tuple-element.28.upper, bf16[512,2048]{1,0:T(8,128)(2,1)S(1)} %get-tuple-element.29.lower, f32[64,128]{1,0:T(8,128)S(1)} %shard_map.80._, f32[256,128]{1,0:T(8,128)S(1)} %collective-permute-done.12.refs_0_, ...), custom_call_target="tpu_custom_call" | custom-call | flops 805306368 | bytes 4194304 | tf_op jit(solution)/shard_map/pallas_call | solution.py:128
  42.6 2.5 %collective-permute-start.18 = (f32[256,128]{1,0:T(8,128)S(1)}, f32[256,128]{1,0:T(8,128)S(1)}, u32[]{:S(2)}, u32[]{:S(2)}) collective-permute-start(f32[256,128]{1,0:T(8,128)S(1)} %get-tuple-element.35), channel_id=1, source_target_pairs={{0,8},{1,9},{2,10},{3,11},{4,12},{5,13},{6,14},{7,15},{8,0},{9,1},... | collective-permute-start | bytes 393224 | tf_op jit(solution)/shard_map/ppermute | solution.py:185
  45.1 0.0 collective-permute-done.21
  45.1 0.0 collective-permute-done.20
  45.1 0.0 collective-permute-done.19
  45.2 3.3 %collective-permute-start.22 = (f32[64,128]{1,0:T(8,128)S(1)}, f32[64,128]{1,0:T(8,128)S(1)}, u32[]{:S(2)}, u32[]{:S(2)}) collective-permute-start(f32[64,128]{1,0:T(8,128)S(1)} %add_add_fusion), channel_id=1, source_target_pairs={{0,12},{1,13},{2,14},{3,15},{4,8},{5,9},{6,10},{7,11},{8,4},{9,5},... | collective-permute-start | bytes 98312 | tf_op jit(solution)/shard_map/ppermute | solution.py:185
  48.5 0.0 collective-permute-start.24
  48.5 1.1 %collective-permute-start.23 = (f32[64,128]{1,0:T(8,128)S(1)}, f32[64,128]{1,0:T(8,128)S(1)}, u32[]{:S(2)}, u32[]{:S(2)}) collective-permute-start(f32[64,128]{1,0:T(8,128)S(1)} %add_add_fusion), channel_id=1, source_target_pairs={{0,8},{1,9},{2,10},{3,11},{4,12},{5,13},{6,14},{7,15},{8,0},{9,1},... | collective-permute-start | bytes 98312 | tf_op jit(solution)/shard_map/ppermute | solution.py:185
  49.6 1.4 %collective-permute-done.22 = f32[64,128]{1,0:T(8,128)S(1)} collective-permute-done((f32[64,128]{1,0:T(8,128)S(1)}, f32[64,128]{1,0:T(8,128)S(1)}, u32[]{:S(2)}, u32[]{:S(2)}) %collective-permute-start.22) | collective-permute-done | bytes 32800 | tf_op jit(solution)/shard_map/ppermute | solution.py:185
  51.0 1.9 %collective-permute-done.18 = f32[256,128]{1,0:T(8,128)S(1)} collective-permute-done((f32[256,128]{1,0:T(8,128)S(1)}, f32[256,128]{1,0:T(8,128)S(1)}, u32[]{:S(2)}, u32[]{:S(2)}) %collective-permute-start.18) | collective-permute-done | bytes 131104 | tf_op jit(solution)/shard_map/ppermute | solution.py:185
  53.0 0.7 %add_bitcast_fusion = f32[1,256,128]{2,1,0:T(8,128)} fusion(f32[256,128]{1,0:T(8,128)S(1)} %get-tuple-element.34, f32[256,128]{1,0:T(8,128)S(1)} %collective-permute-done.18), kind=kLoop, calls=%fused_computation.1 | loop fusion | flops 32768 | bytes 393216 | tf_op jit(solution)/shard_map/broadcast_in_dim | solution.py:278
  53.7 0.0 collective-permute-done.24
  53.7 0.0 collective-permute-done.23
  53.7 0.0 copy-done
  53.7 0.0 copy-done.3
  53.7 0.8 %convolution_bitcast_fusion = f32[64,128]{1,0:T(8,128)} fusion(f32[64,64]{1,0:T(8,128)S(1)} %copy-done, f32[64,128]{1,0:T(8,128)S(1)} %copy-done.3, f32[64,128]{1,0:T(8,128)S(1)} %add_add_fusion, f32[64,128]{1,0:T(8,128)S(1)} %collective-permute-done.24, f32[64,128]{1,0:T(8,128)S(1)} %collective-permute-done.22, f32[64,128]{1,0:T(8,128)S(1)} %collective-permute-done.23), kind=kOutput, calls=%fused_computation | convolution fusion | flops 3178496 | bytes 212992 | tf_op jit(solution)/shard_map/dot_general | solution.py:20
  (5 shorter events, 0.0 us)
Async XLA Ops:
  0.6 53.0 %copy-start = (f32[64,64]{1,0:T(8,128)S(1)}, f32[64,64]{1,0:T(8,128)}, u32[]{:S(2)}) copy-start(f32[64,64]{1,0:T(8,128)} %param.10) | copy-start | bytes 49156
  0.6 11.6 %collective-permute-start = (f32[256,128]{1,0:T(8,128)}, f32[256,128]{1,0:T(8,128)S(1)}, u32[]{:S(2)}, u32[]{:S(2)}) collective-permute-start(f32[256,128]{1,0:T(8,128)} %bitcast.14), channel_id=1, source_target_pairs={{0,2},{1,3},{2,0},{3,1},{4,6},{5,7},{6,4},{7,5},{8,10},{9,11},{10,... | collective-permute-start | bytes 393224 | tf_op jit(solution)/shard_map/ppermute | solution.py:185
  3.6 8.6 %collective-permute-start.4 = (f32[256,128]{1,0:T(8,128)}, f32[256,128]{1,0:T(8,128)S(1)}, u32[]{:S(2)}, u32[]{:S(2)}) collective-permute-start(f32[256,128]{1,0:T(8,128)} %bitcast.15), channel_id=1, source_target_pairs={{0,4},{1,5},{2,6},{3,7},{4,0},{5,1},{6,2},{7,3},{8,12},{9,13},{10,... | collective-permute-start | bytes 393224 | tf_op jit(solution)/shard_map/ppermute | solution.py:185
  5.2 7.6 %collective-permute-start.2 = (f32[256,128]{1,0:T(8,128)}, f32[256,128]{1,0:T(8,128)S(1)}, u32[]{:S(2)}, u32[]{:S(2)}) collective-permute-start(f32[256,128]{1,0:T(8,128)} %bitcast.16), channel_id=1, source_target_pairs={{0,6},{1,7},{2,4},{3,5},{4,2},{5,3},{6,0},{7,1},{8,14},{9,15},{10,... | collective-permute-start | bytes 393224 | tf_op jit(solution)/shard_map/ppermute | solution.py:185
  5.2 8.2 %collective-permute-start.7 = (f32[256,128]{1,0:T(8,128)}, f32[256,128]{1,0:T(8,128)S(1)}, u32[]{:S(2)}, u32[]{:S(2)}) collective-permute-start(f32[256,128]{1,0:T(8,128)} %bitcast.17), channel_id=1, source_target_pairs={{0,1},{1,0},{2,3},{3,2},{4,5},{5,4},{6,7},{7,6},{8,9},{9,8},{10,11... | collective-permute-start | bytes 393224 | tf_op jit(solution)/shard_map/ppermute | solution.py:185
  5.2 7.0 %collective-permute-start.1 = (f32[64,256]{1,0:T(8,128)}, f32[64,256]{1,0:T(8,128)S(1)}, u32[]{:S(2)}, u32[]{:S(2)}) collective-permute-start(f32[64,256]{1,0:T(8,128)} %bitcast.19), channel_id=1, source_target_pairs={{0,8},{1,9},{2,10},{3,11},{4,12},{5,13},{6,14},{7,15},{8,0},{9,1},... | collective-permute-start | bytes 196616 | tf_op jit(solution)/shard_map/ppermute | solution.py:185
  8.3 6.1 %copy-start.1 = (f32[1,256,128]{2,1,0:T(8,128)S(1)}, f32[1,256,128]{2,1,0:T(8,128)}, u32[]{:S(2)}) copy-start(f32[1,256,128]{2,1,0:T(8,128)} %param.8) | copy-start | bytes 393220
  12.2 1.4 %collective-permute-start.5 = (f32[256,128]{1,0:T(8,128)S(1)}, f32[256,128]{1,0:T(8,128)S(1)}, u32[]{:S(2)}, u32[]{:S(2)}) collective-permute-start(f32[256,128]{1,0:T(8,128)S(1)} %collective-permute-done.4.refs_3_), channel_id=1, source_target_pairs={{0,1},{1,0},{2,3},{3,2},{4,5},{5,4},{6,7},{7,6},{8,9},{9,8},{10,11... | collective-permute-start | bytes 393224 | tf_op jit(solution)/shard_map/ppermute | solution.py:185
  12.9 1.3 %collective-permute-start.3 = (f32[256,128]{1,0:T(8,128)S(1)}, f32[256,128]{1,0:T(8,128)S(1)}, u32[]{:S(2)}, u32[]{:S(2)}) collective-permute-start(f32[256,128]{1,0:T(8,128)S(1)} %collective-permute-done.2.refs_1_), channel_id=1, source_target_pairs={{0,1},{1,0},{2,3},{3,2},{4,5},{5,4},{6,7},{7,6},{8,9},{9,8},{10,11... | collective-permute-start | bytes 393224 | tf_op jit(solution)/shard_map/ppermute | solution.py:185
  12.9 1.5 %collective-permute-start.6 = (f32[256,128]{1,0:T(8,128)S(1)}, f32[256,128]{1,0:T(8,128)S(1)}, u32[]{:S(2)}, u32[]{:S(2)}) collective-permute-start(f32[256,128]{1,0:T(8,128)S(1)} %collective-permute-done.refs_5_), channel_id=1, source_target_pairs={{0,1},{1,0},{2,3},{3,2},{4,5},{5,4},{6,7},{7,6},{8,9},{9,8},{10,11... | collective-permute-start | bytes 393224 | tf_op jit(solution)/shard_map/ppermute | solution.py:185
  14.4 5.8 %copy-start.2 = (f32[1,64,256]{2,1,0:T(8,128)S(1)}, f32[1,64,256]{2,1,0:T(8,128)}, u32[]{:S(2)}) copy-start(f32[1,64,256]{2,1,0:T(8,128)} %param.9) | copy-start | bytes 196612
  15.7 11.8 %collective-permute-start.10 = (f32[256,128]{1,0:T(8,128)S(1)}, f32[256,128]{1,0:T(8,128)S(1)}, u32[]{:S(2)}, u32[]{:S(2)}) collective-permute-start(f32[256,128]{1,0:T(8,128)S(1)} %get-tuple-element.26.refs_2_.refs_8_), channel_id=1, source_target_pairs={{0,16},{1,17},{2,18},{3,19},{4,20},{5,21},{6,22},{7,23},{8,24},{9,... | collective-permute-start | bytes 393224 | tf_op jit(solution)/shard_map/ppermute | solution.py:185
  17.5 10.1 %collective-permute-start.9 = (f32[256,128]{1,0:T(8,128)S(1)}, f32[256,128]{1,0:T(8,128)S(1)}, u32[]{:S(2)}, u32[]{:S(2)}) collective-permute-start(f32[256,128]{1,0:T(8,128)S(1)} %get-tuple-element.27.refs_3_.refs_9_), channel_id=1, source_target_pairs={{0,24},{1,25},{2,26},{3,27},{4,28},{5,29},{6,30},{7,31},{8,16},{9,... | collective-permute-start | bytes 393224 | tf_op jit(solution)/shard_map/ppermute | solution.py:185
  24.4 12.9 %collective-permute-start.8 = (f32[64,2176]{1,0:T(8,128)S(1)}, f32[64,2176]{1,0:T(8,128)S(1)}, u32[]{:S(2)}, u32[]{:S(2)}) collective-permute-start(f32[64,2176]{1,0:T(8,128)S(1)} %get-tuple-element.30.sums), channel_id=1, source_target_pairs={{0,1},{1,0},{2,3},{3,2},{4,5},{5,4},{6,7},{7,6},{8,9},{9,8},{10,11... | collective-permute-start | bytes 1671176 | tf_op jit(solution)/shard_map/ppermute | solution.py:185
  27.5 6.4 %collective-permute-start.15 = (f32[256,128]{1,0:T(8,128)S(1)}, f32[256,128]{1,0:T(8,128)S(1)}, u32[]{:S(2)}, u32[]{:S(2)}) collective-permute-start(f32[256,128]{1,0:T(8,128)S(1)} %add_select_fusion.refs_7_), channel_id=1, source_target_pairs={{0,2},{1,3},{2,0},{3,1},{4,6},{5,7},{6,4},{7,5},{8,10},{9,11},{10,... | collective-permute-start | bytes 393224 | tf_op jit(solution)/shard_map/ppermute | solution.py:185
  29.1 5.7 %collective-permute-start.13 = (f32[256,128]{1,0:T(8,128)S(1)}, f32[256,128]{1,0:T(8,128)S(1)}, u32[]{:S(2)}, u32[]{:S(2)}) collective-permute-start(f32[256,128]{1,0:T(8,128)S(1)} %add_select_fusion.refs_7_), channel_id=1, source_target_pairs={{0,4},{1,5},{2,6},{3,7},{4,0},{5,1},{6,2},{7,3},{8,12},{9,13},{10,... | collective-permute-start | bytes 393224 | tf_op jit(solution)/shard_map/ppermute | solution.py:185
  29.1 6.9 %collective-permute-start.11 = (f32[256,128]{1,0:T(8,128)S(1)}, f32[256,128]{1,0:T(8,128)S(1)}, u32[]{:S(2)}, u32[]{:S(2)}) collective-permute-start(f32[256,128]{1,0:T(8,128)S(1)} %add_select_fusion.refs_7_), channel_id=1, source_target_pairs={{0,6},{1,7},{2,4},{3,5},{4,2},{5,3},{6,0},{7,1},{8,14},{9,15},{10,... | collective-permute-start | bytes 393224 | tf_op jit(solution)/shard_map/ppermute | solution.py:185
  31.1 4.9 %collective-permute-start.17 = (f32[256,128]{1,0:T(8,128)S(1)}, f32[256,128]{1,0:T(8,128)S(1)}, u32[]{:S(2)}, u32[]{:S(2)}) collective-permute-start(f32[256,128]{1,0:T(8,128)S(1)} %add_select_fusion.refs_7_), channel_id=1, source_target_pairs={{0,1},{1,0},{2,3},{3,2},{4,5},{5,4},{6,7},{7,6},{8,9},{9,8},{10,11... | collective-permute-start | bytes 393224 | tf_op jit(solution)/shard_map/ppermute | solution.py:185
  34.0 2.0 %collective-permute-start.16 = (f32[256,128]{1,0:T(8,128)S(1)}, f32[256,128]{1,0:T(8,128)S(1)}, u32[]{:S(2)}, u32[]{:S(2)}) collective-permute-start(f32[256,128]{1,0:T(8,128)S(1)} %collective-permute-done.15.refs_5_), channel_id=1, source_target_pairs={{0,1},{1,0},{2,3},{3,2},{4,5},{5,4},{6,7},{7,6},{8,9},{9,8},{10,11... | collective-permute-start | bytes 393224 | tf_op jit(solution)/shard_map/ppermute | solution.py:185
  34.8 1.3 %collective-permute-start.14 = (f32[256,128]{1,0:T(8,128)S(1)}, f32[256,128]{1,0:T(8,128)S(1)}, u32[]{:S(2)}, u32[]{:S(2)}) collective-permute-start(f32[256,128]{1,0:T(8,128)S(1)} %collective-permute-done.13.refs_3_), channel_id=1, source_target_pairs={{0,1},{1,0},{2,3},{3,2},{4,5},{5,4},{6,7},{7,6},{8,9},{9,8},{10,11... | collective-permute-start | bytes 393224 | tf_op jit(solution)/shard_map/ppermute | solution.py:185
  36.0 1.3 %collective-permute-start.12 = (f32[256,128]{1,0:T(8,128)S(1)}, f32[256,128]{1,0:T(8,128)S(1)}, u32[]{:S(2)}, u32[]{:S(2)}) collective-permute-start(f32[256,128]{1,0:T(8,128)S(1)} %collective-permute-done.11.refs_1_), channel_id=1, source_target_pairs={{0,1},{1,0},{2,3},{3,2},{4,5},{5,4},{6,7},{7,6},{8,9},{9,8},{10,11... | collective-permute-start | bytes 393224 | tf_op jit(solution)/shard_map/ppermute | solution.py:185
  37.8 7.4 %collective-permute-start.21 = (f32[64,128]{1,0:T(8,128)S(1)}, f32[64,128]{1,0:T(8,128)S(1)}, u32[]{:S(2)}, u32[]{:S(2)}) collective-permute-start(f32[64,128]{1,0:T(8,128)S(1)} %shard_map.80._), channel_id=1, source_target_pairs={{0,2},{1,3},{2,0},{3,1},{4,6},{5,7},{6,4},{7,5},{8,10},{9,11},{10,... | collective-permute-start | bytes 98312 | tf_op jit(solution)/shard_map/ppermute | solution.py:185
  39.5 5.6 %collective-permute-start.20 = (f32[64,128]{1,0:T(8,128)S(1)}, f32[64,128]{1,0:T(8,128)S(1)}, u32[]{:S(2)}, u32[]{:S(2)}) collective-permute-start(f32[64,128]{1,0:T(8,128)S(1)} %shard_map.80._), channel_id=1, source_target_pairs={{0,16},{1,17},{2,18},{3,19},{4,20},{5,21},{6,22},{7,23},{8,24},{9,... | collective-permute-start | bytes 98312 | tf_op jit(solution)/shard_map/ppermute | solution.py:185
  40.0 5.1 %collective-permute-start.19 = (f32[64,128]{1,0:T(8,128)S(1)}, f32[64,128]{1,0:T(8,128)S(1)}, u32[]{:S(2)}, u32[]{:S(2)}) collective-permute-start(f32[64,128]{1,0:T(8,128)S(1)} %shard_map.80._), channel_id=1, source_target_pairs={{0,18},{1,19},{2,16},{3,17},{4,22},{5,23},{6,20},{7,21},{8,26},{9,... | collective-permute-start | bytes 98312 | tf_op jit(solution)/shard_map/ppermute | solution.py:185
  41.3 12.3 %copy-start.3 = (f32[64,128]{1,0:T(8,128)S(1)}, f32[64,128]{1,0:T(8,128)}, u32[]{:S(2)}) copy-start(f32[64,128]{1,0:T(8,128)} %param.11) | copy-start | bytes 98308
  42.6 10.3 %collective-permute-start.18 = (f32[256,128]{1,0:T(8,128)S(1)}, f32[256,128]{1,0:T(8,128)S(1)}, u32[]{:S(2)}, u32[]{:S(2)}) collective-permute-start(f32[256,128]{1,0:T(8,128)S(1)} %get-tuple-element.35), channel_id=1, source_target_pairs={{0,8},{1,9},{2,10},{3,11},{4,12},{5,13},{6,14},{7,15},{8,0},{9,1},... | collective-permute-start | bytes 393224 | tf_op jit(solution)/shard_map/ppermute | solution.py:185
  45.2 5.9 %collective-permute-start.22 = (f32[64,128]{1,0:T(8,128)S(1)}, f32[64,128]{1,0:T(8,128)S(1)}, u32[]{:S(2)}, u32[]{:S(2)}) collective-permute-start(f32[64,128]{1,0:T(8,128)S(1)} %add_add_fusion), channel_id=1, source_target_pairs={{0,12},{1,13},{2,14},{3,15},{4,8},{5,9},{6,10},{7,11},{8,4},{9,5},... | collective-permute-start | bytes 98312 | tf_op jit(solution)/shard_map/ppermute | solution.py:185
  48.5 5.1 %collective-permute-start.24 = (f32[64,128]{1,0:T(8,128)S(1)}, f32[64,128]{1,0:T(8,128)S(1)}, u32[]{:S(2)}, u32[]{:S(2)}) collective-permute-start(f32[64,128]{1,0:T(8,128)S(1)} %add_add_fusion), channel_id=1, source_target_pairs={{0,4},{1,5},{2,6},{3,7},{4,0},{5,1},{6,2},{7,3},{8,12},{9,13},{10,... | collective-permute-start | bytes 98312 | tf_op jit(solution)/shard_map/ppermute | solution.py:185
  48.5 5.1 %collective-permute-start.23 = (f32[64,128]{1,0:T(8,128)S(1)}, f32[64,128]{1,0:T(8,128)S(1)}, u32[]{:S(2)}, u32[]{:S(2)}) collective-permute-start(f32[64,128]{1,0:T(8,128)S(1)} %add_add_fusion), channel_id=1, source_target_pairs={{0,8},{1,9},{2,10},{3,11},{4,12},{5,13},{6,14},{7,15},{8,0},{9,1},... | collective-permute-start | bytes 98312 | tf_op jit(solution)/shard_map/ppermute | solution.py:185

commit v4 on v3

--- a/solution.py
+++ b/solution.py
@@ -11,7 +11,8 @@
 AXES = ("tm", "blk")
 HIGH = lax.Precision.HIGH
 VMEM_LIMIT = 16 << 20
-ORDER = (7, 6, 5, 4, 3, 2, 1, 0)
+EARLY = (0, 1, 2, 3, 4, 5, 6)
+LATE = (7,)
 CHUNK = 32
 ROWS = 256
 
@@ -98,71 +99,102 @@
     )(where, pltpu.with_memory_space_constraint(tile, pltpu.HBM), *rows, *values)
 
 
-def product_kernel(count, sign, upper, lower, _, *refs):
-    parts, rest = refs[:count], refs[count:]
-    columns = rest[-1]
-    outs = rest[:-1]
-    high_count = len(outs) if sign > 0 else len(outs) // 2
-    bases = outs[: len(outs) - high_count]
-    outs = outs[len(outs) - high_count :]
+def product_kernel(members, sign, blocks, height, chained, *refs):
+    upper, lower, sums, swapped, _, *refs = refs
+    count = blocks + (1 if height else 0)
+    columns, outs, refs = refs[-1], refs[-1 - count : -1], refs[: -1 - count]
+    parts, bases = refs[: len(members)], refs[len(members) :]
     piece, width = parts[0].shape
-    for j, part in zip(ORDER, parts):
-        at = pl.ds(j * piece, piece)
+    depth = len(members) * piece
+    for k, part in enumerate(parts):
+        at = pl.ds(k * piece, piece)
         columns[at, :width], columns[at, width:] = split(part[...])
-    for e, out in enumerate(outs):
-        for r in range(0, piece, ROWS):
-            at, to = pl.ds(e * piece + r, ROWS), pl.ds(r, ROWS)
-            both = jnp.dot(upper[at], columns[...], preferred_element_type=jnp.float32)
-            more = jnp.dot(lower[at], columns[:, :width], preferred_element_type=jnp.float32)
-            total = both[:, :width] + both[:, width:] + more
-            out[to] = total if sign > 0 else bases[e][to] - total
-
-
-def tile_product(halves, parts, bases=None):
-    rows, cols = halves[0].shape
+
+    def product(upper, lower):
+        both = jnp.dot(upper, columns[...], preferred_element_type=jnp.float32)
+        more = jnp.dot(lower, columns[:, :width], preferred_element_type=jnp.float32)
+        return sign * (both[:, :width] + both[:, width:] + more)
+
+    first = members[0] * piece
+    if height:
+        weights = [
+            sums[:, pl.ds(j * piece, piece)] + swapped[:, pl.ds((j ^ 1) * piece, piece)]
+            for j in members
+        ]
+        total = product(*split(jnp.concatenate(weights, axis=1)))
+        if len(bases) > blocks:
+            total = total + bases[blocks][...]
+        else:
+            at = pl.ds(GROUP * piece, width)
+            total = total + sums[:, at] + swapped[:, at]
+        outs[blocks][...] = total
+    for e in range(blocks):
+        at = (pl.ds(e * piece, piece), pl.ds(first, depth))
+        total = product(upper[at], lower[at])
+        outs[e][...] = bases[e][...] + total if chained else total
+
+
+def tile_product(tile, members, parts, sign=1.0, bases=(), terms=None, rows=True):
+    upper, lower, mark, *sums = tile
+    cols = upper.shape[1]
     piece, width = parts[0].shape
-    high_count = rows // piece
+    blocks = upper.shape[0] // piece if rows else 0
     block = jax.ShapeDtypeStruct((piece, width), jnp.float32)
+    height = sums[0].shape[0] if terms is not None else 0
+    outs = [block] * blocks
+    if height:
+        outs.append(jax.ShapeDtypeStruct((height, width), jnp.float32))
     in_vmem = pl.BlockSpec(memory_space=pltpu.VMEM)
-    operands = [*halves, *(parts[j] for j in ORDER), *(bases or [])]
+    operands = [upper, lower, *(sums if height else [mark, mark]), mark]
+    operands += [parts[j] for j in members]
+    operands += [*(bases if rows else ()), *(terms or ())]
+    depth = len(members) * piece
     return pl.pallas_call(
-        functools.partial(product_kernel, len(parts), 1 if bases is None else -1),
-        out_shape=[block] * high_count,
+        functools.partial(product_kernel, members, sign, blocks, height, bool(bases)),
+        out_shape=outs,
         in_specs=[in_vmem] * len(operands),
-        out_specs=[in_vmem] * high_count,
-        scratch_shapes=[pltpu.VMEM((cols, 2 * width), jnp.bfloat16)],
+        out_specs=[in_vmem] * len(outs),
+        scratch_shapes=[pltpu.VMEM((depth, 2 * width), jnp.bfloat16)],
         cost_estimate=pl.CostEstimate(
-            flops=6 * rows * cols * width, bytes_accessed=4 * rows * cols, transcendentals=0
+            flops=6 * (blocks * piece + height) * depth * width,
+            bytes_accessed=4 * (blocks * piece + height) * depth,
+            transcendentals=0,
         ),
         compiler_params=pltpu.CompilerParams(vmem_limit_bytes=VMEM_LIMIT),
     )(*operands)
 
 
-def terms_kernel(sums, swapped, _, *refs):
-    *parts, out = refs
-    piece = parts[0].shape[0]
-    at = pl.ds(GROUP * piece, out.shape[1])
-    total = sums[:, at] + swapped[:, at]
-    for j, part in zip(ORDER, parts):
-        weights = sums[:, pl.ds(j * piece, piece)] + swapped[:, pl.ds((j ^ 1) * piece, piece)]
-        total = total - three_passes(jnp.concatenate(split(weights), axis=0), *split(part[...]))
-    out[...] = total
-
-
-def terms_product(sums, swapped, mark, parts):
+def finish_kernel(count, tip_inv, tip_rhs, *refs):
+    terms, (own, *others, solved, tip, solved_found, tip_found, sent) = refs[:count], refs[count:]
+    total = own[...]
+    for other in others:
+        total = total + other[...]
+    solved_found[...] = total
+    first = pltpu.make_async_copy(solved_found, solved, sent.at[0])
+    first.start()
+    reduced = tip_rhs[...]
+    for term in terms:
+        reduced = reduced - term[...]
+    stacked = jnp.concatenate(split(tip_inv[...]), axis=0)
+    tip_found[...] = three_passes(stacked, *split(reduced))
+    second = pltpu.make_async_copy(tip_found, tip, sent.at[1])
+    second.start()
+    first.wait()
+    second.wait()
+
+
+def finish(tip_inv, tip_rhs, terms, blocks):
     in_vmem = pl.BlockSpec(memory_space=pltpu.VMEM)
-    height, cols = sums.shape
-    width = parts[0].shape[1]
+    shapes = [blocks[0].shape, tip_rhs.shape]
     return pl.pallas_call(
-        terms_kernel,
-        out_shape=jax.ShapeDtypeStruct((height, width), jnp.float32),
-        in_specs=[in_vmem] * (len(parts) + 3),
-        out_specs=in_vmem,
-        cost_estimate=pl.CostEstimate(
-            flops=6 * height * cols * width, bytes_accessed=8 * height * cols, transcendentals=0
-        ),
+        functools.partial(finish_kernel, len(terms)),
+        out_shape=[jax.ShapeDtypeStruct(shape, jnp.float32) for shape in shapes],
+        in_specs=[in_vmem] * (2 + len(terms) + len(blocks)),
+        out_specs=[pl.BlockSpec(memory_space=pltpu.HBM)] * 2,
+        scratch_shapes=[pltpu.VMEM(shape, jnp.float32) for shape in shapes]
+        + [pltpu.SemaphoreType.DMA((2,))],
         compiler_params=pltpu.CompilerParams(vmem_limit_bytes=VMEM_LIMIT),
-    )(sums, swapped, mark, *(parts[j] for j in ORDER))
+    )(tip_inv, tip_rhs, *terms, *blocks)
 
 
 def on_device(propagator, inv_diag, rhs, arrow, tip_inv, tip_rhs):
@@ -214,22 +246,29 @@
         cols = [lax.dynamic_slice_in_dim(tile, (low ^ j) * piece, piece, 1) for j in range(GROUP)]
         return jnp.concatenate(cols, axis=1)
 
-    def apply_tile(tile, mark, parts, bases=None):
+    def apply_tile(tile, mark, parts, sign=1.0, bases=(), sums=()):
         if by_kernel:
-            return tile_product([*tile, mark], parts, bases)
-        total = dot(in_order(tile), jnp.concatenate(parts, axis=0))
+            tile = [*tile, mark, *sums]
+            if not sums:
+                found = tile_product(tile, EARLY, parts, sign, bases)
+                return tile_product(tile, LATE, parts, sign, found)
+            *found, terms = tile_product(tile, EARLY, parts, sign, bases, ())
+            (terms,) = tile_product(tile, LATE, parts, sign, (), (terms,), False)
+            tile[2] = terms
+            return [*tile_product(tile, LATE, parts, sign, found), terms]
+        columns = jnp.concatenate(parts, axis=0)
+        total = sign * dot(in_order(tile), columns)
         found = [total[e * piece : (e + 1) * piece] for e in range(high_count)]
-        return found if bases is None else [b - f for b, f in zip(bases, found)]
-
-    def subtract_product(sums, swapped, mark, parts):
-        if by_kernel:
-            return terms_product(sums, swapped, mark, parts)
-        total = sums[:, GROUP * piece :] + swapped[:, GROUP * piece :]
-        for j, part in enumerate(parts):
-            k = j ^ 1
-            weights = sums[:, j * piece : (j + 1) * piece] + swapped[:, k * piece : (k + 1) * piece]
-            total = total - dot(weights, part)
-        return total
+        found = [b + f for b, f in zip(bases, found)] if bases else found
+        if sums:
+            weights, swapped = sums
+            terms = weights[:, GROUP * piece :] + swapped[:, GROUP * piece :]
+            for j, part in enumerate(parts):
+                k = j ^ 1
+                weight = weights[:, j * piece : (j + 1) * piece]
+                terms = terms + sign * dot(weight + swapped[:, k * piece : (k + 1) * piece], part)
+            found.append(terms)
+        return found
 
     def tip_rounds():
         bits = [1 << k for k in range(1, blocks.bit_length() - 1)]
@@ -241,13 +280,14 @@
             rounds.append([(0, ahead) for ahead in range(1, steps)])
         for k in range(0, len(bits), 2):
             a, *b = bits[k : k + 2]
-            rounds.append([(a, 0)] + [(f, 0) for f in b] + [(a | f, 0) for f in b])
+            rounds.insert(0, [(a, 0)] + [(f, 0) for f in b] + [(a | f, 0) for f in b])
         return rounds
 
     sent = scatter(rhs[0])
     arrows = [arrow[0]] + [move(arrow[0], e * GROUP) for e in range(1, high_count)]
     tile, mark, _ = prepared(inv_diag[0])
-    sent[0], mark, *arrows[1:] = tie(sent[0], mark, *arrows[1:])
+    sent[0], *arrows[1:] = tie(sent[0], *arrows[1:])
+    sent[1], mark = tie(sent[1], mark)
     mine = mark
     partial = apply_tile(tile, mark, swap(rhs[0], sent))
     if steps == 1:
@@ -263,18 +303,24 @@
             tile, mark, _ = prepared(propagator[0])
         earlier = jnp.where(mine[t : t + 1] > 0.0, sum(arriving), 0.0)
         parts = swap(earlier, scatter(earlier))
-        if t == steps - 2:
-            terms = mark = subtract_product(sums, swapped, mark, parts)
-        partial = apply_tile(tile, mark, parts, partial)
+        if t < steps - 2:
+            partial = apply_tile(tile, mark, parts, -1.0, partial)
+        else:
+            *partial, terms = apply_tile(tile, mark, parts, -1.0, partial, (sums, swapped))
 
     others = [move(partial[e], e * GROUP) for e in range(1, high_count)]
+    terms = [terms]
     for k, moves in enumerate(tip_rounds()):
-        around = [move(terms, flip, ahead) for flip, ahead in reversed(moves)]
+        total = sum(terms[1:], terms[0])
+        around = [move(total, flip, ahead) for flip, ahead in reversed(moves)]
         if k == 1:
             *others, around[0] = tie(*others, around[0])
-        terms = terms + sum(around)
-    solved = partial[0] + sum(others)
-    tip = dot(tip_inv, tip_rhs - terms)
+        terms = [total, *around]
+    if by_kernel:
+        solved, tip = finish(tip_inv, tip_rhs, terms, [partial[0], *others])
+    else:
+        solved = partial[0] + sum(others)
+        tip = dot(tip_inv, tip_rhs - sum(terms))
     return solved[None], tip
 
 

time: 54.6 us -> 52.6 us (0.963)
  starting transfers between devices: 26.8 us -> 25.2 us
  Pallas kernels: 10.7 us -> 11.9 us
  matrix products: 0.77 us -> 0 us
  other arithmetic: 0.79 us -> 0.11 us
    ppermute x25, starting transfers between devices: 26.8 us -> 25.2 us  [move(): return lax.ppermute(value, AXES, route)]
    pallas_call x3 -> x6, Pallas kernels: 3.02 us -> 4.24 us  [the longest x5 3.47 us: tile_product(): pl.pallas_call(functools.partial(product_kernel, members, sign, blocks, h...]
    dot_general x1 -> x0, matrix products: 0.77 us -> none  [dot(): return jnp.dot(a, b, precision=HIGH, preferred_element_type=jnp.float32)]
    broadcast_in_dim x1 -> x0, other arithmetic: 0.67 us -> none  [on_device(): return (solved[None], tip)]
  transfers between devices with their start and end apart: 25 -> 25, of which waited for: 13 -> 14; matrix products, arithmetic and copies ran while one was open for 1% -> 0% of each run, Pallas kernels for 16% -> 20%
where the time goes in v4:
time: 52.6 us; the launch traced here: 52.5 us
  starting transfers between devices  25.2 us (48%)
  waiting for transfers between devices  14.5 us (28%)
  Pallas kernels  11.9 us (23%)
  between operations  0.77 us (1%)
    ppermute x25, starting transfers between devices, move(): return lax.ppermute(value, AXES, route)  25.2 us
    ppermute x25, waiting for transfers between devices, move(): return lax.ppermute(value, AXES, route)  14.5 us
    pallas_call x2, Pallas kernels, split_tile(): pl.pallas_call(functools.partial(split_tile_kernel, piece), out_shape=[ha...  7.66 us
    pallas_call x5, Pallas kernels, tile_product(): pl.pallas_call(functools.partial(product_kernel, members, sign, blocks, h...  3.47 us
  transfers between devices with their start and end apart: 25, of which 14 were waited for; matrix products, arithmetic and copies ran while one was open for 0% of the time, Pallas kernels for 20%

profile of v4, /device:TPU:0, one launch (start us, length us, event | category | flops | bytes accessed | tf_op | source)
XLA Modules:
  0.0 52.5 jit_solution(5450171527147380910)
XLA Ops:
  0.6 3.1 %collective-permute-start.2 = (f32[256,128]{1,0:T(8,128)}, f32[256,128]{1,0:T(8,128)S(1)}, u32[]{:S(2)}, u32[]{:S(2)}) collective-permute-start(f32[256,128]{1,0:T(8,128)} %bitcast.10), channel_id=1, source_target_pairs={{0,4},{1,5},{2,6},{3,7},{4,0},{5,1},{6,2},{7,3},{8,12},{9,13},{10,... | collective-permute-start | bytes 393224 | tf_op jit(solution)/shard_map/ppermute | solution.py:217
  3.7 1.5 %collective-permute-start = (f32[256,128]{1,0:T(8,128)}, f32[256,128]{1,0:T(8,128)S(1)}, u32[]{:S(2)}, u32[]{:S(2)}) collective-permute-start(f32[256,128]{1,0:T(8,128)} %bitcast.11), channel_id=1, source_target_pairs={{0,2},{1,3},{2,0},{3,1},{4,6},{5,7},{6,4},{7,5},{8,10},{9,11},{10,... | collective-permute-start | bytes 393224 | tf_op jit(solution)/shard_map/ppermute | solution.py:217
  5.2 0.1 collective-permute-start.3
  5.3 0.0 collective-permute-start.5
  5.3 3.0 %collective-permute-start.1 = (f32[64,256]{1,0:T(8,128)}, f32[64,256]{1,0:T(8,128)S(1)}, u32[]{:S(2)}, u32[]{:S(2)}) collective-permute-start(f32[64,256]{1,0:T(8,128)} %bitcast.15), channel_id=1, source_target_pairs={{0,8},{1,9},{2,10},{3,11},{4,12},{5,13},{6,14},{7,15},{8,0},{9,1},... | collective-permute-start | bytes 196616 | tf_op jit(solution)/shard_map/ppermute | solution.py:217
  8.2 0.1 pad_add_fusion.where
  8.3 3.4 %shard_map.77 = (bf16[512,2048]{1,0:T(8,128)(2,1)S(1)}, bf16[512,2048]{1,0:T(8,128)(2,1)S(1)}, f32[8,128]{1,0:T(8,128)S(1)}, f32[8,128]{1,0:T(8,128)}) custom-call(s32[3]{0:T(128)S(1)} %pad_add_fusion.where, f32[512,2048]{1,0:T(8,128)} %bitcast.18), custom_call_target="tpu_custom_call" | custom-call | flops 8388608 | bytes 8388608 | tf_op jit(solution)/shard_map/pallas_call | solution.py:85
  11.8 0.0 collective-permute-done.2.refs_9_
  11.8 0.3 collective-permute-start.7
  12.1 0.0 collective-permute-done.1.refs_1_
  12.1 0.0 collective-permute-done.refs_7_
  12.1 0.3 collective-permute-start.6
  12.3 0.4 collective-permute-done.3.refs_11_
  12.8 0.0 collective-permute-start.4
  12.8 0.0 collective-permute-done.5.refs_6_
  12.8 0.4 collective-permute-done.7.refs_10_
  13.2 0.2 collective-permute-done.6.refs_8_
  13.4 0.0 copy-done
  13.4 1.2 %shard_map.78 = (f32[256,128]{1,0:T(8,128)S(1)}, f32[256,128]{1,0:T(8,128)S(1)}) custom-call(bf16[512,2048]{1,0:T(8,128)(2,1)S(1)} %get-tuple-element.29.refs_0_, bf16[512,2048]{1,0:T(8,128)(2,1)S(1)} %get-tuple-element.30.refs_1_, f32[8,128]{1,0:T(8,128)S(1)} %get-tuple-element.32.refs_2_.refs_3_.refs_4_, ...), custom_call_target="tpu_custom_call" | custom-call | flops 704643072 | bytes 3670016 | tf_op jit(solution)/shard_map/pallas_call | solution.py:152
  14.6 0.0 collective-permute-done.4.refs_5_
  14.6 0.0 copy-start.1
  14.6 0.3 shard_map.79
  14.9 3.4 %collective-permute-start.9 = (f32[256,128]{1,0:T(8,128)S(1)}, f32[256,128]{1,0:T(8,128)S(1)}, u32[]{:S(2)}, u32[]{:S(2)}) collective-permute-start(f32[256,128]{1,0:T(8,128)S(1)} %get-tuple-element.38.refs_3_.refs_13_), channel_id=1, source_target_pairs={{0,24},{1,25},{2,26},{3,27},{4,28},{5,29},{6,30},{7,31},{8,16},{9,... | collective-permute-start | bytes 393224 | tf_op jit(solution)/shard_map/ppermute | solution.py:217
  18.3 0.5 collective-permute-start.10
  18.8 0.0 copy-done.1
  18.8 4.2 %shard_map.80 = (bf16[512,2048]{1,0:T(8,128)(2,1)S(1)}, bf16[512,2048]{1,0:T(8,128)(2,1)S(1)}, f32[8,128]{1,0:T(8,128)S(1)}, f32[64,2176]{1,0:T(8,128)S(1)}) custom-call(s32[3]{0:T(128)S(1)} %pad_add_fusion.where, f32[512,2048]{1,0:T(8,128)} %bitcast.17, f32[64,256]{1,0:T(8,128)S(1)} %bitcast.16, f32[64,256]{1,0:T(8,128)S(1)} %collective-permute-done.1.refs_1_, ...), custom_call_target="tpu_custom_call" | custom-call | flops 8388608 | bytes 8388608 | tf_op jit(solution)/shard_map/pallas_call | solution.py:85
  23.0 0.1 collective-permute-start.8
  23.1 2.2 %collective-permute-done.9 = f32[256,128]{1,0:T(8,128)S(1)} collective-permute-done((f32[256,128]{1,0:T(8,128)S(1)}, f32[256,128]{1,0:T(8,128)S(1)}, u32[]{:S(2)}, u32[]{:S(2)}) %collective-permute-start.9) | collective-permute-done | bytes 131104 | tf_op jit(solution)/shard_map/ppermute | solution.py:217
  25.3 0.0 collective-permute-done.10
  25.3 1.6 %collective-permute-start.14 = (f32[256,128]{1,0:T(8,128)S(1)}, f32[256,128]{1,0:T(8,128)S(1)}, u32[]{:S(2)}, u32[]{:S(2)}) collective-permute-start(f32[256,128]{1,0:T(8,128)S(1)} %add_select_fusion.refs_5_), channel_id=1, source_target_pairs={{0,2},{1,3},{2,0},{3,1},{4,6},{5,7},{6,4},{7,5},{8,10},{9,11},{10,... | collective-permute-start | bytes 393224 | tf_op jit(solution)/shard_map/ppermute | solution.py:217
  26.9 2.3 %collective-permute-start.16 = (f32[256,128]{1,0:T(8,128)S(1)}, f32[256,128]{1,0:T(8,128)S(1)}, u32[]{:S(2)}, u32[]{:S(2)}) collective-permute-start(f32[256,128]{1,0:T(8,128)S(1)} %add_select_fusion.refs_5_), channel_id=1, source_target_pairs={{0,4},{1,5},{2,6},{3,7},{4,0},{5,1},{6,2},{7,3},{8,12},{9,13},{10,... | collective-permute-start | bytes 393224 | tf_op jit(solution)/shard_map/ppermute | solution.py:217
  29.2 0.0 collective-permute-start.11
  29.2 0.0 collective-permute-start.13
  29.2 1.1 %collective-permute-done.14.refs_7_ = f32[256,128]{1,0:T(8,128)S(1)} collective-permute-done((f32[256,128]{1,0:T(8,128)S(1)}, f32[256,128]{1,0:T(8,128)S(1)}, u32[]{:S(2)}, u32[]{:S(2)}) %collective-permute-start.14) | collective-permute-done | bytes 131104 | tf_op jit(solution)/shard_map/ppermute | solution.py:217
  30.3 0.0 collective-permute-start.15
  30.4 3.2 %collective-permute-done.16.refs_9_ = f32[256,128]{1,0:T(8,128)S(1)} collective-permute-done((f32[256,128]{1,0:T(8,128)S(1)}, f32[256,128]{1,0:T(8,128)S(1)}, u32[]{:S(2)}, u32[]{:S(2)}) %collective-permute-start.16) | collective-permute-done | bytes 131104 | tf_op jit(solution)/shard_map/ppermute | solution.py:217
  33.5 0.0 collective-permute-start.17
  33.5 1.8 %collective-permute-done.11.refs_11_ = f32[256,128]{1,0:T(8,128)S(1)} collective-permute-done((f32[256,128]{1,0:T(8,128)S(1)}, f32[256,128]{1,0:T(8,128)S(1)}, u32[]{:S(2)}, u32[]{:S(2)}) %collective-permute-start.11) | collective-permute-done | bytes 131104 | tf_op jit(solution)/shard_map/ppermute | solution.py:217
  35.4 0.0 collective-permute-start.12
  35.4 0.0 collective-permute-done.13.refs_6_
  35.4 0.0 collective-permute-done.15.refs_8_
  35.4 0.0 collective-permute-done.17.refs_10_
  35.4 0.0 collective-permute-done.8.refs_3_
  35.4 1.5 %shard_map.81 = (f32[256,128]{1,0:T(8,128)S(1)}, f32[256,128]{1,0:T(8,128)S(1)}, f32[64,128]{1,0:T(8,128)S(1)}) custom-call(bf16[512,2048]{1,0:T(8,128)(2,1)S(1)} %get-tuple-element.39.refs_0_, bf16[512,2048]{1,0:T(8,128)(2,1)S(1)} %get-tuple-element.40.refs_1_, f32[64,2176]{1,0:T(8,128)S(1)} %get-tuple-element.41.refs_2_, ...), custom_call_target="tpu_custom_call" | custom-call | flops 792723456 | bytes 4128768 | tf_op jit(solution)/shard_map/pallas_call | solution.py:152
  36.9 0.0 collective-permute-done.12.refs_5_
  36.9 0.2 shard_map.82.refs_2_.refs_3_.refs_4_
  37.1 2.6 %collective-permute-start.18 = (f32[64,128]{1,0:T(8,128)S(1)}, f32[64,128]{1,0:T(8,128)S(1)}, u32[]{:S(2)}, u32[]{:S(2)}) collective-permute-start(f32[64,128]{1,0:T(8,128)S(1)} %shard_map.82.refs_2_.refs_3_.refs_4_), channel_id=1, source_target_pairs={{0,12},{1,13},{2,14},{3,15},{4,8},{5,9},{6,10},{7,11},{8,4},{9,5},... | collective-permute-start | bytes 98312 | tf_op jit(solution)/shard_map/ppermute | solution.py:217
  39.7 0.7 %collective-permute-start.19 = (f32[64,128]{1,0:T(8,128)S(1)}, f32[64,128]{1,0:T(8,128)S(1)}, u32[]{:S(2)}, u32[]{:S(2)}) collective-permute-start(f32[64,128]{1,0:T(8,128)S(1)} %shard_map.82.refs_2_.refs_3_.refs_4_), channel_id=1, source_target_pairs={{0,8},{1,9},{2,10},{3,11},{4,12},{5,13},{6,14},{7,15},{8,0},{9,1},... | collective-permute-start | bytes 98312 | tf_op jit(solution)/shard_map/ppermute | solution.py:217
  40.4 1.2 %collective-permute-start.20 = (f32[64,128]{1,0:T(8,128)S(1)}, f32[64,128]{1,0:T(8,128)S(1)}, u32[]{:S(2)}, u32[]{:S(2)}) collective-permute-start(f32[64,128]{1,0:T(8,128)S(1)} %shard_map.82.refs_2_.refs_3_.refs_4_), channel_id=1, source_target_pairs={{0,4},{1,5},{2,6},{3,7},{4,0},{5,1},{6,2},{7,3},{8,12},{9,13},{10,... | collective-permute-start | bytes 98312 | tf_op jit(solution)/shard_map/ppermute | solution.py:217
  41.6 0.3 shard_map.83
  41.9 1.1 %collective-permute-start.21 = (f32[256,128]{1,0:T(8,128)S(1)}, f32[256,128]{1,0:T(8,128)S(1)}, u32[]{:S(2)}, u32[]{:S(2)}) collective-permute-start(f32[256,128]{1,0:T(8,128)S(1)} %get-tuple-element.48), channel_id=1, source_target_pairs={{0,8},{1,9},{2,10},{3,11},{4,12},{5,13},{6,14},{7,15},{8,0},{9,1},... | collective-permute-start | bytes 393224 | tf_op jit(solution)/shard_map/ppermute | solution.py:217
  43.0 0.3 collective-permute-done.18
  43.3 1.2 %collective-permute-done.19 = f32[64,128]{1,0:T(8,128)S(1)} collective-permute-done((f32[64,128]{1,0:T(8,128)S(1)}, f32[64,128]{1,0:T(8,128)S(1)}, u32[]{:S(2)}, u32[]{:S(2)}) %collective-permute-start.19) | collective-permute-done | bytes 32800 | tf_op jit(solution)/shard_map/ppermute | solution.py:217
  44.6 0.2 collective-permute-done.20
  44.8 2.5 %collective-permute-start.22 = (f32[64,128]{1,0:T(8,128)S(1)}, f32[64,128]{1,0:T(8,128)S(1)}, u32[]{:S(2)}, u32[]{:S(2)}) collective-permute-start(f32[64,128]{1,0:T(8,128)S(1)} %add_add_fusion.refs_0_), channel_id=1, source_target_pairs={{0,18},{1,19},{2,16},{3,17},{4,22},{5,23},{6,20},{7,21},{8,26},{9,... | collective-permute-start | bytes 98312 | tf_op jit(solution)/shard_map/ppermute | solution.py:217
  47.3 0.5 collective-permute-start.23
  47.8 0.5 %collective-permute-start.24 = (f32[64,128]{1,0:T(8,128)S(1)}, f32[64,128]{1,0:T(8,128)S(1)}, u32[]{:S(2)}, u32[]{:S(2)}) collective-permute-start(f32[64,128]{1,0:T(8,128)S(1)} %add_add_fusion.refs_0_), channel_id=1, source_target_pairs={{0,2},{1,3},{2,0},{3,1},{4,6},{5,7},{6,4},{7,5},{8,10},{9,11},{10,... | collective-permute-start | bytes 98312 | tf_op jit(solution)/shard_map/ppermute | solution.py:217
  48.3 1.3 %collective-permute-done.22.refs_1_ = f32[64,128]{1,0:T(8,128)S(1)} collective-permute-done((f32[64,128]{1,0:T(8,128)S(1)}, f32[64,128]{1,0:T(8,128)S(1)}, u32[]{:S(2)}, u32[]{:S(2)}) %collective-permute-start.22) | collective-permute-done | bytes 32800 | tf_op jit(solution)/shard_map/ppermute | solution.py:217
  49.6 1.1 %collective-permute-done.21.refs_5_ = f32[256,128]{1,0:T(8,128)S(1)} collective-permute-done((f32[256,128]{1,0:T(8,128)S(1)}, f32[256,128]{1,0:T(8,128)S(1)}, u32[]{:S(2)}, u32[]{:S(2)}) %collective-permute-start.21) | collective-permute-done | bytes 131104 | tf_op jit(solution)/shard_map/ppermute | solution.py:217
  50.7 0.5 collective-permute-done.23.refs_2_
  51.2 0.5 collective-permute-done.24.refs_3_
  51.7 0.0 copy-done.2
  51.7 0.0 copy-done.3
  51.7 0.8 %shard_map.84 = (f32[256,128]{1,0:T(8,128)}, f32[64,128]{1,0:T(8,128)}) custom-call(f32[64,64]{1,0:T(8,128)S(1)} %copy-done.2, f32[64,128]{1,0:T(8,128)S(1)} %copy-done.3, f32[64,128]{1,0:T(8,128)S(1)} %add_add_fusion.refs_0_, f32[64,128]{1,0:T(8,128)S(1)} %collective-permute-done.22.refs_1_, f32[64,128]{1,0:T(8,128)S(1)} %collective-permute-done.23.refs_2_, ...), custom_call_target="tpu_custom_call" | custom-call | tf_op jit(solution)/shard_map/pallas_call | solution.py:189
  (6 shorter events, 0.0 us)
Async XLA Ops:
  0.6 11.1 %collective-permute-start.2 = (f32[256,128]{1,0:T(8,128)}, f32[256,128]{1,0:T(8,128)S(1)}, u32[]{:S(2)}, u32[]{:S(2)}) collective-permute-start(f32[256,128]{1,0:T(8,128)} %bitcast.10), channel_id=1, source_target_pairs={{0,4},{1,5},{2,6},{3,7},{4,0},{5,1},{6,2},{7,3},{8,12},{9,13},{10,... | collective-permute-start | bytes 393224 | tf_op jit(solution)/shard_map/ppermute | solution.py:217
  3.7 8.3 %collective-permute-start = (f32[256,128]{1,0:T(8,128)}, f32[256,128]{1,0:T(8,128)S(1)}, u32[]{:S(2)}, u32[]{:S(2)}) collective-permute-start(f32[256,128]{1,0:T(8,128)} %bitcast.11), channel_id=1, source_target_pairs={{0,2},{1,3},{2,0},{3,1},{4,6},{5,7},{6,4},{7,5},{8,10},{9,11},{10,... | collective-permute-start | bytes 393224 | tf_op jit(solution)/shard_map/ppermute | solution.py:217
  5.2 7.6 %collective-permute-start.3 = (f32[256,128]{1,0:T(8,128)}, f32[256,128]{1,0:T(8,128)S(1)}, u32[]{:S(2)}, u32[]{:S(2)}) collective-permute-start(f32[256,128]{1,0:T(8,128)} %bitcast.12), channel_id=1, source_target_pairs={{0,6},{1,7},{2,4},{3,5},{4,2},{5,3},{6,0},{7,1},{8,14},{9,15},{10,... | collective-permute-start | bytes 393224 | tf_op jit(solution)/shard_map/ppermute | solution.py:217
  5.3 7.5 %collective-permute-start.5 = (f32[256,128]{1,0:T(8,128)}, f32[256,128]{1,0:T(8,128)S(1)}, u32[]{:S(2)}, u32[]{:S(2)}) collective-permute-start(f32[256,128]{1,0:T(8,128)} %bitcast.13), channel_id=1, source_target_pairs={{0,1},{1,0},{2,3},{3,2},{4,5},{5,4},{6,7},{7,6},{8,9},{9,8},{10,11... | collective-permute-start | bytes 393224 | tf_op jit(solution)/shard_map/ppermute | solution.py:217
  5.3 6.8 %collective-permute-start.1 = (f32[64,256]{1,0:T(8,128)}, f32[64,256]{1,0:T(8,128)S(1)}, u32[]{:S(2)}, u32[]{:S(2)}) collective-permute-start(f32[64,256]{1,0:T(8,128)} %bitcast.15), channel_id=1, source_target_pairs={{0,8},{1,9},{2,10},{3,11},{4,12},{5,13},{6,14},{7,15},{8,0},{9,1},... | collective-permute-start | bytes 196616 | tf_op jit(solution)/shard_map/ppermute | solution.py:217
  8.3 5.1 %copy-start = (f32[1,256,128]{2,1,0:T(8,128)S(1)}, f32[1,256,128]{2,1,0:T(8,128)}, u32[]{:S(2)}) copy-start(f32[1,256,128]{2,1,0:T(8,128)} %param.8) | copy-start | bytes 393220
  11.8 1.4 %collective-permute-start.7 = (f32[256,128]{1,0:T(8,128)S(1)}, f32[256,128]{1,0:T(8,128)S(1)}, u32[]{:S(2)}, u32[]{:S(2)}) collective-permute-start(f32[256,128]{1,0:T(8,128)S(1)} %collective-permute-done.2.refs_9_), channel_id=1, source_target_pairs={{0,1},{1,0},{2,3},{3,2},{4,5},{5,4},{6,7},{7,6},{8,9},{9,8},{10,11... | collective-permute-start | bytes 393224 | tf_op jit(solution)/shard_map/ppermute | solution.py:217
  12.1 1.4 %collective-permute-start.6 = (f32[256,128]{1,0:T(8,128)S(1)}, f32[256,128]{1,0:T(8,128)S(1)}, u32[]{:S(2)}, u32[]{:S(2)}) collective-permute-start(f32[256,128]{1,0:T(8,128)S(1)} %collective-permute-done.refs_7_), channel_id=1, source_target_pairs={{0,1},{1,0},{2,3},{3,2},{4,5},{5,4},{6,7},{7,6},{8,9},{9,8},{10,11... | collective-permute-start | bytes 393224 | tf_op jit(solution)/shard_map/ppermute | solution.py:217
  12.8 1.8 %collective-permute-start.4 = (f32[256,128]{1,0:T(8,128)S(1)}, f32[256,128]{1,0:T(8,128)S(1)}, u32[]{:S(2)}, u32[]{:S(2)}) collective-permute-start(f32[256,128]{1,0:T(8,128)S(1)} %collective-permute-done.3.refs_11_), channel_id=1, source_target_pairs={{0,1},{1,0},{2,3},{3,2},{4,5},{5,4},{6,7},{7,6},{8,9},{9,8},{10,11... | collective-permute-start | bytes 393224 | tf_op jit(solution)/shard_map/ppermute | solution.py:217
  14.6 4.2 %copy-start.1 = (f32[1,64,256]{2,1,0:T(8,128)S(1)}, f32[1,64,256]{2,1,0:T(8,128)}, u32[]{:S(2)}) copy-start(f32[1,64,256]{2,1,0:T(8,128)} %param.9) | copy-start | bytes 196612
  14.9 10.4 %collective-permute-start.9 = (f32[256,128]{1,0:T(8,128)S(1)}, f32[256,128]{1,0:T(8,128)S(1)}, u32[]{:S(2)}, u32[]{:S(2)}) collective-permute-start(f32[256,128]{1,0:T(8,128)S(1)} %get-tuple-element.38.refs_3_.refs_13_), channel_id=1, source_target_pairs={{0,24},{1,25},{2,26},{3,27},{4,28},{5,29},{6,30},{7,31},{8,16},{9,... | collective-permute-start | bytes 393224 | tf_op jit(solution)/shard_map/ppermute | solution.py:217
  18.3 7.0 %collective-permute-start.10 = (f32[256,128]{1,0:T(8,128)S(1)}, f32[256,128]{1,0:T(8,128)S(1)}, u32[]{:S(2)}, u32[]{:S(2)}) collective-permute-start(f32[256,128]{1,0:T(8,128)S(1)} %get-tuple-element.37.refs_2_.refs_12_), channel_id=1, source_target_pairs={{0,16},{1,17},{2,18},{3,19},{4,20},{5,21},{6,22},{7,23},{8,24},{9,... | collective-permute-start | bytes 393224 | tf_op jit(solution)/shard_map/ppermute | solution.py:217
  23.0 12.4 %collective-permute-start.8 = (f32[64,2176]{1,0:T(8,128)S(1)}, f32[64,2176]{1,0:T(8,128)S(1)}, u32[]{:S(2)}, u32[]{:S(2)}) collective-permute-start(f32[64,2176]{1,0:T(8,128)S(1)} %get-tuple-element.41.refs_2_), channel_id=1, source_target_pairs={{0,1},{1,0},{2,3},{3,2},{4,5},{5,4},{6,7},{7,6},{8,9},{9,8},{10,11... | collective-permute-start | bytes 1671176 | tf_op jit(solution)/shard_map/ppermute | solution.py:217
  25.3 5.0 %collective-permute-start.14 = (f32[256,128]{1,0:T(8,128)S(1)}, f32[256,128]{1,0:T(8,128)S(1)}, u32[]{:S(2)}, u32[]{:S(2)}) collective-permute-start(f32[256,128]{1,0:T(8,128)S(1)} %add_select_fusion.refs_5_), channel_id=1, source_target_pairs={{0,2},{1,3},{2,0},{3,1},{4,6},{5,7},{6,4},{7,5},{8,10},{9,11},{10,... | collective-permute-start | bytes 393224 | tf_op jit(solution)/shard_map/ppermute | solution.py:217
  26.9 6.7 %collective-permute-start.16 = (f32[256,128]{1,0:T(8,128)S(1)}, f32[256,128]{1,0:T(8,128)S(1)}, u32[]{:S(2)}, u32[]{:S(2)}) collective-permute-start(f32[256,128]{1,0:T(8,128)S(1)} %add_select_fusion.refs_5_), channel_id=1, source_target_pairs={{0,4},{1,5},{2,6},{3,7},{4,0},{5,1},{6,2},{7,3},{8,12},{9,13},{10,... | collective-permute-start | bytes 393224 | tf_op jit(solution)/shard_map/ppermute | solution.py:217
  29.2 6.2 %collective-permute-start.11 = (f32[256,128]{1,0:T(8,128)S(1)}, f32[256,128]{1,0:T(8,128)S(1)}, u32[]{:S(2)}, u32[]{:S(2)}) collective-permute-start(f32[256,128]{1,0:T(8,128)S(1)} %add_select_fusion.refs_5_), channel_id=1, source_target_pairs={{0,6},{1,7},{2,4},{3,5},{4,2},{5,3},{6,0},{7,1},{8,14},{9,15},{10,... | collective-permute-start | bytes 393224 | tf_op jit(solution)/shard_map/ppermute | solution.py:217
  29.2 6.2 %collective-permute-start.13 = (f32[256,128]{1,0:T(8,128)S(1)}, f32[256,128]{1,0:T(8,128)S(1)}, u32[]{:S(2)}, u32[]{:S(2)}) collective-permute-start(f32[256,128]{1,0:T(8,128)S(1)} %add_select_fusion.refs_5_), channel_id=1, source_target_pairs={{0,1},{1,0},{2,3},{3,2},{4,5},{5,4},{6,7},{7,6},{8,9},{9,8},{10,11... | collective-permute-start | bytes 393224 | tf_op jit(solution)/shard_map/ppermute | solution.py:217
  30.3 5.0 %collective-permute-start.15 = (f32[256,128]{1,0:T(8,128)S(1)}, f32[256,128]{1,0:T(8,128)S(1)}, u32[]{:S(2)}, u32[]{:S(2)}) collective-permute-start(f32[256,128]{1,0:T(8,128)S(1)} %collective-permute-done.14.refs_7_), channel_id=1, source_target_pairs={{0,1},{1,0},{2,3},{3,2},{4,5},{5,4},{6,7},{7,6},{8,9},{9,8},{10,11... | collective-permute-start | bytes 393224 | tf_op jit(solution)/shard_map/ppermute | solution.py:217
  33.5 1.9 %collective-permute-start.17 = (f32[256,128]{1,0:T(8,128)S(1)}, f32[256,128]{1,0:T(8,128)S(1)}, u32[]{:S(2)}, u32[]{:S(2)}) collective-permute-start(f32[256,128]{1,0:T(8,128)S(1)} %collective-permute-done.16.refs_9_), channel_id=1, source_target_pairs={{0,1},{1,0},{2,3},{3,2},{4,5},{5,4},{6,7},{7,6},{8,9},{9,8},{10,11... | collective-permute-start | bytes 393224 | tf_op jit(solution)/shard_map/ppermute | solution.py:217
  35.4 1.5 %collective-permute-start.12 = (f32[256,128]{1,0:T(8,128)S(1)}, f32[256,128]{1,0:T(8,128)S(1)}, u32[]{:S(2)}, u32[]{:S(2)}) collective-permute-start(f32[256,128]{1,0:T(8,128)S(1)} %collective-permute-done.11.refs_11_), channel_id=1, source_target_pairs={{0,1},{1,0},{2,3},{3,2},{4,5},{5,4},{6,7},{7,6},{8,9},{9,8},{10,11... | collective-permute-start | bytes 393224 | tf_op jit(solution)/shard_map/ppermute | solution.py:217
  37.1 6.2 %collective-permute-start.18 = (f32[64,128]{1,0:T(8,128)S(1)}, f32[64,128]{1,0:T(8,128)S(1)}, u32[]{:S(2)}, u32[]{:S(2)}) collective-permute-start(f32[64,128]{1,0:T(8,128)S(1)} %shard_map.82.refs_2_.refs_3_.refs_4_), channel_id=1, source_target_pairs={{0,12},{1,13},{2,14},{3,15},{4,8},{5,9},{6,10},{7,11},{8,4},{9,5},... | collective-permute-start | bytes 98312 | tf_op jit(solution)/shard_map/ppermute | solution.py:217
  39.7 4.9 %collective-permute-start.19 = (f32[64,128]{1,0:T(8,128)S(1)}, f32[64,128]{1,0:T(8,128)S(1)}, u32[]{:S(2)}, u32[]{:S(2)}) collective-permute-start(f32[64,128]{1,0:T(8,128)S(1)} %shard_map.82.refs_2_.refs_3_.refs_4_), channel_id=1, source_target_pairs={{0,8},{1,9},{2,10},{3,11},{4,12},{5,13},{6,14},{7,15},{8,0},{9,1},... | collective-permute-start | bytes 98312 | tf_op jit(solution)/shard_map/ppermute | solution.py:217
  40.4 4.3 %collective-permute-start.20 = (f32[64,128]{1,0:T(8,128)S(1)}, f32[64,128]{1,0:T(8,128)S(1)}, u32[]{:S(2)}, u32[]{:S(2)}) collective-permute-start(f32[64,128]{1,0:T(8,128)S(1)} %shard_map.82.refs_2_.refs_3_.refs_4_), channel_id=1, source_target_pairs={{0,4},{1,5},{2,6},{3,7},{4,0},{5,1},{6,2},{7,3},{8,12},{9,13},{10,... | collective-permute-start | bytes 98312 | tf_op jit(solution)/shard_map/ppermute | solution.py:217
  41.6 10.1 %copy-start.2 = (f32[64,64]{1,0:T(8,128)S(1)}, f32[64,64]{1,0:T(8,128)}, u32[]{:S(2)}) copy-start(f32[64,64]{1,0:T(8,128)} %tip_inv.1) | copy-start | bytes 49156
  41.6 10.1 %copy-start.3 = (f32[64,128]{1,0:T(8,128)S(1)}, f32[64,128]{1,0:T(8,128)}, u32[]{:S(2)}) copy-start(f32[64,128]{1,0:T(8,128)} %tip_rhs.1) | copy-start | bytes 98308
  41.9 8.8 %collective-permute-start.21 = (f32[256,128]{1,0:T(8,128)S(1)}, f32[256,128]{1,0:T(8,128)S(1)}, u32[]{:S(2)}, u32[]{:S(2)}) collective-permute-start(f32[256,128]{1,0:T(8,128)S(1)} %get-tuple-element.48), channel_id=1, source_target_pairs={{0,8},{1,9},{2,10},{3,11},{4,12},{5,13},{6,14},{7,15},{8,0},{9,1},... | collective-permute-start | bytes 393224 | tf_op jit(solution)/shard_map/ppermute | solution.py:217
  44.8 4.9 %collective-permute-start.22 = (f32[64,128]{1,0:T(8,128)S(1)}, f32[64,128]{1,0:T(8,128)S(1)}, u32[]{:S(2)}, u32[]{:S(2)}) collective-permute-start(f32[64,128]{1,0:T(8,128)S(1)} %add_add_fusion.refs_0_), channel_id=1, source_target_pairs={{0,18},{1,19},{2,16},{3,17},{4,22},{5,23},{6,20},{7,21},{8,26},{9,... | collective-permute-start | bytes 98312 | tf_op jit(solution)/shard_map/ppermute | solution.py:217
  47.3 3.9 %collective-permute-start.23 = (f32[64,128]{1,0:T(8,128)S(1)}, f32[64,128]{1,0:T(8,128)S(1)}, u32[]{:S(2)}, u32[]{:S(2)}) collective-permute-start(f32[64,128]{1,0:T(8,128)S(1)} %add_add_fusion.refs_0_), channel_id=1, source_target_pairs={{0,16},{1,17},{2,18},{3,19},{4,20},{5,21},{6,22},{7,23},{8,24},{9,... | collective-permute-start | bytes 98312 | tf_op jit(solution)/shard_map/ppermute | solution.py:217
  47.8 3.9 %collective-permute-start.24 = (f32[64,128]{1,0:T(8,128)S(1)}, f32[64,128]{1,0:T(8,128)S(1)}, u32[]{:S(2)}, u32[]{:S(2)}) collective-permute-start(f32[64,128]{1,0:T(8,128)S(1)} %add_add_fusion.refs_0_), channel_id=1, source_target_pairs={{0,2},{1,3},{2,0},{3,1},{4,6},{5,7},{6,4},{7,5},{8,10},{9,11},{10,... | collective-permute-start | bytes 98312 | tf_op jit(solution)/shard_map/ppermute | solution.py:217

commit v5 on v4

--- a/solution.py
+++ b/solution.py
@@ -12,6 +12,9 @@
 HIGH = lax.Precision.HIGH
 VMEM_LIMIT = 16 << 20
 EARLY = (0, 1, 2, 3, 4, 5, 6)
+PRE = (0, 1)
+REST = (2, 3, 4, 5, 6)
+PRE_TIE = 2
 LATE = (7,)
 CHUNK = 32
 ROWS = 256
@@ -38,8 +41,14 @@
     return both[:height] + both[height:] + more
 
 
-def split_tile_kernel(piece, where, tile, *refs):
+def place():
+    position = lax.axis_index("blk")
+    return lax.rem(position, GROUP), lax.div(position, GROUP), lax.axis_index("tm")
+
+
+def split_tile_kernel(piece, tile, *refs):
     *given, upper, lower, mark, sums, staged, arrived = refs
+    where = place()
     high_count, group = arrived.shape
     rows, values = given[:high_count], given[high_count:]
     blocks = [(e, j) for j in range(group) for e in range(high_count)]
@@ -74,7 +83,7 @@
             sums[to] = sums[to] + total if e else total
 
 
-def split_tile(tile, where, piece, steps, rows=(), values=()):
+def split_tile(tile, piece, steps, rows=(), values=()):
     high_count, group = tile.shape[0] // piece, tile.shape[1] // piece
     half = jax.ShapeDtypeStruct(tile.shape, jnp.bfloat16)
     mark = jax.ShapeDtypeStruct((-(-steps // 8) * 8, 128), jnp.float32)
@@ -85,7 +94,7 @@
     return pl.pallas_call(
         functools.partial(split_tile_kernel, piece),
         out_shape=[half, half, mark, sums],
-        in_specs=[pl.BlockSpec(memory_space=pltpu.SMEM), pl.BlockSpec(memory_space=pltpu.HBM)]
+        in_specs=[pl.BlockSpec(memory_space=pltpu.HBM)]
         + [in_vmem] * (len(rows) + len(values)),
         out_specs=[in_vmem] * 4,
         scratch_shapes=[
@@ -96,7 +105,7 @@
             flops=8 * tile.size, bytes_accessed=8 * tile.size, transcendentals=0
         ),
         compiler_params=pltpu.CompilerParams(vmem_limit_bytes=VMEM_LIMIT),
-    )(where, pltpu.with_memory_space_constraint(tile, pltpu.HBM), *rows, *values)
+    )(pltpu.with_memory_space_constraint(tile, pltpu.HBM), *rows, *values)
 
 
 def product_kernel(members, sign, blocks, height, chained, *refs):
@@ -226,11 +235,10 @@
         return parts
 
     by_kernel = piece % 256 == 0 and width % 128 == 0
-    where = jnp.stack([low, high, step]).astype(jnp.int32)
 
     def prepared(tile, rows=(), values=()):
         if by_kernel:
-            *halves, mark, sums = split_tile(tile, where, piece, steps, rows, values)
+            *halves, mark, sums = split_tile(tile, piece, steps, rows, values)
             return halves, mark, sums
         mark = jnp.where(jnp.arange(steps)[:, None] + 1 == step, 1.0, jnp.zeros((1, width)))
         if not rows:
@@ -246,13 +254,13 @@
         cols = [lax.dynamic_slice_in_dim(tile, (low ^ j) * piece, piece, 1) for j in range(GROUP)]
         return jnp.concatenate(cols, axis=1)
 
-    def apply_tile(tile, mark, parts, sign=1.0, bases=(), sums=()):
+    def apply_tile(tile, mark, parts, sign=1.0, bases=(), sums=(), sums_terms=()):
         if by_kernel:
             tile = [*tile, mark, *sums]
             if not sums:
                 found = tile_product(tile, EARLY, parts, sign, bases)
                 return tile_product(tile, LATE, parts, sign, found)
-            *found, terms = tile_product(tile, EARLY, parts, sign, bases, ())
+            *found, terms = tile_product(tile, REST if sums_terms else EARLY, parts, sign, bases, sums_terms)
             (terms,) = tile_product(tile, LATE, parts, sign, (), (terms,), False)
             tile[2] = terms
             return [*tile_product(tile, LATE, parts, sign, found), terms]
@@ -302,11 +310,19 @@
         elif t == 0:
             tile, mark, _ = prepared(propagator[0])
         earlier = jnp.where(mine[t : t + 1] > 0.0, sum(arriving), 0.0)
-        parts = swap(earlier, scatter(earlier))
+        sent = scatter(earlier)
+        parts = swap(earlier, sent)
         if t < steps - 2:
             partial = apply_tile(tile, mark, parts, -1.0, partial)
         else:
-            *partial, terms = apply_tile(tile, mark, parts, -1.0, partial, (sums, swapped))
+            pre = ()
+            if PRE and by_kernel:
+                *partial, pre = tile_product([*tile, mark, sums, swapped], PRE, parts, -1.0, partial, ())
+                tied = tie(sent[PRE_TIE], pre)
+                parts[2 * PRE_TIE + 2], pre = tied
+                parts[2 * PRE_TIE + 3] = move(parts[2 * PRE_TIE + 2], 1)
+                pre = (pre,)
+            *partial, terms = apply_tile(tile, mark, parts, -1.0, partial, (sums, swapped), pre)
 
     others = [move(partial[e], e * GROUP) for e in range(1, high_count)]
     terms = [terms]
@@ -314,7 +330,7 @@
         total = sum(terms[1:], terms[0])
         around = [move(total, flip, ahead) for flip, ahead in reversed(moves)]
         if k == 1:
-            *others, around[0] = tie(*others, around[0])
+            around[0], *others = tie(around[0], *others)
         terms = [total, *around]
     if by_kernel:
         solved, tip = finish(tip_inv, tip_rhs, terms, [partial[0], *others])

time: 52.6 us -> 51.3 us (0.975)
  starting transfers between devices: 25.2 us -> 23.8 us
  waiting for transfers between devices: 14.5 us -> 15.6 us
  Pallas kernels: 11.9 us -> 10.9 us
    ppermute x25, starting transfers between devices: 25.2 us -> 23.8 us  [move(): return lax.ppermute(value, AXES, route)]
    ppermute x25, waiting for transfers between devices: 14.5 us -> 15.6 us  [move(): return lax.ppermute(value, AXES, route)]
    pallas_call x2, Pallas kernels: 7.66 us -> 6.61 us  [split_tile(): pl.pallas_call(functools.partial(split_tile_kernel, piece), out_shape=[ha...]
    pallas_call x5 -> x6, Pallas kernels: 3.47 us -> 3.55 us  [tile_product(): pl.pallas_call(functools.partial(product_kernel, members, sign, blocks, h...]
  transfers between devices with their start and end apart: 25 -> 25, of which waited for: 14 -> 13; matrix products, arithmetic and copies ran while one was open for 0% -> 0% of each run, Pallas kernels for 20% -> 19%
where the time goes in v5:
time: 51.3 us; the launch traced here: 51.2 us
  starting transfers between devices  23.8 us (46%)
  waiting for transfers between devices  15.6 us (30%)
  Pallas kernels  10.9 us (21%)
  between operations  0.76 us (1%)
    ppermute x25, starting transfers between devices, move(): return lax.ppermute(value, AXES, route)  23.8 us
    ppermute x25, waiting for transfers between devices, move(): return lax.ppermute(value, AXES, route)  15.6 us
    pallas_call x2, Pallas kernels, split_tile(): pl.pallas_call(functools.partial(split_tile_kernel, piece), out_shape=[ha...  6.61 us
    pallas_call x6, Pallas kernels, tile_product(): pl.pallas_call(functools.partial(product_kernel, members, sign, blocks, h...  3.55 us
  transfers between devices with their start and end apart: 25, of which 13 were waited for; matrix products, arithmetic and copies ran while one was open for 0% of the time, Pallas kernels for 19%

profile of v5, /device:TPU:0, one launch (start us, length us, event | category | flops | bytes accessed | tf_op | source)
XLA Modules:
  0.0 51.2 jit_solution(8708424427919217287)
XLA Ops:
  0.6 3.1 %collective-permute-start.2 = (f32[256,128]{1,0:T(8,128)}, f32[256,128]{1,0:T(8,128)S(1)}, u32[]{:S(2)}, u32[]{:S(2)}) collective-permute-start(f32[256,128]{1,0:T(8,128)} %bitcast.7), channel_id=1, source_target_pairs={{0,4},{1,5},{2,6},{3,7},{4,0},{5,1},{6,2},{7,3},{8,12},{9,13},{10,... | collective-permute-start | bytes 393224 | tf_op jit(solution)/shard_map/ppermute | solution.py:226
  3.7 1.5 %collective-permute-start = (f32[256,128]{1,0:T(8,128)}, f32[256,128]{1,0:T(8,128)S(1)}, u32[]{:S(2)}, u32[]{:S(2)}) collective-permute-start(f32[256,128]{1,0:T(8,128)} %bitcast.8), channel_id=1, source_target_pairs={{0,2},{1,3},{2,0},{3,1},{4,6},{5,7},{6,4},{7,5},{8,10},{9,11},{10,... | collective-permute-start | bytes 393224 | tf_op jit(solution)/shard_map/ppermute | solution.py:226
  5.2 2.6 %collective-permute-start.1 = (f32[64,256]{1,0:T(8,128)}, f32[64,256]{1,0:T(8,128)S(1)}, u32[]{:S(2)}, u32[]{:S(2)}) collective-permute-start(f32[64,256]{1,0:T(8,128)} %bitcast.12), channel_id=1, source_target_pairs={{0,8},{1,9},{2,10},{3,11},{4,12},{5,13},{6,14},{7,15},{8,0},{9,1},... | collective-permute-start | bytes 196616 | tf_op jit(solution)/shard_map/ppermute | solution.py:226
  7.8 0.4 collective-permute-start.3
  8.2 0.0 collective-permute-start.5
  8.2 0.0 copy-start
  8.2 2.9 %shard_map.77 = (bf16[512,2048]{1,0:T(8,128)(2,1)S(1)}, bf16[512,2048]{1,0:T(8,128)(2,1)S(1)}, f32[8,128]{1,0:T(8,128)S(1)}, f32[8,128]{1,0:T(8,128)}) custom-call(f32[512,2048]{1,0:T(8,128)} %bitcast.14), custom_call_target="tpu_custom_call" | custom-call | flops 8388608 | bytes 8388608 | tf_op jit(solution)/shard_map/pallas_call | solution.py:94
  11.2 0.0 collective-permute-done.2.refs_9_
  11.2 0.6 %collective-permute-start.7 = (f32[256,128]{1,0:T(8,128)S(1)}, f32[256,128]{1,0:T(8,128)S(1)}, u32[]{:S(2)}, u32[]{:S(2)}) collective-permute-start(f32[256,128]{1,0:T(8,128)S(1)} %collective-permute-done.2.refs_9_), channel_id=1, source_target_pairs={{0,1},{1,0},{2,3},{3,2},{4,5},{5,4},{6,7},{7,6},{8,9},{9,8},{10,11... | collective-permute-start | bytes 393224 | tf_op jit(solution)/shard_map/ppermute | solution.py:226
  11.7 0.0 collective-permute-done.1.refs_1_
  11.8 0.0 collective-permute-done.refs_7_
  11.8 0.1 collective-permute-start.6
  11.8 2.0 %collective-permute-done.3.refs_11_ = f32[256,128]{1,0:T(8,128)S(1)} collective-permute-done((f32[256,128]{1,0:T(8,128)}, f32[256,128]{1,0:T(8,128)S(1)}, u32[]{:S(2)}, u32[]{:S(2)}) %collective-permute-start.3) | collective-permute-done | bytes 131104 | tf_op jit(solution)/shard_map/ppermute | solution.py:226
  13.9 0.0 collective-permute-start.4
  13.9 0.0 collective-permute-done.5.refs_6_
  13.9 0.0 collective-permute-done.7.refs_10_
  13.9 0.0 collective-permute-done.6.refs_8_
  13.9 0.0 copy-done
  13.9 1.2 %shard_map.78 = (f32[256,128]{1,0:T(8,128)S(1)}, f32[256,128]{1,0:T(8,128)S(1)}) custom-call(bf16[512,2048]{1,0:T(8,128)(2,1)S(1)} %get-tuple-element.34.refs_0_, bf16[512,2048]{1,0:T(8,128)(2,1)S(1)} %get-tuple-element.35.refs_1_, f32[8,128]{1,0:T(8,128)S(1)} %get-tuple-element.37.refs_2_.refs_3_.refs_4_, ...), custom_call_target="tpu_custom_call" | custom-call | flops 704643072 | bytes 3670016 | tf_op jit(solution)/shard_map/pallas_call | solution.py:161
  15.1 0.1 collective-permute-done.4.refs_5_
  15.2 0.3 shard_map.79
  15.5 2.5 %collective-permute-start.9 = (f32[256,128]{1,0:T(8,128)S(1)}, f32[256,128]{1,0:T(8,128)S(1)}, u32[]{:S(2)}, u32[]{:S(2)}) collective-permute-start(f32[256,128]{1,0:T(8,128)S(1)} %get-tuple-element.43.refs_3_.refs_8_), channel_id=1, source_target_pairs={{0,24},{1,25},{2,26},{3,27},{4,28},{5,29},{6,30},{7,31},{8,16},{9,... | collective-permute-start | bytes 393224 | tf_op jit(solution)/shard_map/ppermute | solution.py:226
  18.0 0.5 collective-permute-start.10
  18.5 0.0 copy-done.1
  18.5 3.7 %shard_map.80 = (bf16[512,2048]{1,0:T(8,128)(2,1)S(1)}, bf16[512,2048]{1,0:T(8,128)(2,1)S(1)}, f32[8,128]{1,0:T(8,128)S(1)}, f32[64,2176]{1,0:T(8,128)S(1)}) custom-call(f32[512,2048]{1,0:T(8,128)} %bitcast.15, f32[64,256]{1,0:T(8,128)S(1)} %bitcast.13, f32[64,256]{1,0:T(8,128)S(1)} %collective-permute-done.1.refs_1_, ...), custom_call_target="tpu_custom_call" | custom-call | flops 8388608 | bytes 8388608 | tf_op jit(solution)/shard_map/pallas_call | solution.py:94
  22.2 0.1 collective-permute-start.8
  22.3 3.8 %collective-permute-done.9 = f32[256,128]{1,0:T(8,128)S(1)} collective-permute-done((f32[256,128]{1,0:T(8,128)S(1)}, f32[256,128]{1,0:T(8,128)S(1)}, u32[]{:S(2)}, u32[]{:S(2)}) %collective-permute-start.9) | collective-permute-done | bytes 131104 | tf_op jit(solution)/shard_map/ppermute | solution.py:226
  26.1 0.1 collective-permute-done.10
  26.2 0.5 %collective-permute-start.14 = (f32[256,128]{1,0:T(8,128)S(1)}, f32[256,128]{1,0:T(8,128)S(1)}, u32[]{:S(2)}, u32[]{:S(2)}) collective-permute-start(f32[256,128]{1,0:T(8,128)S(1)} %add_select_fusion.refs_5_), channel_id=1, source_target_pairs={{0,2},{1,3},{2,0},{3,1},{4,6},{5,7},{6,4},{7,5},{8,10},{9,11},{10,... | collective-permute-start | bytes 393224 | tf_op jit(solution)/shard_map/ppermute | solution.py:226
  26.7 1.4 %collective-permute-start.16 = (f32[256,128]{1,0:T(8,128)S(1)}, f32[256,128]{1,0:T(8,128)S(1)}, u32[]{:S(2)}, u32[]{:S(2)}) collective-permute-start(f32[256,128]{1,0:T(8,128)S(1)} %add_select_fusion.refs_5_), channel_id=1, source_target_pairs={{0,4},{1,5},{2,6},{3,7},{4,0},{5,1},{6,2},{7,3},{8,12},{9,13},{10,... | collective-permute-start | bytes 393224 | tf_op jit(solution)/shard_map/ppermute | solution.py:226
  28.1 0.0 collective-permute-start.12
  28.1 1.6 %collective-permute-start.11 = (f32[256,128]{1,0:T(8,128)S(1)}, f32[256,128]{1,0:T(8,128)S(1)}, u32[]{:S(2)}, u32[]{:S(2)}) collective-permute-start(f32[256,128]{1,0:T(8,128)S(1)} %add_select_fusion.refs_5_), channel_id=1, source_target_pairs={{0,6},{1,7},{2,4},{3,5},{4,2},{5,3},{6,0},{7,1},{8,14},{9,15},{10,... | collective-permute-start | bytes 393224 | tf_op jit(solution)/shard_map/ppermute | solution.py:226
  29.8 1.7 %collective-permute-done.14.refs_5_ = f32[256,128]{1,0:T(8,128)S(1)} collective-permute-done((f32[256,128]{1,0:T(8,128)S(1)}, f32[256,128]{1,0:T(8,128)S(1)}, u32[]{:S(2)}, u32[]{:S(2)}) %collective-permute-start.14) | collective-permute-done | bytes 131104 | tf_op jit(solution)/shard_map/ppermute | solution.py:226
  31.5 0.0 collective-permute-start.15
  31.5 0.6 %collective-permute-done.16.refs_7_ = f32[256,128]{1,0:T(8,128)S(1)} collective-permute-done((f32[256,128]{1,0:T(8,128)S(1)}, f32[256,128]{1,0:T(8,128)S(1)}, u32[]{:S(2)}, u32[]{:S(2)}) %collective-permute-start.16) | collective-permute-done | bytes 131104 | tf_op jit(solution)/shard_map/ppermute | solution.py:226
  32.1 0.0 collective-permute-start.17
  32.1 0.0 collective-permute-done.12.refs_6_
  32.1 0.0 collective-permute-done.8.refs_3_
  32.1 0.5 %shard_map.81 = (f32[256,128]{1,0:T(8,128)S(1)}, f32[256,128]{1,0:T(8,128)S(1)}, f32[64,128]{1,0:T(8,128)S(1)}) custom-call(bf16[512,2048]{1,0:T(8,128)(2,1)S(1)} %get-tuple-element.44.refs_0_, bf16[512,2048]{1,0:T(8,128)(2,1)S(1)} %get-tuple-element.45.refs_1_, f32[64,2176]{1,0:T(8,128)S(1)} %get-tuple-element.46.refs_2_, ...), custom_call_target="tpu_custom_call" | custom-call | flops 226492416 | bytes 1179648 | tf_op jit(solution)/shard_map/pallas_call | solution.py:161
  32.7 2.9 %collective-permute-done.11.refs_9_ = f32[256,128]{1,0:T(8,128)S(1)} collective-permute-done((f32[256,128]{1,0:T(8,128)S(1)}, f32[256,128]{1,0:T(8,128)S(1)}, u32[]{:S(2)}, u32[]{:S(2)}) %collective-permute-start.11) | collective-permute-done | bytes 131104 | tf_op jit(solution)/shard_map/ppermute | solution.py:226
  35.5 0.0 collective-permute-start.13
  35.5 0.0 collective-permute-done.15.refs_6_
  35.5 0.0 collective-permute-done.17.refs_8_
  35.5 1.1 %shard_map.82 = (f32[256,128]{1,0:T(8,128)S(1)}, f32[256,128]{1,0:T(8,128)S(1)}, f32[64,128]{1,0:T(8,128)S(1)}) custom-call(bf16[512,2048]{1,0:T(8,128)(2,1)S(1)} %get-tuple-element.44.refs_0_, bf16[512,2048]{1,0:T(8,128)(2,1)S(1)} %get-tuple-element.45.refs_1_, f32[64,2176]{1,0:T(8,128)S(1)} %get-tuple-element.46.refs_2_, ...), custom_call_target="tpu_custom_call" | custom-call | flops 566231040 | bytes 2949120 | tf_op jit(solution)/shard_map/pallas_call | solution.py:161
  36.6 0.3 collective-permute-done.13.refs_5_
  36.9 0.2 shard_map.83.refs_2_.refs_3_.refs_4_
  37.0 2.4 %collective-permute-start.18 = (f32[64,128]{1,0:T(8,128)S(1)}, f32[64,128]{1,0:T(8,128)S(1)}, u32[]{:S(2)}, u32[]{:S(2)}) collective-permute-start(f32[64,128]{1,0:T(8,128)S(1)} %shard_map.83.refs_2_.refs_3_.refs_4_), channel_id=1, source_target_pairs={{0,12},{1,13},{2,14},{3,15},{4,8},{5,9},{6,10},{7,11},{8,4},{9,5},... | collective-permute-start | bytes 98312 | tf_op jit(solution)/shard_map/ppermute | solution.py:226
  39.5 0.0 collective-permute-start.19
  39.5 2.0 %collective-permute-start.20 = (f32[64,128]{1,0:T(8,128)S(1)}, f32[64,128]{1,0:T(8,128)S(1)}, u32[]{:S(2)}, u32[]{:S(2)}) collective-permute-start(f32[64,128]{1,0:T(8,128)S(1)} %shard_map.83.refs_2_.refs_3_.refs_4_), channel_id=1, source_target_pairs={{0,4},{1,5},{2,6},{3,7},{4,0},{5,1},{6,2},{7,3},{8,12},{9,13},{10,... | collective-permute-start | bytes 98312 | tf_op jit(solution)/shard_map/ppermute | solution.py:226
  41.5 0.3 shard_map.84
  41.8 1.0 %collective-permute-start.22 = (f32[256,128]{1,0:T(8,128)S(1)}, f32[256,128]{1,0:T(8,128)S(1)}, u32[]{:S(2)}, u32[]{:S(2)}) collective-permute-start(f32[256,128]{1,0:T(8,128)S(1)} %get-tuple-element.58), channel_id=1, source_target_pairs={{0,8},{1,9},{2,10},{3,11},{4,12},{5,13},{6,14},{7,15},{8,0},{9,1},... | collective-permute-start | bytes 393224 | tf_op jit(solution)/shard_map/ppermute | solution.py:226
  42.8 0.1 collective-permute-done.18
  42.8 1.5 %collective-permute-done.19 = f32[64,128]{1,0:T(8,128)S(1)} collective-permute-done((f32[64,128]{1,0:T(8,128)S(1)}, f32[64,128]{1,0:T(8,128)S(1)}, u32[]{:S(2)}, u32[]{:S(2)}) %collective-permute-start.19) | collective-permute-done | bytes 32800 | tf_op jit(solution)/shard_map/ppermute | solution.py:226
  44.3 0.0 collective-permute-done.20
  44.3 1.6 %collective-permute-start.21 = (f32[64,128]{1,0:T(8,128)S(1)}, f32[64,128]{1,0:T(8,128)S(1)}, u32[]{:S(2)}, u32[]{:S(2)}) collective-permute-start(f32[64,128]{1,0:T(8,128)S(1)} %add_add_fusion.refs_0_), channel_id=1, source_target_pairs={{0,18},{1,19},{2,16},{3,17},{4,22},{5,23},{6,20},{7,21},{8,26},{9,... | collective-permute-start | bytes 98312 | tf_op jit(solution)/shard_map/ppermute | solution.py:226
  45.9 0.6 %collective-permute-start.23 = (f32[64,128]{1,0:T(8,128)S(1)}, f32[64,128]{1,0:T(8,128)S(1)}, u32[]{:S(2)}, u32[]{:S(2)}) collective-permute-start(f32[64,128]{1,0:T(8,128)S(1)} %add_add_fusion.refs_0_), channel_id=1, source_target_pairs={{0,16},{1,17},{2,18},{3,19},{4,20},{5,21},{6,22},{7,23},{8,24},{9,... | collective-permute-start | bytes 98312 | tf_op jit(solution)/shard_map/ppermute | solution.py:226
  46.5 1.4 %collective-permute-start.24 = (f32[64,128]{1,0:T(8,128)S(1)}, f32[64,128]{1,0:T(8,128)S(1)}, u32[]{:S(2)}, u32[]{:S(2)}) collective-permute-start(f32[64,128]{1,0:T(8,128)S(1)} %add_add_fusion.refs_0_), channel_id=1, source_target_pairs={{0,2},{1,3},{2,0},{3,1},{4,6},{5,7},{6,4},{7,5},{8,10},{9,11},{10,... | collective-permute-start | bytes 98312 | tf_op jit(solution)/shard_map/ppermute | solution.py:226
  47.9 1.5 %collective-permute-done.21.refs_1_ = f32[64,128]{1,0:T(8,128)S(1)} collective-permute-done((f32[64,128]{1,0:T(8,128)S(1)}, f32[64,128]{1,0:T(8,128)S(1)}, u32[]{:S(2)}, u32[]{:S(2)}) %collective-permute-start.21) | collective-permute-done | bytes 32800 | tf_op jit(solution)/shard_map/ppermute | solution.py:226
  49.4 0.8 %collective-permute-done.22.refs_5_ = f32[256,128]{1,0:T(8,128)S(1)} collective-permute-done((f32[256,128]{1,0:T(8,128)S(1)}, f32[256,128]{1,0:T(8,128)S(1)}, u32[]{:S(2)}, u32[]{:S(2)}) %collective-permute-start.22) | collective-permute-done | bytes 131104 | tf_op jit(solution)/shard_map/ppermute | solution.py:226
  50.1 0.0 collective-permute-done.23.refs_2_
  50.1 0.3 collective-permute-done.24.refs_3_
  50.4 0.0 copy-done.2
  50.4 0.0 copy-done.3
  50.4 0.8 %shard_map.85 = (f32[256,128]{1,0:T(8,128)}, f32[64,128]{1,0:T(8,128)}) custom-call(f32[64,64]{1,0:T(8,128)S(1)} %copy-done.2, f32[64,128]{1,0:T(8,128)S(1)} %copy-done.3, f32[64,128]{1,0:T(8,128)S(1)} %add_add_fusion.refs_0_, f32[64,128]{1,0:T(8,128)S(1)} %collective-permute-done.21.refs_1_, f32[64,128]{1,0:T(8,128)S(1)} %collective-permute-done.23.refs_2_, ...), custom_call_target="tpu_custom_call" | custom-call | tf_op jit(solution)/shard_map/pallas_call | solution.py:198
  (6 shorter events, 0.0 us)
Async XLA Ops:
  0.6 10.5 %collective-permute-start.2 = (f32[256,128]{1,0:T(8,128)}, f32[256,128]{1,0:T(8,128)S(1)}, u32[]{:S(2)}, u32[]{:S(2)}) collective-permute-start(f32[256,128]{1,0:T(8,128)} %bitcast.7), channel_id=1, source_target_pairs={{0,4},{1,5},{2,6},{3,7},{4,0},{5,1},{6,2},{7,3},{8,12},{9,13},{10,... | collective-permute-start | bytes 393224 | tf_op jit(solution)/shard_map/ppermute | solution.py:226
  3.7 8.0 %collective-permute-start = (f32[256,128]{1,0:T(8,128)}, f32[256,128]{1,0:T(8,128)S(1)}, u32[]{:S(2)}, u32[]{:S(2)}) collective-permute-start(f32[256,128]{1,0:T(8,128)} %bitcast.8), channel_id=1, source_target_pairs={{0,2},{1,3},{2,0},{3,1},{4,6},{5,7},{6,4},{7,5},{8,10},{9,11},{10,... | collective-permute-start | bytes 393224 | tf_op jit(solution)/shard_map/ppermute | solution.py:226
  5.2 6.5 %collective-permute-start.1 = (f32[64,256]{1,0:T(8,128)}, f32[64,256]{1,0:T(8,128)S(1)}, u32[]{:S(2)}, u32[]{:S(2)}) collective-permute-start(f32[64,256]{1,0:T(8,128)} %bitcast.12), channel_id=1, source_target_pairs={{0,8},{1,9},{2,10},{3,11},{4,12},{5,13},{6,14},{7,15},{8,0},{9,1},... | collective-permute-start | bytes 196616 | tf_op jit(solution)/shard_map/ppermute | solution.py:226
  7.8 6.1 %collective-permute-start.3 = (f32[256,128]{1,0:T(8,128)}, f32[256,128]{1,0:T(8,128)S(1)}, u32[]{:S(2)}, u32[]{:S(2)}) collective-permute-start(f32[256,128]{1,0:T(8,128)} %bitcast.9), channel_id=1, source_target_pairs={{0,6},{1,7},{2,4},{3,5},{4,2},{5,3},{6,0},{7,1},{8,14},{9,15},{10,... | collective-permute-start | bytes 393224 | tf_op jit(solution)/shard_map/ppermute | solution.py:226
  8.2 5.7 %collective-permute-start.5 = (f32[256,128]{1,0:T(8,128)}, f32[256,128]{1,0:T(8,128)S(1)}, u32[]{:S(2)}, u32[]{:S(2)}) collective-permute-start(f32[256,128]{1,0:T(8,128)} %bitcast.10), channel_id=1, source_target_pairs={{0,1},{1,0},{2,3},{3,2},{4,5},{5,4},{6,7},{7,6},{8,9},{9,8},{10,11... | collective-permute-start | bytes 393224 | tf_op jit(solution)/shard_map/ppermute | solution.py:226
  8.2 5.7 %copy-start = (f32[1,256,128]{2,1,0:T(8,128)S(1)}, f32[1,256,128]{2,1,0:T(8,128)}, u32[]{:S(2)}) copy-start(f32[1,256,128]{2,1,0:T(8,128)} %param.8) | copy-start | bytes 393220
  11.2 2.7 %collective-permute-start.7 = (f32[256,128]{1,0:T(8,128)S(1)}, f32[256,128]{1,0:T(8,128)S(1)}, u32[]{:S(2)}, u32[]{:S(2)}) collective-permute-start(f32[256,128]{1,0:T(8,128)S(1)} %collective-permute-done.2.refs_9_), channel_id=1, source_target_pairs={{0,1},{1,0},{2,3},{3,2},{4,5},{5,4},{6,7},{7,6},{8,9},{9,8},{10,11... | collective-permute-start | bytes 393224 | tf_op jit(solution)/shard_map/ppermute | solution.py:226
  11.8 2.1 %collective-permute-start.6 = (f32[256,128]{1,0:T(8,128)S(1)}, f32[256,128]{1,0:T(8,128)S(1)}, u32[]{:S(2)}, u32[]{:S(2)}) collective-permute-start(f32[256,128]{1,0:T(8,128)S(1)} %collective-permute-done.refs_7_), channel_id=1, source_target_pairs={{0,1},{1,0},{2,3},{3,2},{4,5},{5,4},{6,7},{7,6},{8,9},{9,8},{10,11... | collective-permute-start | bytes 393224 | tf_op jit(solution)/shard_map/ppermute | solution.py:226
  13.9 1.3 %collective-permute-start.4 = (f32[256,128]{1,0:T(8,128)S(1)}, f32[256,128]{1,0:T(8,128)S(1)}, u32[]{:S(2)}, u32[]{:S(2)}) collective-permute-start(f32[256,128]{1,0:T(8,128)S(1)} %collective-permute-done.3.refs_11_), channel_id=1, source_target_pairs={{0,1},{1,0},{2,3},{3,2},{4,5},{5,4},{6,7},{7,6},{8,9},{9,8},{10,11... | collective-permute-start | bytes 393224 | tf_op jit(solution)/shard_map/ppermute | solution.py:226
  15.2 3.3 %copy-start.1 = (f32[1,64,256]{2,1,0:T(8,128)S(1)}, f32[1,64,256]{2,1,0:T(8,128)}, u32[]{:S(2)}) copy-start(f32[1,64,256]{2,1,0:T(8,128)} %param.9) | copy-start | bytes 196612
  15.5 10.6 %collective-permute-start.9 = (f32[256,128]{1,0:T(8,128)S(1)}, f32[256,128]{1,0:T(8,128)S(1)}, u32[]{:S(2)}, u32[]{:S(2)}) collective-permute-start(f32[256,128]{1,0:T(8,128)S(1)} %get-tuple-element.43.refs_3_.refs_8_), channel_id=1, source_target_pairs={{0,24},{1,25},{2,26},{3,27},{4,28},{5,29},{6,30},{7,31},{8,16},{9,... | collective-permute-start | bytes 393224 | tf_op jit(solution)/shard_map/ppermute | solution.py:226
  18.0 8.2 %collective-permute-start.10 = (f32[256,128]{1,0:T(8,128)S(1)}, f32[256,128]{1,0:T(8,128)S(1)}, u32[]{:S(2)}, u32[]{:S(2)}) collective-permute-start(f32[256,128]{1,0:T(8,128)S(1)} %get-tuple-element.42.refs_2_.refs_7_), channel_id=1, source_target_pairs={{0,16},{1,17},{2,18},{3,19},{4,20},{5,21},{6,22},{7,23},{8,24},{9,... | collective-permute-start | bytes 393224 | tf_op jit(solution)/shard_map/ppermute | solution.py:226
  22.2 9.9 %collective-permute-start.8 = (f32[64,2176]{1,0:T(8,128)S(1)}, f32[64,2176]{1,0:T(8,128)S(1)}, u32[]{:S(2)}, u32[]{:S(2)}) collective-permute-start(f32[64,2176]{1,0:T(8,128)S(1)} %get-tuple-element.46.refs_2_), channel_id=1, source_target_pairs={{0,1},{1,0},{2,3},{3,2},{4,5},{5,4},{6,7},{7,6},{8,9},{9,8},{10,11... | collective-permute-start | bytes 1671176 | tf_op jit(solution)/shard_map/ppermute | solution.py:226
  26.2 5.3 %collective-permute-start.14 = (f32[256,128]{1,0:T(8,128)S(1)}, f32[256,128]{1,0:T(8,128)S(1)}, u32[]{:S(2)}, u32[]{:S(2)}) collective-permute-start(f32[256,128]{1,0:T(8,128)S(1)} %add_select_fusion.refs_5_), channel_id=1, source_target_pairs={{0,2},{1,3},{2,0},{3,1},{4,6},{5,7},{6,4},{7,5},{8,10},{9,11},{10,... | collective-permute-start | bytes 393224 | tf_op jit(solution)/shard_map/ppermute | solution.py:226
  26.7 5.4 %collective-permute-start.16 = (f32[256,128]{1,0:T(8,128)S(1)}, f32[256,128]{1,0:T(8,128)S(1)}, u32[]{:S(2)}, u32[]{:S(2)}) collective-permute-start(f32[256,128]{1,0:T(8,128)S(1)} %add_select_fusion.refs_5_), channel_id=1, source_target_pairs={{0,4},{1,5},{2,6},{3,7},{4,0},{5,1},{6,2},{7,3},{8,12},{9,13},{10,... | collective-permute-start | bytes 393224 | tf_op jit(solution)/shard_map/ppermute | solution.py:226
  28.1 4.0 %collective-permute-start.12 = (f32[256,128]{1,0:T(8,128)S(1)}, f32[256,128]{1,0:T(8,128)S(1)}, u32[]{:S(2)}, u32[]{:S(2)}) collective-permute-start(f32[256,128]{1,0:T(8,128)S(1)} %add_select_fusion.refs_5_), channel_id=1, source_target_pairs={{0,1},{1,0},{2,3},{3,2},{4,5},{5,4},{6,7},{7,6},{8,9},{9,8},{10,11... | collective-permute-start | bytes 393224 | tf_op jit(solution)/shard_map/ppermute | solution.py:226
  28.1 7.4 %collective-permute-start.11 = (f32[256,128]{1,0:T(8,128)S(1)}, f32[256,128]{1,0:T(8,128)S(1)}, u32[]{:S(2)}, u32[]{:S(2)}) collective-permute-start(f32[256,128]{1,0:T(8,128)S(1)} %add_select_fusion.refs_5_), channel_id=1, source_target_pairs={{0,6},{1,7},{2,4},{3,5},{4,2},{5,3},{6,0},{7,1},{8,14},{9,15},{10,... | collective-permute-start | bytes 393224 | tf_op jit(solution)/shard_map/ppermute | solution.py:226
  31.5 4.0 %collective-permute-start.15 = (f32[256,128]{1,0:T(8,128)S(1)}, f32[256,128]{1,0:T(8,128)S(1)}, u32[]{:S(2)}, u32[]{:S(2)}) collective-permute-start(f32[256,128]{1,0:T(8,128)S(1)} %collective-permute-done.14.refs_5_), channel_id=1, source_target_pairs={{0,1},{1,0},{2,3},{3,2},{4,5},{5,4},{6,7},{7,6},{8,9},{9,8},{10,11... | collective-permute-start | bytes 393224 | tf_op jit(solution)/shard_map/ppermute | solution.py:226
  32.1 3.4 %collective-permute-start.17 = (f32[256,128]{1,0:T(8,128)S(1)}, f32[256,128]{1,0:T(8,128)S(1)}, u32[]{:S(2)}, u32[]{:S(2)}) collective-permute-start(f32[256,128]{1,0:T(8,128)S(1)} %collective-permute-done.16.refs_7_), channel_id=1, source_target_pairs={{0,1},{1,0},{2,3},{3,2},{4,5},{5,4},{6,7},{7,6},{8,9},{9,8},{10,11... | collective-permute-start | bytes 393224 | tf_op jit(solution)/shard_map/ppermute | solution.py:226
  35.5 1.3 %collective-permute-start.13 = (f32[256,128]{1,0:T(8,128)S(1)}, f32[256,128]{1,0:T(8,128)S(1)}, u32[]{:S(2)}, u32[]{:S(2)}) collective-permute-start(f32[256,128]{1,0:T(8,128)S(1)} %collective-permute-done.11.refs_9_), channel_id=1, source_target_pairs={{0,1},{1,0},{2,3},{3,2},{4,5},{5,4},{6,7},{7,6},{8,9},{9,8},{10,11... | collective-permute-start | bytes 393224 | tf_op jit(solution)/shard_map/ppermute | solution.py:226
  37.0 5.8 %collective-permute-start.18 = (f32[64,128]{1,0:T(8,128)S(1)}, f32[64,128]{1,0:T(8,128)S(1)}, u32[]{:S(2)}, u32[]{:S(2)}) collective-permute-start(f32[64,128]{1,0:T(8,128)S(1)} %shard_map.83.refs_2_.refs_3_.refs_4_), channel_id=1, source_target_pairs={{0,12},{1,13},{2,14},{3,15},{4,8},{5,9},{6,10},{7,11},{8,4},{9,5},... | collective-permute-start | bytes 98312 | tf_op jit(solution)/shard_map/ppermute | solution.py:226
  39.5 4.8 %collective-permute-start.19 = (f32[64,128]{1,0:T(8,128)S(1)}, f32[64,128]{1,0:T(8,128)S(1)}, u32[]{:S(2)}, u32[]{:S(2)}) collective-permute-start(f32[64,128]{1,0:T(8,128)S(1)} %shard_map.83.refs_2_.refs_3_.refs_4_), channel_id=1, source_target_pairs={{0,8},{1,9},{2,10},{3,11},{4,12},{5,13},{6,14},{7,15},{8,0},{9,1},... | collective-permute-start | bytes 98312 | tf_op jit(solution)/shard_map/ppermute | solution.py:226
  39.5 4.8 %collective-permute-start.20 = (f32[64,128]{1,0:T(8,128)S(1)}, f32[64,128]{1,0:T(8,128)S(1)}, u32[]{:S(2)}, u32[]{:S(2)}) collective-permute-start(f32[64,128]{1,0:T(8,128)S(1)} %shard_map.83.refs_2_.refs_3_.refs_4_), channel_id=1, source_target_pairs={{0,4},{1,5},{2,6},{3,7},{4,0},{5,1},{6,2},{7,3},{8,12},{9,13},{10,... | collective-permute-start | bytes 98312 | tf_op jit(solution)/shard_map/ppermute | solution.py:226
  41.5 8.9 %copy-start.2 = (f32[64,64]{1,0:T(8,128)S(1)}, f32[64,64]{1,0:T(8,128)}, u32[]{:S(2)}) copy-start(f32[64,64]{1,0:T(8,128)} %tip_inv.1) | copy-start | bytes 49156
  41.5 8.9 %copy-start.3 = (f32[64,128]{1,0:T(8,128)S(1)}, f32[64,128]{1,0:T(8,128)}, u32[]{:S(2)}) copy-start(f32[64,128]{1,0:T(8,128)} %tip_rhs.1) | copy-start | bytes 98308
  41.8 8.3 %collective-permute-start.22 = (f32[256,128]{1,0:T(8,128)S(1)}, f32[256,128]{1,0:T(8,128)S(1)}, u32[]{:S(2)}, u32[]{:S(2)}) collective-permute-start(f32[256,128]{1,0:T(8,128)S(1)} %get-tuple-element.58), channel_id=1, source_target_pairs={{0,8},{1,9},{2,10},{3,11},{4,12},{5,13},{6,14},{7,15},{8,0},{9,1},... | collective-permute-start | bytes 393224 | tf_op jit(solution)/shard_map/ppermute | solution.py:226
  44.3 5.1 %collective-permute-start.21 = (f32[64,128]{1,0:T(8,128)S(1)}, f32[64,128]{1,0:T(8,128)S(1)}, u32[]{:S(2)}, u32[]{:S(2)}) collective-permute-start(f32[64,128]{1,0:T(8,128)S(1)} %add_add_fusion.refs_0_), channel_id=1, source_target_pairs={{0,18},{1,19},{2,16},{3,17},{4,22},{5,23},{6,20},{7,21},{8,26},{9,... | collective-permute-start | bytes 98312 | tf_op jit(solution)/shard_map/ppermute | solution.py:226
  45.9 4.3 %collective-permute-start.23 = (f32[64,128]{1,0:T(8,128)S(1)}, f32[64,128]{1,0:T(8,128)S(1)}, u32[]{:S(2)}, u32[]{:S(2)}) collective-permute-start(f32[64,128]{1,0:T(8,128)S(1)} %add_add_fusion.refs_0_), channel_id=1, source_target_pairs={{0,16},{1,17},{2,18},{3,19},{4,20},{5,21},{6,22},{7,23},{8,24},{9,... | collective-permute-start | bytes 98312 | tf_op jit(solution)/shard_map/ppermute | solution.py:226
  46.5 3.9 %collective-permute-start.24 = (f32[64,128]{1,0:T(8,128)S(1)}, f32[64,128]{1,0:T(8,128)S(1)}, u32[]{:S(2)}, u32[]{:S(2)}) collective-permute-start(f32[64,128]{1,0:T(8,128)S(1)} %add_add_fusion.refs_0_), channel_id=1, source_target_pairs={{0,2},{1,3},{2,0},{3,1},{4,6},{5,7},{6,4},{7,5},{8,10},{9,11},{10,... | collective-permute-start | bytes 98312 | tf_op jit(solution)/shard_map/ppermute | solution.py:226

commit v6 on v5

--- a/solution.py
+++ b/solution.py
@@ -102,7 +102,7 @@
             pltpu.SemaphoreType.DMA((high_count, group)),
         ],
         cost_estimate=pl.CostEstimate(
-            flops=8 * tile.size, bytes_accessed=8 * tile.size, transcendentals=0
+            flops=100 * tile.size, bytes_accessed=16 * tile.size, transcendentals=0
         ),
         compiler_params=pltpu.CompilerParams(vmem_limit_bytes=VMEM_LIMIT),
     )(pltpu.with_memory_space_constraint(tile, pltpu.HBM), *rows, *values)
@@ -165,8 +165,8 @@
         out_specs=[in_vmem] * len(outs),
         scratch_shapes=[pltpu.VMEM((depth, 2 * width), jnp.bfloat16)],
         cost_estimate=pl.CostEstimate(
-            flops=6 * (blocks * piece + height) * depth * width,
-            bytes_accessed=4 * (blocks * piece + height) * depth,
+            flops=40 * (blocks * piece + height) * depth * width,
+            bytes_accessed=40 * (blocks * piece + height) * depth,
             transcendentals=0,
         ),
         compiler_params=pltpu.CompilerParams(vmem_limit_bytes=VMEM_LIMIT),
@@ -294,7 +294,7 @@
     sent = scatter(rhs[0])
     arrows = [arrow[0]] + [move(arrow[0], e * GROUP) for e in range(1, high_count)]
     tile, mark, _ = prepared(inv_diag[0])
-    sent[0], *arrows[1:] = tie(sent[0], *arrows[1:])
+    *arrows[1:], mark = tie(*arrows[1:], mark)
     sent[1], mark = tie(sent[1], mark)
     mine = mark
     partial = apply_tile(tile, mark, swap(rhs[0], sent))
@@ -309,7 +309,7 @@
             swapped = move(sums, 1)
         elif t == 0:
             tile, mark, _ = prepared(propagator[0])
-        earlier = jnp.where(mine[t : t + 1] > 0.0, sum(arriving), 0.0)
+        earlier = jnp.where(mine[t : t + 1] > 0.0, sum(arriving[::-1]), 0.0)
         sent = scatter(earlier)
         parts = swap(earlier, sent)
         if t < steps - 2:
@@ -330,7 +330,7 @@
         total = sum(terms[1:], terms[0])
         around = [move(total, flip, ahead) for flip, ahead in reversed(moves)]
         if k == 1:
-            around[0], *others = tie(around[0], *others)
+            *others, around[0] = tie(*others, around[0])
         terms = [total, *around]
     if by_kernel:
         solved, tip = finish(tip_inv, tip_rhs, terms, [partial[0], *others])

time: 51.3 us -> 51.3 us (level)
  no operation moved by 1% of the time
where the time goes in v6:
time: 51.3 us; the launch traced here: 51.2 us
  starting transfers between devices  23.8 us (46%)
  waiting for transfers between devices  15.6 us (30%)
  Pallas kernels  10.9 us (21%)
  between operations  0.77 us (2%)
    ppermute x25, starting transfers between devices, move(): return lax.ppermute(value, AXES, route)  23.8 us
    ppermute x25, waiting for transfers between devices, move(): return lax.ppermute(value, AXES, route)  15.6 us
    pallas_call x2, Pallas kernels, split_tile(): pl.pallas_call(functools.partial(split_tile_kernel, piece), out_shape=[ha...  6.61 us
    pallas_call x6, Pallas kernels, tile_product(): pl.pallas_call(functools.partial(product_kernel, members, sign, blocks, h...  3.55 us
  transfers between devices with their start and end apart: 25, of which 13 were waited for; matrix products, arithmetic and copies ran while one was open for 0% of the time, Pallas kernels for 19%

profile of v6, /device:TPU:0, one launch (start us, length us, event | category | flops | bytes accessed | tf_op | source)
XLA Modules:
  0.0 51.2 jit_solution(11130101164378341973)
XLA Ops:
  0.6 3.1 %collective-permute-start.1 = (f32[256,128]{1,0:T(8,128)}, f32[256,128]{1,0:T(8,128)S(1)}, u32[]{:S(2)}, u32[]{:S(2)}) collective-permute-start(f32[256,128]{1,0:T(8,128)} %bitcast.9), channel_id=1, source_target_pairs={{0,4},{1,5},{2,6},{3,7},{4,0},{5,1},{6,2},{7,3},{8,12},{9,13},{10,... | collective-permute-start | bytes 393224 | tf_op jit(solution)/shard_map/ppermute | solution.py:226
  3.7 1.5 %collective-permute-start.5 = (f32[256,128]{1,0:T(8,128)}, f32[256,128]{1,0:T(8,128)S(1)}, u32[]{:S(2)}, u32[]{:S(2)}) collective-permute-start(f32[256,128]{1,0:T(8,128)} %bitcast.10), channel_id=1, source_target_pairs={{0,2},{1,3},{2,0},{3,1},{4,6},{5,7},{6,4},{7,5},{8,10},{9,11},{10,... | collective-permute-start | bytes 393224 | tf_op jit(solution)/shard_map/ppermute | solution.py:226
  5.2 2.6 %collective-permute-start = (f32[64,256]{1,0:T(8,128)}, f32[64,256]{1,0:T(8,128)S(1)}, u32[]{:S(2)}, u32[]{:S(2)}) collective-permute-start(f32[64,256]{1,0:T(8,128)} %bitcast.7), channel_id=1, source_target_pairs={{0,8},{1,9},{2,10},{3,11},{4,12},{5,13},{6,14},{7,15},{8,0},{9,1},... | collective-permute-start | bytes 196616 | tf_op jit(solution)/shard_map/ppermute | solution.py:226
  7.8 0.4 collective-permute-start.2
  8.2 0.0 collective-permute-start.4
  8.2 0.0 copy-start.3
  8.2 2.9 %shard_map.77 = (bf16[512,2048]{1,0:T(8,128)(2,1)S(1)}, bf16[512,2048]{1,0:T(8,128)(2,1)S(1)}, f32[8,128]{1,0:T(8,128)S(1)}, f32[8,128]{1,0:T(8,128)}) custom-call(f32[512,2048]{1,0:T(8,128)} %bitcast.14), custom_call_target="tpu_custom_call" | custom-call | flops 104857600 | bytes 16777216 | tf_op jit(solution)/shard_map/pallas_call | solution.py:94
  11.2 0.0 collective-permute-done.refs_1_
  11.2 0.0 collective-permute-done.1.refs_9_
  11.2 0.6 %collective-permute-start.7 = (f32[256,128]{1,0:T(8,128)S(1)}, f32[256,128]{1,0:T(8,128)S(1)}, u32[]{:S(2)}, u32[]{:S(2)}) collective-permute-start(f32[256,128]{1,0:T(8,128)S(1)} %collective-permute-done.1.refs_9_), channel_id=1, source_target_pairs={{0,1},{1,0},{2,3},{3,2},{4,5},{5,4},{6,7},{7,6},{8,9},{9,8},{10,11... | collective-permute-start | bytes 393224 | tf_op jit(solution)/shard_map/ppermute | solution.py:226
  11.8 0.0 collective-permute-done.5.refs_7_
  11.8 0.1 collective-permute-start.6
  11.8 2.0 %collective-permute-done.2.refs_11_ = f32[256,128]{1,0:T(8,128)S(1)} collective-permute-done((f32[256,128]{1,0:T(8,128)}, f32[256,128]{1,0:T(8,128)S(1)}, u32[]{:S(2)}, u32[]{:S(2)}) %collective-permute-start.2) | collective-permute-done | bytes 131104 | tf_op jit(solution)/shard_map/ppermute | solution.py:226
  13.9 0.0 collective-permute-start.3
  13.9 0.0 collective-permute-done.4.refs_6_
  13.9 0.0 collective-permute-done.7.refs_10_
  13.9 0.0 collective-permute-done.6.refs_8_
  13.9 0.0 copy-done.3
  13.9 1.2 %shard_map.78 = (f32[256,128]{1,0:T(8,128)S(1)}, f32[256,128]{1,0:T(8,128)S(1)}) custom-call(bf16[512,2048]{1,0:T(8,128)(2,1)S(1)} %get-tuple-element.35.refs_0_, bf16[512,2048]{1,0:T(8,128)(2,1)S(1)} %get-tuple-element.36.refs_1_, f32[8,128]{1,0:T(8,128)S(1)} %get-tuple-element.38.refs_2_.refs_3_.refs_4_, ...), custom_call_target="tpu_custom_call" | custom-call | flops 4697620480 | bytes 36700160 | tf_op jit(solution)/shard_map/pallas_call | solution.py:161
  15.1 0.1 collective-permute-done.3.refs_5_
  15.2 0.3 shard_map.79
  15.5 2.5 %collective-permute-start.9 = (f32[256,128]{1,0:T(8,128)S(1)}, f32[256,128]{1,0:T(8,128)S(1)}, u32[]{:S(2)}, u32[]{:S(2)}) collective-permute-start(f32[256,128]{1,0:T(8,128)S(1)} %get-tuple-element.43.refs_3_.refs_8_), channel_id=1, source_target_pairs={{0,24},{1,25},{2,26},{3,27},{4,28},{5,29},{6,30},{7,31},{8,16},{9,... | collective-permute-start | bytes 393224 | tf_op jit(solution)/shard_map/ppermute | solution.py:226
  18.0 0.5 collective-permute-start.10
  18.5 0.0 copy-done
  18.5 3.7 %shard_map.80 = (bf16[512,2048]{1,0:T(8,128)(2,1)S(1)}, bf16[512,2048]{1,0:T(8,128)(2,1)S(1)}, f32[8,128]{1,0:T(8,128)S(1)}, f32[64,2176]{1,0:T(8,128)S(1)}) custom-call(f32[512,2048]{1,0:T(8,128)} %bitcast.15, f32[64,256]{1,0:T(8,128)S(1)} %bitcast.8, f32[64,256]{1,0:T(8,128)S(1)} %collective-permute-done.refs_1_, ...), custom_call_target="tpu_custom_call" | custom-call | flops 104857600 | bytes 16777216 | tf_op jit(solution)/shard_map/pallas_call | solution.py:94
  22.2 0.1 collective-permute-start.8
  22.3 3.8 %collective-permute-done.9 = f32[256,128]{1,0:T(8,128)S(1)} collective-permute-done((f32[256,128]{1,0:T(8,128)S(1)}, f32[256,128]{1,0:T(8,128)S(1)}, u32[]{:S(2)}, u32[]{:S(2)}) %collective-permute-start.9) | collective-permute-done | bytes 131104 | tf_op jit(solution)/shard_map/ppermute | solution.py:226
  26.1 0.1 collective-permute-done.10
  26.2 0.5 %collective-permute-start.14 = (f32[256,128]{1,0:T(8,128)S(1)}, f32[256,128]{1,0:T(8,128)S(1)}, u32[]{:S(2)}, u32[]{:S(2)}) collective-permute-start(f32[256,128]{1,0:T(8,128)S(1)} %add_select_fusion.refs_5_), channel_id=1, source_target_pairs={{0,2},{1,3},{2,0},{3,1},{4,6},{5,7},{6,4},{7,5},{8,10},{9,11},{10,... | collective-permute-start | bytes 393224 | tf_op jit(solution)/shard_map/ppermute | solution.py:226
  26.7 1.4 %collective-permute-start.16 = (f32[256,128]{1,0:T(8,128)S(1)}, f32[256,128]{1,0:T(8,128)S(1)}, u32[]{:S(2)}, u32[]{:S(2)}) collective-permute-start(f32[256,128]{1,0:T(8,128)S(1)} %add_select_fusion.refs_5_), channel_id=1, source_target_pairs={{0,4},{1,5},{2,6},{3,7},{4,0},{5,1},{6,2},{7,3},{8,12},{9,13},{10,... | collective-permute-start | bytes 393224 | tf_op jit(solution)/shard_map/ppermute | solution.py:226
  28.1 0.0 collective-permute-start.12
  28.1 1.6 %collective-permute-start.11 = (f32[256,128]{1,0:T(8,128)S(1)}, f32[256,128]{1,0:T(8,128)S(1)}, u32[]{:S(2)}, u32[]{:S(2)}) collective-permute-start(f32[256,128]{1,0:T(8,128)S(1)} %add_select_fusion.refs_5_), channel_id=1, source_target_pairs={{0,6},{1,7},{2,4},{3,5},{4,2},{5,3},{6,0},{7,1},{8,14},{9,15},{10,... | collective-permute-start | bytes 393224 | tf_op jit(solution)/shard_map/ppermute | solution.py:226
  29.8 1.7 %collective-permute-done.14.refs_5_ = f32[256,128]{1,0:T(8,128)S(1)} collective-permute-done((f32[256,128]{1,0:T(8,128)S(1)}, f32[256,128]{1,0:T(8,128)S(1)}, u32[]{:S(2)}, u32[]{:S(2)}) %collective-permute-start.14) | collective-permute-done | bytes 131104 | tf_op jit(solution)/shard_map/ppermute | solution.py:226
  31.5 0.0 collective-permute-start.15
  31.5 0.6 %collective-permute-done.16.refs_7_ = f32[256,128]{1,0:T(8,128)S(1)} collective-permute-done((f32[256,128]{1,0:T(8,128)S(1)}, f32[256,128]{1,0:T(8,128)S(1)}, u32[]{:S(2)}, u32[]{:S(2)}) %collective-permute-start.16) | collective-permute-done | bytes 131104 | tf_op jit(solution)/shard_map/ppermute | solution.py:226
  32.1 0.0 collective-permute-start.17
  32.1 0.0 collective-permute-done.12.refs_6_
  32.1 0.0 collective-permute-done.8.refs_3_
  32.1 0.5 %shard_map.81 = (f32[256,128]{1,0:T(8,128)S(1)}, f32[256,128]{1,0:T(8,128)S(1)}, f32[64,128]{1,0:T(8,128)S(1)}) custom-call(bf16[512,2048]{1,0:T(8,128)(2,1)S(1)} %get-tuple-element.44.refs_0_, bf16[512,2048]{1,0:T(8,128)(2,1)S(1)} %get-tuple-element.45.refs_1_, f32[64,2176]{1,0:T(8,128)S(1)} %get-tuple-element.46.refs_2_, ...), custom_call_target="tpu_custom_call" | custom-call | flops 1509949440 | bytes 11796480 | tf_op jit(solution)/shard_map/pallas_call | solution.py:161
  32.7 2.9 %collective-permute-done.11.refs_9_ = f32[256,128]{1,0:T(8,128)S(1)} collective-permute-done((f32[256,128]{1,0:T(8,128)S(1)}, f32[256,128]{1,0:T(8,128)S(1)}, u32[]{:S(2)}, u32[]{:S(2)}) %collective-permute-start.11) | collective-permute-done | bytes 131104 | tf_op jit(solution)/shard_map/ppermute | solution.py:226
  35.5 0.0 collective-permute-start.13
  35.5 0.0 collective-permute-done.15.refs_6_
  35.5 0.0 collective-permute-done.17.refs_8_
  35.5 1.1 %shard_map.82 = (f32[256,128]{1,0:T(8,128)S(1)}, f32[256,128]{1,0:T(8,128)S(1)}, f32[64,128]{1,0:T(8,128)S(1)}) custom-call(bf16[512,2048]{1,0:T(8,128)(2,1)S(1)} %get-tuple-element.44.refs_0_, bf16[512,2048]{1,0:T(8,128)(2,1)S(1)} %get-tuple-element.45.refs_1_, f32[64,2176]{1,0:T(8,128)S(1)} %get-tuple-element.46.refs_2_, ...), custom_call_target="tpu_custom_call" | custom-call | flops 3774873600 | bytes 29491200 | tf_op jit(solution)/shard_map/pallas_call | solution.py:161
  36.6 0.3 collective-permute-done.13.refs_5_
  36.9 0.2 shard_map.83.refs_2_.refs_3_.refs_4_
  37.0 2.4 %collective-permute-start.18 = (f32[64,128]{1,0:T(8,128)S(1)}, f32[64,128]{1,0:T(8,128)S(1)}, u32[]{:S(2)}, u32[]{:S(2)}) collective-permute-start(f32[64,128]{1,0:T(8,128)S(1)} %shard_map.83.refs_2_.refs_3_.refs_4_), channel_id=1, source_target_pairs={{0,12},{1,13},{2,14},{3,15},{4,8},{5,9},{6,10},{7,11},{8,4},{9,5},... | collective-permute-start | bytes 98312 | tf_op jit(solution)/shard_map/ppermute | solution.py:226
  39.5 0.0 collective-permute-start.19
  39.5 2.0 %collective-permute-start.20 = (f32[64,128]{1,0:T(8,128)S(1)}, f32[64,128]{1,0:T(8,128)S(1)}, u32[]{:S(2)}, u32[]{:S(2)}) collective-permute-start(f32[64,128]{1,0:T(8,128)S(1)} %shard_map.83.refs_2_.refs_3_.refs_4_), channel_id=1, source_target_pairs={{0,4},{1,5},{2,6},{3,7},{4,0},{5,1},{6,2},{7,3},{8,12},{9,13},{10,... | collective-permute-start | bytes 98312 | tf_op jit(solution)/shard_map/ppermute | solution.py:226
  41.5 0.3 shard_map.84
  41.8 1.0 %collective-permute-start.21 = (f32[256,128]{1,0:T(8,128)S(1)}, f32[256,128]{1,0:T(8,128)S(1)}, u32[]{:S(2)}, u32[]{:S(2)}) collective-permute-start(f32[256,128]{1,0:T(8,128)S(1)} %get-tuple-element.58), channel_id=1, source_target_pairs={{0,8},{1,9},{2,10},{3,11},{4,12},{5,13},{6,14},{7,15},{8,0},{9,1},... | collective-permute-start | bytes 393224 | tf_op jit(solution)/shard_map/ppermute | solution.py:226
  42.8 0.1 collective-permute-done.18
  42.8 1.5 %collective-permute-done.19 = f32[64,128]{1,0:T(8,128)S(1)} collective-permute-done((f32[64,128]{1,0:T(8,128)S(1)}, f32[64,128]{1,0:T(8,128)S(1)}, u32[]{:S(2)}, u32[]{:S(2)}) %collective-permute-start.19) | collective-permute-done | bytes 32800 | tf_op jit(solution)/shard_map/ppermute | solution.py:226
  44.3 0.0 collective-permute-done.20
  44.3 1.6 %collective-permute-start.22 = (f32[64,128]{1,0:T(8,128)S(1)}, f32[64,128]{1,0:T(8,128)S(1)}, u32[]{:S(2)}, u32[]{:S(2)}) collective-permute-start(f32[64,128]{1,0:T(8,128)S(1)} %add_add_fusion.refs_0_), channel_id=1, source_target_pairs={{0,18},{1,19},{2,16},{3,17},{4,22},{5,23},{6,20},{7,21},{8,26},{9,... | collective-permute-start | bytes 98312 | tf_op jit(solution)/shard_map/ppermute | solution.py:226
  45.9 0.6 %collective-permute-start.23 = (f32[64,128]{1,0:T(8,128)S(1)}, f32[64,128]{1,0:T(8,128)S(1)}, u32[]{:S(2)}, u32[]{:S(2)}) collective-permute-start(f32[64,128]{1,0:T(8,128)S(1)} %add_add_fusion.refs_0_), channel_id=1, source_target_pairs={{0,16},{1,17},{2,18},{3,19},{4,20},{5,21},{6,22},{7,23},{8,24},{9,... | collective-permute-start | bytes 98312 | tf_op jit(solution)/shard_map/ppermute | solution.py:226
  46.5 1.4 %collective-permute-start.24 = (f32[64,128]{1,0:T(8,128)S(1)}, f32[64,128]{1,0:T(8,128)S(1)}, u32[]{:S(2)}, u32[]{:S(2)}) collective-permute-start(f32[64,128]{1,0:T(8,128)S(1)} %add_add_fusion.refs_0_), channel_id=1, source_target_pairs={{0,2},{1,3},{2,0},{3,1},{4,6},{5,7},{6,4},{7,5},{8,10},{9,11},{10,... | collective-permute-start | bytes 98312 | tf_op jit(solution)/shard_map/ppermute | solution.py:226
  47.9 1.5 %collective-permute-done.22.refs_1_ = f32[64,128]{1,0:T(8,128)S(1)} collective-permute-done((f32[64,128]{1,0:T(8,128)S(1)}, f32[64,128]{1,0:T(8,128)S(1)}, u32[]{:S(2)}, u32[]{:S(2)}) %collective-permute-start.22) | collective-permute-done | bytes 32800 | tf_op jit(solution)/shard_map/ppermute | solution.py:226
  49.4 0.8 %collective-permute-done.21.refs_5_ = f32[256,128]{1,0:T(8,128)S(1)} collective-permute-done((f32[256,128]{1,0:T(8,128)S(1)}, f32[256,128]{1,0:T(8,128)S(1)}, u32[]{:S(2)}, u32[]{:S(2)}) %collective-permute-start.21) | collective-permute-done | bytes 131104 | tf_op jit(solution)/shard_map/ppermute | solution.py:226
  50.1 0.0 collective-permute-done.23.refs_2_
  50.1 0.3 collective-permute-done.24.refs_3_
  50.4 0.0 copy-done.1
  50.4 0.0 copy-done.2
  50.4 0.8 %shard_map.85 = (f32[256,128]{1,0:T(8,128)}, f32[64,128]{1,0:T(8,128)}) custom-call(f32[64,64]{1,0:T(8,128)S(1)} %copy-done.1, f32[64,128]{1,0:T(8,128)S(1)} %copy-done.2, f32[64,128]{1,0:T(8,128)S(1)} %add_add_fusion.refs_0_, f32[64,128]{1,0:T(8,128)S(1)} %collective-permute-done.22.refs_1_, f32[64,128]{1,0:T(8,128)S(1)} %collective-permute-done.23.refs_2_, ...), custom_call_target="tpu_custom_call" | custom-call | tf_op jit(solution)/shard_map/pallas_call | solution.py:198
  (6 shorter events, 0.0 us)
Async XLA Ops:
  0.6 10.5 %collective-permute-start.1 = (f32[256,128]{1,0:T(8,128)}, f32[256,128]{1,0:T(8,128)S(1)}, u32[]{:S(2)}, u32[]{:S(2)}) collective-permute-start(f32[256,128]{1,0:T(8,128)} %bitcast.9), channel_id=1, source_target_pairs={{0,4},{1,5},{2,6},{3,7},{4,0},{5,1},{6,2},{7,3},{8,12},{9,13},{10,... | collective-permute-start | bytes 393224 | tf_op jit(solution)/shard_map/ppermute | solution.py:226
  3.7 8.0 %collective-permute-start.5 = (f32[256,128]{1,0:T(8,128)}, f32[256,128]{1,0:T(8,128)S(1)}, u32[]{:S(2)}, u32[]{:S(2)}) collective-permute-start(f32[256,128]{1,0:T(8,128)} %bitcast.10), channel_id=1, source_target_pairs={{0,2},{1,3},{2,0},{3,1},{4,6},{5,7},{6,4},{7,5},{8,10},{9,11},{10,... | collective-permute-start | bytes 393224 | tf_op jit(solution)/shard_map/ppermute | solution.py:226
  5.2 6.0 %collective-permute-start = (f32[64,256]{1,0:T(8,128)}, f32[64,256]{1,0:T(8,128)S(1)}, u32[]{:S(2)}, u32[]{:S(2)}) collective-permute-start(f32[64,256]{1,0:T(8,128)} %bitcast.7), channel_id=1, source_target_pairs={{0,8},{1,9},{2,10},{3,11},{4,12},{5,13},{6,14},{7,15},{8,0},{9,1},... | collective-permute-start | bytes 196616 | tf_op jit(solution)/shard_map/ppermute | solution.py:226
  7.8 6.1 %collective-permute-start.2 = (f32[256,128]{1,0:T(8,128)}, f32[256,128]{1,0:T(8,128)S(1)}, u32[]{:S(2)}, u32[]{:S(2)}) collective-permute-start(f32[256,128]{1,0:T(8,128)} %bitcast.11), channel_id=1, source_target_pairs={{0,6},{1,7},{2,4},{3,5},{4,2},{5,3},{6,0},{7,1},{8,14},{9,15},{10,... | collective-permute-start | bytes 393224 | tf_op jit(solution)/shard_map/ppermute | solution.py:226
  8.2 5.7 %collective-permute-start.4 = (f32[256,128]{1,0:T(8,128)}, f32[256,128]{1,0:T(8,128)S(1)}, u32[]{:S(2)}, u32[]{:S(2)}) collective-permute-start(f32[256,128]{1,0:T(8,128)} %bitcast.12), channel_id=1, source_target_pairs={{0,1},{1,0},{2,3},{3,2},{4,5},{5,4},{6,7},{7,6},{8,9},{9,8},{10,11... | collective-permute-start | bytes 393224 | tf_op jit(solution)/shard_map/ppermute | solution.py:226
  8.2 5.7 %copy-start.3 = (f32[1,256,128]{2,1,0:T(8,128)S(1)}, f32[1,256,128]{2,1,0:T(8,128)}, u32[]{:S(2)}) copy-start(f32[1,256,128]{2,1,0:T(8,128)} %param.8) | copy-start | bytes 393220
  11.2 2.7 %collective-permute-start.7 = (f32[256,128]{1,0:T(8,128)S(1)}, f32[256,128]{1,0:T(8,128)S(1)}, u32[]{:S(2)}, u32[]{:S(2)}) collective-permute-start(f32[256,128]{1,0:T(8,128)S(1)} %collective-permute-done.1.refs_9_), channel_id=1, source_target_pairs={{0,1},{1,0},{2,3},{3,2},{4,5},{5,4},{6,7},{7,6},{8,9},{9,8},{10,11... | collective-permute-start | bytes 393224 | tf_op jit(solution)/shard_map/ppermute | solution.py:226
  11.8 2.1 %collective-permute-start.6 = (f32[256,128]{1,0:T(8,128)S(1)}, f32[256,128]{1,0:T(8,128)S(1)}, u32[]{:S(2)}, u32[]{:S(2)}) collective-permute-start(f32[256,128]{1,0:T(8,128)S(1)} %collective-permute-done.5.refs_7_), channel_id=1, source_target_pairs={{0,1},{1,0},{2,3},{3,2},{4,5},{5,4},{6,7},{7,6},{8,9},{9,8},{10,11... | collective-permute-start | bytes 393224 | tf_op jit(solution)/shard_map/ppermute | solution.py:226
  13.9 1.3 %collective-permute-start.3 = (f32[256,128]{1,0:T(8,128)S(1)}, f32[256,128]{1,0:T(8,128)S(1)}, u32[]{:S(2)}, u32[]{:S(2)}) collective-permute-start(f32[256,128]{1,0:T(8,128)S(1)} %collective-permute-done.2.refs_11_), channel_id=1, source_target_pairs={{0,1},{1,0},{2,3},{3,2},{4,5},{5,4},{6,7},{7,6},{8,9},{9,8},{10,11... | collective-permute-start | bytes 393224 | tf_op jit(solution)/shard_map/ppermute | solution.py:226
  15.2 3.3 %copy-start = (f32[1,64,256]{2,1,0:T(8,128)S(1)}, f32[1,64,256]{2,1,0:T(8,128)}, u32[]{:S(2)}) copy-start(f32[1,64,256]{2,1,0:T(8,128)} %param.9) | copy-start | bytes 196612
  15.5 10.6 %collective-permute-start.9 = (f32[256,128]{1,0:T(8,128)S(1)}, f32[256,128]{1,0:T(8,128)S(1)}, u32[]{:S(2)}, u32[]{:S(2)}) collective-permute-start(f32[256,128]{1,0:T(8,128)S(1)} %get-tuple-element.43.refs_3_.refs_8_), channel_id=1, source_target_pairs={{0,24},{1,25},{2,26},{3,27},{4,28},{5,29},{6,30},{7,31},{8,16},{9,... | collective-permute-start | bytes 393224 | tf_op jit(solution)/shard_map/ppermute | solution.py:226
  18.0 8.2 %collective-permute-start.10 = (f32[256,128]{1,0:T(8,128)S(1)}, f32[256,128]{1,0:T(8,128)S(1)}, u32[]{:S(2)}, u32[]{:S(2)}) collective-permute-start(f32[256,128]{1,0:T(8,128)S(1)} %get-tuple-element.42.refs_2_.refs_7_), channel_id=1, source_target_pairs={{0,16},{1,17},{2,18},{3,19},{4,20},{5,21},{6,22},{7,23},{8,24},{9,... | collective-permute-start | bytes 393224 | tf_op jit(solution)/shard_map/ppermute | solution.py:226
  22.2 9.9 %collective-permute-start.8 = (f32[64,2176]{1,0:T(8,128)S(1)}, f32[64,2176]{1,0:T(8,128)S(1)}, u32[]{:S(2)}, u32[]{:S(2)}) collective-permute-start(f32[64,2176]{1,0:T(8,128)S(1)} %get-tuple-element.46.refs_2_), channel_id=1, source_target_pairs={{0,1},{1,0},{2,3},{3,2},{4,5},{5,4},{6,7},{7,6},{8,9},{9,8},{10,11... | collective-permute-start | bytes 1671176 | tf_op jit(solution)/shard_map/ppermute | solution.py:226
  26.2 5.3 %collective-permute-start.14 = (f32[256,128]{1,0:T(8,128)S(1)}, f32[256,128]{1,0:T(8,128)S(1)}, u32[]{:S(2)}, u32[]{:S(2)}) collective-permute-start(f32[256,128]{1,0:T(8,128)S(1)} %add_select_fusion.refs_5_), channel_id=1, source_target_pairs={{0,2},{1,3},{2,0},{3,1},{4,6},{5,7},{6,4},{7,5},{8,10},{9,11},{10,... | collective-permute-start | bytes 393224 | tf_op jit(solution)/shard_map/ppermute | solution.py:226
  26.7 5.4 %collective-permute-start.16 = (f32[256,128]{1,0:T(8,128)S(1)}, f32[256,128]{1,0:T(8,128)S(1)}, u32[]{:S(2)}, u32[]{:S(2)}) collective-permute-start(f32[256,128]{1,0:T(8,128)S(1)} %add_select_fusion.refs_5_), channel_id=1, source_target_pairs={{0,4},{1,5},{2,6},{3,7},{4,0},{5,1},{6,2},{7,3},{8,12},{9,13},{10,... | collective-permute-start | bytes 393224 | tf_op jit(solution)/shard_map/ppermute | solution.py:226
  28.1 4.0 %collective-permute-start.12 = (f32[256,128]{1,0:T(8,128)S(1)}, f32[256,128]{1,0:T(8,128)S(1)}, u32[]{:S(2)}, u32[]{:S(2)}) collective-permute-start(f32[256,128]{1,0:T(8,128)S(1)} %add_select_fusion.refs_5_), channel_id=1, source_target_pairs={{0,1},{1,0},{2,3},{3,2},{4,5},{5,4},{6,7},{7,6},{8,9},{9,8},{10,11... | collective-permute-start | bytes 393224 | tf_op jit(solution)/shard_map/ppermute | solution.py:226
  28.1 7.4 %collective-permute-start.11 = (f32[256,128]{1,0:T(8,128)S(1)}, f32[256,128]{1,0:T(8,128)S(1)}, u32[]{:S(2)}, u32[]{:S(2)}) collective-permute-start(f32[256,128]{1,0:T(8,128)S(1)} %add_select_fusion.refs_5_), channel_id=1, source_target_pairs={{0,6},{1,7},{2,4},{3,5},{4,2},{5,3},{6,0},{7,1},{8,14},{9,15},{10,... | collective-permute-start | bytes 393224 | tf_op jit(solution)/shard_map/ppermute | solution.py:226
  31.5 4.0 %collective-permute-start.15 = (f32[256,128]{1,0:T(8,128)S(1)}, f32[256,128]{1,0:T(8,128)S(1)}, u32[]{:S(2)}, u32[]{:S(2)}) collective-permute-start(f32[256,128]{1,0:T(8,128)S(1)} %collective-permute-done.14.refs_5_), channel_id=1, source_target_pairs={{0,1},{1,0},{2,3},{3,2},{4,5},{5,4},{6,7},{7,6},{8,9},{9,8},{10,11... | collective-permute-start | bytes 393224 | tf_op jit(solution)/shard_map/ppermute | solution.py:226
  32.1 3.4 %collective-permute-start.17 = (f32[256,128]{1,0:T(8,128)S(1)}, f32[256,128]{1,0:T(8,128)S(1)}, u32[]{:S(2)}, u32[]{:S(2)}) collective-permute-start(f32[256,128]{1,0:T(8,128)S(1)} %collective-permute-done.16.refs_7_), channel_id=1, source_target_pairs={{0,1},{1,0},{2,3},{3,2},{4,5},{5,4},{6,7},{7,6},{8,9},{9,8},{10,11... | collective-permute-start | bytes 393224 | tf_op jit(solution)/shard_map/ppermute | solution.py:226
  35.5 1.3 %collective-permute-start.13 = (f32[256,128]{1,0:T(8,128)S(1)}, f32[256,128]{1,0:T(8,128)S(1)}, u32[]{:S(2)}, u32[]{:S(2)}) collective-permute-start(f32[256,128]{1,0:T(8,128)S(1)} %collective-permute-done.11.refs_9_), channel_id=1, source_target_pairs={{0,1},{1,0},{2,3},{3,2},{4,5},{5,4},{6,7},{7,6},{8,9},{9,8},{10,11... | collective-permute-start | bytes 393224 | tf_op jit(solution)/shard_map/ppermute | solution.py:226
  37.0 5.8 %collective-permute-start.18 = (f32[64,128]{1,0:T(8,128)S(1)}, f32[64,128]{1,0:T(8,128)S(1)}, u32[]{:S(2)}, u32[]{:S(2)}) collective-permute-start(f32[64,128]{1,0:T(8,128)S(1)} %shard_map.83.refs_2_.refs_3_.refs_4_), channel_id=1, source_target_pairs={{0,12},{1,13},{2,14},{3,15},{4,8},{5,9},{6,10},{7,11},{8,4},{9,5},... | collective-permute-start | bytes 98312 | tf_op jit(solution)/shard_map/ppermute | solution.py:226
  39.5 4.8 %collective-permute-start.19 = (f32[64,128]{1,0:T(8,128)S(1)}, f32[64,128]{1,0:T(8,128)S(1)}, u32[]{:S(2)}, u32[]{:S(2)}) collective-permute-start(f32[64,128]{1,0:T(8,128)S(1)} %shard_map.83.refs_2_.refs_3_.refs_4_), channel_id=1, source_target_pairs={{0,8},{1,9},{2,10},{3,11},{4,12},{5,13},{6,14},{7,15},{8,0},{9,1},... | collective-permute-start | bytes 98312 | tf_op jit(solution)/shard_map/ppermute | solution.py:226
  39.5 4.8 %collective-permute-start.20 = (f32[64,128]{1,0:T(8,128)S(1)}, f32[64,128]{1,0:T(8,128)S(1)}, u32[]{:S(2)}, u32[]{:S(2)}) collective-permute-start(f32[64,128]{1,0:T(8,128)S(1)} %shard_map.83.refs_2_.refs_3_.refs_4_), channel_id=1, source_target_pairs={{0,4},{1,5},{2,6},{3,7},{4,0},{5,1},{6,2},{7,3},{8,12},{9,13},{10,... | collective-permute-start | bytes 98312 | tf_op jit(solution)/shard_map/ppermute | solution.py:226
  41.5 8.9 %copy-start.1 = (f32[64,64]{1,0:T(8,128)S(1)}, f32[64,64]{1,0:T(8,128)}, u32[]{:S(2)}) copy-start(f32[64,64]{1,0:T(8,128)} %tip_inv.1) | copy-start | bytes 49156
  41.5 8.9 %copy-start.2 = (f32[64,128]{1,0:T(8,128)S(1)}, f32[64,128]{1,0:T(8,128)}, u32[]{:S(2)}) copy-start(f32[64,128]{1,0:T(8,128)} %tip_rhs.1) | copy-start | bytes 98308
  41.8 8.3 %collective-permute-start.21 = (f32[256,128]{1,0:T(8,128)S(1)}, f32[256,128]{1,0:T(8,128)S(1)}, u32[]{:S(2)}, u32[]{:S(2)}) collective-permute-start(f32[256,128]{1,0:T(8,128)S(1)} %get-tuple-element.58), channel_id=1, source_target_pairs={{0,8},{1,9},{2,10},{3,11},{4,12},{5,13},{6,14},{7,15},{8,0},{9,1},... | collective-permute-start | bytes 393224 | tf_op jit(solution)/shard_map/ppermute | solution.py:226
  44.3 5.1 %collective-permute-start.22 = (f32[64,128]{1,0:T(8,128)S(1)}, f32[64,128]{1,0:T(8,128)S(1)}, u32[]{:S(2)}, u32[]{:S(2)}) collective-permute-start(f32[64,128]{1,0:T(8,128)S(1)} %add_add_fusion.refs_0_), channel_id=1, source_target_pairs={{0,18},{1,19},{2,16},{3,17},{4,22},{5,23},{6,20},{7,21},{8,26},{9,... | collective-permute-start | bytes 98312 | tf_op jit(solution)/shard_map/ppermute | solution.py:226
  45.9 4.3 %collective-permute-start.23 = (f32[64,128]{1,0:T(8,128)S(1)}, f32[64,128]{1,0:T(8,128)S(1)}, u32[]{:S(2)}, u32[]{:S(2)}) collective-permute-start(f32[64,128]{1,0:T(8,128)S(1)} %add_add_fusion.refs_0_), channel_id=1, source_target_pairs={{0,16},{1,17},{2,18},{3,19},{4,20},{5,21},{6,22},{7,23},{8,24},{9,... | collective-permute-start | bytes 98312 | tf_op jit(solution)/shard_map/ppermute | solution.py:226
  46.5 3.9 %collective-permute-start.24 = (f32[64,128]{1,0:T(8,128)S(1)}, f32[64,128]{1,0:T(8,128)S(1)}, u32[]{:S(2)}, u32[]{:S(2)}) collective-permute-start(f32[64,128]{1,0:T(8,128)S(1)} %add_add_fusion.refs_0_), channel_id=1, source_target_pairs={{0,2},{1,3},{2,0},{3,1},{4,6},{5,7},{6,4},{7,5},{8,10},{9,11},{10,... | collective-permute-start | bytes 98312 | tf_op jit(solution)/shard_map/ppermute | solution.py:226
